TPU v7x, 256 devices: a whole 4x4x8 slice. The times are simulated.
256 devices in a mesh: group: 16 (over z_hi, y, core), mp: 16 (over x, z_lo).
Axes of the slice: x: 4, y: 4, z: 8 (z_hi: 2, z_lo: 4; z = z_hi * 4 + z_lo), core: 2. Of those that a mesh axis runs over, the one named last changes fastest.
Arguments:
- token_ids: int32 [512], replicated, may hold values from 0 to 76031
- page_ids: int32 [512], replicated, may hold values from 0 to 31, never falling along the last dimension, each value on 1 to 48 neighbouring positions
- tap_layer: int32 [32], replicated, may hold values from 0 to 1, as said below
- teacher_in: bfloat16 [512, 8192], P(None, 'mp'), may hold values from -60 to 60
- teacher_gain: bfloat16 [8192], P('mp'), may hold values from 0.25 to 1.75
- teacher_gate: bfloat16 [8192, 16384], P('mp', 'group'), may hold values from -0.0625 to 0.0625
- teacher_up: bfloat16 [8192, 16384], P('mp', 'group'), may hold values from -0.0625 to 0.0625
- teacher_down: bfloat16 [16384, 8192], P('group', 'mp'), may hold values from -0.375 to 0.375
- student_embed: bfloat16 [76032, 3584], P('mp', 'group'), may hold values from -25 to 25
- student_gain: bfloat16 [3584], P('group'), may hold values from 0.25 to 1.75
- student_gate: bfloat16 [3584, 10240], P('group', 'mp'), may hold values from -0.09375 to 0.09375
- student_up: bfloat16 [3584, 10240], P('group', 'mp'), may hold values from -0.09375 to 0.09375
- student_down: bfloat16 [10240, 3584], P('mp', 'group'), may hold values from -0.0625 to 0.0625
- projection: bfloat16 [3584, 8192], P('group', 'mp'), may hold values from -0.09375 to 0.09375
Outputs:
- loss: float32 [], replicated
- grad_gate: float32 [3584, 10240], P('group', 'mp')
- grad_up: float32 [3584, 10240], P('group', 'mp')
- grad_down: float32 [10240, 3584], P('mp', 'group')
- grad_proj: float32 [3584, 8192], P('group', 'mp')
Inputs may be any that keep to these rules, and one draw needn't show every extreme that they name: `page_ids`: pages are runs of consecutive tokens numbered in order from 0; each of the 32 pages holds 1 to 48 tokens. `tap_layer`: 0 matches a page to the teacher layer's input, 1 to its output; both values occur.
All inputs are finite; a program needn't handle non-finite values.
Results may differ from a plain program's by a relative error of at most 0.04.
Values may be sent and summed in bfloat16 or wider, within the bound.
No kernel may reach another device: no remote copies, remote signals or barrier semaphores. Data moves between devices by JAX's collectives and lax.ppermute only.
A program may use at most 64 MiB of HBM per device.

v0:
```python
import jax
import jax.numpy as jnp
from jax import lax
from jax.sharding import PartitionSpec as P

DT = 8192
DS = 3584


EPS = 1e-06


def silu_parts(values):
    sigmoid = jax.nn.sigmoid(values)
    return (values * sigmoid, sigmoid * (1.0 + values * (1.0 - sigmoid)))


def transpose_product(left, right):
    return lax.dot_general(
        left, right, (((0,), (0,)), ((), ())), preferred_element_type=jnp.float32
    )


def product_transposed(left, right):
    return lax.dot_general(
        left, right, (((1,), (1,)), ((), ())), preferred_element_type=jnp.float32
    )


def shards(
    token_ids,
    page_ids,
    tap_layer,
    teacher_in,
    teacher_gain,
    teacher_gate,
    teacher_up,
    teacher_down,
    student_embed,
    student_gain,
    student_gate,
    student_up,
    student_down,
    projection,
):
    group_count = lax.axis_size("group")
    group_index = lax.axis_index("group")
    model_index = lax.axis_index("mp")
    tokens = teacher_in.shape[0]
    group_rows = tokens // group_count
    row_start = group_index * group_rows
    teacher_float = teacher_in.astype(jnp.float32)
    teacher_square = lax.psum(jnp.sum(teacher_float * teacher_float, axis=1), "mp")
    teacher_normed = (
        teacher_float
        * lax.rsqrt(teacher_square / DT + EPS)[:, None]
        * teacher_gain.astype(jnp.float32)
    ).astype(jnp.bfloat16)
    teacher_both = jnp.concatenate([teacher_gate, teacher_up], axis=1)
    teacher_width = teacher_gate.shape[1]
    rows = teacher_normed
    teacher_sums = lax.psum_scatter(
        jnp.dot(rows, teacher_both, preferred_element_type=jnp.float32).astype(jnp.bfloat16),
        "mp",
        scatter_dimension=0,
        tiled=True,
    ).astype(jnp.float32)
    teacher_active, _ = silu_parts(teacher_sums[:, :teacher_width])
    teacher_share = (teacher_active * teacher_sums[:, teacher_width:]).astype(jnp.bfloat16)
    teacher_partial = jnp.dot(
        lax.all_gather(teacher_share, "mp", axis=0, tiled=True),
        teacher_down,
        preferred_element_type=jnp.float32,
    )
    teacher_added = lax.psum_scatter(
        teacher_partial.astype(jnp.bfloat16), "group", scatter_dimension=0, tiled=True
    ).astype(jnp.float32)
    teacher_in_rows = lax.dynamic_slice_in_dim(teacher_in, row_start, group_rows, 0)
    teacher_out = (teacher_in_rows.astype(jnp.float32) + teacher_added).astype(jnp.bfloat16)
    vocab_rows = student_embed.shape[0]
    local_ids = token_ids - model_index * vocab_rows
    inside = (local_ids >= 0) & (local_ids < vocab_rows)
    picked = jnp.take(student_embed, jnp.clip(local_ids, 0, vocab_rows - 1), axis=0)
    picked = jnp.where(inside[:, None], picked.astype(jnp.float32), 0.0)
    student_in = lax.psum(picked.astype(jnp.bfloat16), "mp")
    student_float = student_in.astype(jnp.float32)
    student_square = lax.psum(jnp.sum(student_float * student_float, axis=1), "group")
    student_normed = (
        student_float
        * lax.rsqrt(student_square / DS + EPS)[:, None]
        * student_gain.astype(jnp.float32)
    ).astype(jnp.bfloat16)
    student_both = jnp.concatenate([student_gate, student_up], axis=1)
    student_width = student_gate.shape[1]
    rows = student_normed
    student_sums = lax.psum_scatter(
        jnp.dot(rows, student_both, preferred_element_type=jnp.float32).astype(jnp.bfloat16),
        "group",
        scatter_dimension=0,
        tiled=True,
    ).astype(jnp.float32)
    active, slope = silu_parts(student_sums[:, :student_width])
    hidden_share = (active * student_sums[:, student_width:]).astype(jnp.bfloat16)
    student_hidden = lax.all_gather(hidden_share, "group", axis=0, tiled=True)
    down_partial = jnp.dot(student_hidden, student_down, preferred_element_type=jnp.float32)
    student_out = (
        student_float + lax.psum(down_partial.astype(jnp.bfloat16), "mp").astype(jnp.float32)
    ).astype(jnp.bfloat16)
    rows = student_out
    predicted = lax.psum_scatter(
        jnp.dot(rows, projection, preferred_element_type=jnp.float32).astype(jnp.bfloat16),
        "group",
        scatter_dimension=0,
        tiled=True,
    ).astype(jnp.float32)
    pages = tap_layer.shape[0]
    member = page_ids[:, None] == jnp.arange(pages, dtype=jnp.int32)[None, :]
    counts = jnp.sum(member.astype(jnp.float32), axis=0)
    page_weight = 1.0 / (pages * counts)
    token_weight = jnp.sum(jnp.where(member, page_weight[None, :], 0.0), axis=1)
    token_tap = jnp.sum(jnp.where(member, tap_layer[None, :], 0), axis=1)
    weight = lax.dynamic_slice_in_dim(token_weight, row_start, group_rows, 0)
    tapped = lax.dynamic_slice_in_dim(token_tap, row_start, group_rows, 0)
    target = jnp.where((tapped == 1)[:, None], teacher_out, teacher_in_rows)
    difference = predicted - target.astype(jnp.float32)
    loss = lax.psum(jnp.sum(weight[:, None] * difference * difference) / DT, ("group", "mp"))
    pred_grad = (tokens / 16 * weight[:, None] * difference).astype(jnp.bfloat16)
    pred_all = lax.all_gather(pred_grad, "group", axis=0, tiled=True)
    grad_proj = transpose_product(student_out, pred_all)
    out_partial = product_transposed(pred_all, projection)
    out_grad = lax.psum(out_partial.astype(jnp.bfloat16), "mp")
    grad_down = transpose_product(student_hidden, out_grad)
    rows = out_grad
    hidden_grad = lax.psum_scatter(
        product_transposed(rows, student_down).astype(jnp.bfloat16),
        "group",
        scatter_dimension=0,
        tiled=True,
    ).astype(jnp.float32)
    gate_share = (hidden_grad * student_sums[:, student_width:] * slope).astype(jnp.bfloat16)
    up_share = (hidden_grad * active).astype(jnp.bfloat16)
    gate_grad, up_grad = (
        lax.all_gather(gate_share, "group", axis=0, tiled=True),
        lax.all_gather(up_share, "group", axis=0, tiled=True),
    )
    grad_gate = transpose_product(student_normed, gate_grad)
    grad_up = transpose_product(student_normed, up_grad)
    return (loss, grad_gate, grad_up, grad_down, grad_proj)


def solution(mesh):
    placed = (
        P(),
        P(),
        P(),
        P(None, "mp"),
        P("mp"),
        P("mp", "group"),
        P("mp", "group"),
        P("group", "mp"),
        P("mp", "group"),
        P("group"),
        P("group", "mp"),
        P("group", "mp"),
        P("mp", "group"),
        P("group", "mp"),
    )
    return jax.shard_map(
        shards,
        mesh=mesh,
        in_specs=placed,
        out_specs=(P(), P("group", "mp"), P("group", "mp"), P("mp", "group"), P("group", "mp")),
        check_vma=False,
    )
```

profile of v0, /device:TPU:1, one launch (start us, length us, event | category | flops | bytes accessed | tf_op | source)
XLA Modules:
  0.0 1127.4 jit_solution(8249608957255865822)
XLA Ops:
  8.0 3.6 copy.21
  11.6 2.6 gather_fusion
  14.2 1.1 copy.22
  16.1 150.4 %all-reduce.4.cloned.1.call-done = bf16[512,224]{0,1:T(8,128)(2,1)} async-done(((bf16[512,224]{0,1:T(8,128)(2,1)}), bf16[512,224]{0,1:T(8,128)(2,1)}) %all-reduce.4.cloned.1.call-update) | async-done | bytes 229392 | tf_op jit(solution)/shard_map/psum | solution.py:85
  166.5 1.0 fusion.12
  167.5 53.5 %psum.43 = f32[512]{0:T(512)S(1)} all-reduce(f32[512]{0:T(512)S(1)} %fusion.12), channel_id=1, replica_groups=mesh['group'=16,'mp'=16] {'group'}, use_global_device_ids=true, to_apply=%region_4.5 | all-reduce | flops 512 | bytes 4096 | tf_op jit(solution)/shard_map/psum | solution.py:87
  221.0 2.9 convolution_convert_fusion.1
  224.2 33.1 %psum.45 = f32[512]{0:T(512)S(1)} all-reduce(f32[512]{0:T(512)S(1)} %fusion.3), channel_id=1, replica_groups=mesh['group'=16,'mp'=16] {'mp'}, use_global_device_ids=true, to_apply=%region_10.11 | all-reduce | flops 512 | bytes 4096 | tf_op jit(solution)/shard_map/psum | solution.py:53
  257.3 3.9 convolution_convert_fusion
  261.4 38.8 %reduce-scatter.6.cloned.1.call-done = bf16[32,1280]{1,0:T(8,128)(2,1)} async-done(((bf16[512,1280]{1,0:T(8,128)(2,1)}), bf16[32,1280]{1,0:T(8,128)(2,1)}) %reduce-scatter.6.cloned.1.call-update) | async-done | bytes 81936 | tf_op jit(solution)/shard_map/reduce_scatter | solution.py:96
  301.1 30.9 %all_gather.15 = bf16[512,640]{1,0:T(8,128)(2,1)S(1)} all-gather(bf16[32,640]{1,0:T(8,128)(2,1)S(1)} %multiply_convert_fusion), channel_id=1, replica_groups=mesh['group'=16,'mp'=16] {'group'}, dimensions={0}, use_global_device_ids=true | all-gather | bytes 696320 | tf_op jit(solution)/shard_map/all_gather | solution.py:104
  332.1 1.1 convolution_convert_fusion.6
  333.2 49.1 %reduce-scatter.10.cloned.1.call-done = bf16[32,2048]{1,0:T(8,128)(2,1)} async-done(((bf16[512,2048]{1,0:T(8,128)(2,1)}), bf16[32,2048]{1,0:T(8,128)(2,1)}) %reduce-scatter.10.cloned.1.call-update) | async-done | bytes 131088 | tf_op jit(solution)/shard_map/reduce_scatter | solution.py:62
  382.3 0.9 convert_element_type.112
  384.0 156.6 %all-reduce.6.cloned.1.call-done = bf16[512,224]{0,1:T(8,128)(2,1)} async-done(((bf16[512,224]{0,1:T(8,128)(2,1)}), bf16[512,224]{0,1:T(8,128)(2,1)}) %all-reduce.6.cloned.1.call-update) | async-done | bytes 229392 | tf_op jit(solution)/shard_map/psum | solution.py:107
  540.6 2.1 convolution_convert_fusion.3
  542.7 81.5 %all-gather.2.cloned.1.call-done = bf16[512,1024]{1,0:T(8,128)(2,1)} async-done(((bf16[32,1024]{1,0:T(8,128)(2,1)}), bf16[512,1024]{1,0:T(8,128)(2,1)}) %all-gather.2.cloned.1.call-update) | async-done | bytes 1048592 | tf_op jit(solution)/shard_map/all_gather | solution.py:71
  624.3 2.7 convolution_convert_fusion.4
  627.5 84.6 %reduce-scatter.8.cloned.1.call-done = bf16[32,512]{1,0:T(8,128)(2,1)} async-done(((bf16[512,512]{1,0:T(8,128)(2,1)}), bf16[32,512]{1,0:T(8,128)(2,1)}) %reduce-scatter.8.cloned.1.call-update) | async-done | bytes 32784 | tf_op jit(solution)/shard_map/reduce_scatter | solution.py:110
  712.2 78.3 %reduce-scatter.12.cloned.1.call-done = bf16[32,512]{1,0:T(8,128)(2,1)} async-done(((bf16[512,512]{1,0:T(8,128)(2,1)}), bf16[32,512]{1,0:T(8,128)(2,1)}) %reduce-scatter.12.cloned.1.call-update) | async-done | bytes 32784 | tf_op jit(solution)/shard_map/reduce_scatter | solution.py:75
  790.5 1.5 multiply_convert_fusion.1
  792.0 30.2 %all_gather.17 = bf16[512,512]{1,0:T(8,128)(2,1)S(1)} all-gather(bf16[32,512]{1,0:T(8,128)(2,1)S(1)} %get-tuple-element.9), channel_id=1, replica_groups=mesh['group'=16,'mp'=16] {'group'}, dimensions={0}, use_global_device_ids=true | all-gather | bytes 557056 | tf_op jit(solution)/shard_map/all_gather | solution.py:128
  822.1 1.0 convolution_convert_fusion.5
  823.2 144.5 %all-reduce.8.cloned.1.call-done = bf16[512,224]{0,1:T(8,128)(2,1)} async-done(((bf16[512,224]{0,1:T(8,128)(2,1)}), bf16[512,224]{0,1:T(8,128)(2,1)}) %all-reduce.8.cloned.1.call-update) | async-done | bytes 229392 | tf_op jit(solution)/shard_map/psum | solution.py:131
  967.7 2.3 convolution_convert_fusion.2
  970.7 86.1 %psum.46 = f32[]{:T(128)} all-reduce(f32[]{:T(128)S(6)} %div.39), channel_id=1, replica_groups=mesh['group'=16,'mp'=16] {'group','mp'}, use_global_device_ids=true, to_apply=%region_14.15 | all-reduce | flops 1 | bytes 8 | tf_op jit(solution)/shard_map/psum | solution.py:126
  1056.8 1.1 fusion.17
  1057.9 1.2 fusion.33
  1059.9 31.0 %all_gather.19 = bf16[512,640]{1,0:T(8,128)(2,1)S(1)} all-gather(bf16[32,640]{1,0:T(8,128)(2,1)S(1)} %get-tuple-element.11), channel_id=1, replica_groups=mesh['group'=16,'mp'=16] {'group'}, dimensions={0}, use_global_device_ids=true | all-gather | bytes 696320 | tf_op jit(solution)/shard_map/all_gather | solution.py:144
  1090.9 27.6 %all_gather.18 = bf16[512,640]{1,0:T(8,128)(2,1)S(1)} all-gather(bf16[32,640]{1,0:T(8,128)(2,1)S(1)} %get-tuple-element.12), channel_id=1, replica_groups=mesh['group'=16,'mp'=16] {'group'}, dimensions={0}, use_global_device_ids=true | all-gather | bytes 696320 | tf_op jit(solution)/shard_map/all_gather | solution.py:143
  1118.5 1.2 fusion.28
  1119.7 1.2 fusion.30
  (61 shorter events, 5.2 us)
Async XLA Ops:
  7.2 617.1 %copy-start = (bf16[1024,512]{1,0:T(8,128)(2,1)S(1)}, bf16[1024,512]{1,0:T(8,128)(2,1)}, u32[]{:S(2)}) copy-start(bf16[1024,512]{1,0:T(8,128)(2,1)} %param.21) | copy-start | bytes 3145732
  7.2 159.3 %all-reduce.4.cloned.1.call-start = ((), (), s32[]{:S(2)}) async-start(), calls=%async_computation.5 | async-start | bytes 458752 | tf_op jit(solution)/shard_map/psum | solution.py:85
  11.6 4.5 copy-start.11
  16.0 207.9 %copy-start.8 = (bf16[512]{0:T(512)(128)(2,1)S(1)}, bf16[512]{0:T(512)(128)(2,1)}, u32[]{:S(2)}) copy-start(bf16[512]{0:T(512)(128)(2,1)} %param.18) | copy-start | bytes 3076
  16.0 208.0 %copy-start.6 = (bf16[512,512]{1,0:T(8,128)(2,1)S(1)}, bf16[512,512]{1,0:T(8,128)(2,1)}, u32[]{:S(2)}) copy-start(bf16[512,512]{1,0:T(8,128)(2,1)} %param.17) | copy-start | bytes 1572868
  16.1 284.1 %reduce-scatter.6.cloned.1.call-start = ((), (), s32[]{:S(2)}) async-start(), calls=%async_computation.6 | async-start | bytes 1392640 | tf_op jit(solution)/shard_map/reduce_scatter | solution.py:96
  167.5 89.8 %copy-start.10 = (bf16[512,1024]{1,0:T(8,128)(2,1)S(1)}, bf16[512,1024]{1,0:T(8,128)(2,1)}, u32[]{:S(2)}) copy-start(bf16[512,1024]{1,0:T(8,128)(2,1)} %param.20) | copy-start | bytes 3145732
  223.9 158.4 %reduce-scatter.10.cloned.1.call-start = ((), (), s32[]{:S(2)}) async-start(), calls=%async_computation.9 | async-start | bytes 2228224 | tf_op jit(solution)/shard_map/reduce_scatter | solution.py:62
  261.3 70.8 %copy-start.2 = (bf16[640,224]{0,1:T(8,128)(2,1)S(1)}, bf16[640,224]{0,1:T(8,128)(2,1)}, u32[]{:S(2)}) copy-start(bf16[640,224]{0,1:T(8,128)(2,1)} %param.26) | copy-start | bytes 860164
  261.3 279.3 %copy-start.1 = (bf16[512,224]{0,1:T(8,128)(2,1)S(1)}, bf16[512,224]{0,1:T(8,128)(2,1)}, u32[]{:S(2)}) copy-start(bf16[512,224]{0,1:T(8,128)(2,1)} %all-reduce.4.cloned.1.call-done) | copy-start | bytes 688132
  261.3 279.3 %copy-start.3 = (bf16[224,512]{1,0:T(8,128)(2,1)S(1)}, bf16[224,512]{1,0:T(8,128)(2,1)}, u32[]{:S(2)}) copy-start(bf16[224,512]{1,0:T(8,128)(2,1)} %param.27) | copy-start | bytes 688132
  261.3 279.3 %all-reduce.6.cloned.1.call-start = ((), (), s32[]{:S(2)}) async-start(), calls=%async_computation.7 | async-start | bytes 458752 | tf_op jit(solution)/shard_map/psum | solution.py:107
  333.2 291.1 %all-gather.2.cloned.1.call-start = ((), (), s32[]{:S(2)}) async-start(), calls=%async_computation.10 | async-start | bytes 1114112 | tf_op jit(solution)/shard_map/all_gather | solution.py:71
  383.9 328.2 %reduce-scatter.8.cloned.1.call-start = ((), (), s32[]{:S(2)}) async-start(), calls=%async_computation.8 | async-start | bytes 557056 | tf_op jit(solution)/shard_map/reduce_scatter | solution.py:110
  542.7 84.4 %copy-start.7 = (s32[512]{0:T(512)S(1)}, s32[512]{0:T(512)}, u32[]{:S(2)}) copy-start(s32[512]{0:T(512)} %param.15) | copy-start | bytes 6148
  542.7 84.4 %copy-start.9 = (s32[32]{0:T(128)S(1)}, s32[32]{0:T(128)}, u32[]{:S(2)}) copy-start(s32[32]{0:T(128)} %param.16) | copy-start | bytes 388
  542.7 247.8 %reduce-scatter.12.cloned.1.call-start = ((), (), s32[]{:S(2)}) async-start(), calls=%async_computation.11 | async-start | bytes 557056 | tf_op jit(solution)/shard_map/reduce_scatter | solution.py:75
  627.0 429.8 %copy-start.4 = (bf16[512,224]{0,1:T(8,128)(2,1)S(1)}, bf16[512,224]{0,1:T(8,128)(2,1)}, u32[]{:S(2)}) copy-start(bf16[512,224]{0,1:T(8,128)(2,1)} %all-reduce.6.cloned.1.call-done) | copy-start | bytes 688132
  627.0 340.7 %all-reduce.8.cloned.1.call-start = ((), (), s32[]{:S(2)}) async-start(), calls=%async_computation.12 | async-start | bytes 458752 | tf_op jit(solution)/shard_map/psum | solution.py:131
  823.2 235.8 %reduce-scatter.14.cloned.1.call-start = ((), (), s32[]{:S(2)}) async-start(), calls=%async_computation.13 | async-start | bytes 696320 | tf_op jit(solution)/shard_map/reduce_scatter | solution.py:134
  967.7 90.1 %copy-start.5 = (bf16[512,224]{0,1:T(8,128)(2,1)S(1)}, bf16[512,224]{0,1:T(8,128)(2,1)}, u32[]{:S(2)}) copy-start(bf16[512,224]{0,1:T(8,128)(2,1)} %all-reduce.8.cloned.1.call-done) | copy-start | bytes 688132
Sparse Core Ops, SparseCore 0:
  16.2 150.2 all-reduce.3
  224.0 76.0 reduce-scatter.5
  302.9 79.3 reduce-scatter.9
  385.5 154.9 all-reduce.5
  542.8 81.4 all-gather.1
  628.7 83.3 reduce-scatter.7
  717.3 73.1 reduce-scatter.11
  823.3 144.3 all-reduce.7
  972.3 85.1 reduce-scatter.13
where the time goes:
time: 1130 us
  waiting for transfers between devices  784 us (69%)
  blocking collectives  292 us (26%)
  matrix products  20.6 us (2%)
  between operations  14.7 us (1%)
    psum x1, waiting for transfers between devices, shards(): lax.psum(down_partial.astype(jnp.bfloat16), 'mp').astype(jnp.float32)  157 us
    psum x1, waiting for transfers between devices, shards(): student_in = lax.psum(picked.astype(jnp.bfloat16), 'mp')  150 us
    psum x1, waiting for transfers between devices, shards(): out_grad = lax.psum(out_partial.astype(jnp.bfloat16), 'mp')  144 us
    psum x1, blocking collectives, shards(): lax.psum(jnp.sum(weight[:, None] * difference * difference) / DT, ('group...  86.1 us
    reduce_scatter x1, waiting for transfers between devices, shards(): lax.psum_scatter(jnp.dot(rows, projection, preferred_element_type=jnp.flo...  84.6 us
    all_gather x1, waiting for transfers between devices, shards(): lax.all_gather(teacher_share, 'mp', axis=0, tiled=True)  81.5 us
    reduce_scatter x1, waiting for transfers between devices, shards(): lax.psum_scatter(teacher_partial.astype(jnp.bfloat16), 'group', scatter_d...  78.3 us
    psum x1, blocking collectives, shards(): lax.psum(jnp.sum(student_float * student_float, axis=1), 'group')  53.5 us
  transfers between devices with their start and end apart: 9, of which 8 were waited for; matrix products, arithmetic and copies ran while one was open for 1% of the time, Pallas kernels for 0%

commit v1 on v0

v1 whole, which is shorter than its diff:
```python
import jax
import jax.numpy as jnp
from jax import lax
from jax.sharding import Mesh, PartitionSpec as P

DT = 8192
DS = 3584

EPS = 1e-06

F32 = jnp.float32
BF16 = jnp.bfloat16
GROUP = ("zh", "y", "c")
MODEL = ("x", "zl")
SWAP = [(0, 1), (1, 0)]
LANES = 256


def silu_parts(values):
    sigmoid = jax.nn.sigmoid(values)
    return (values * sigmoid, sigmoid * (1.0 + values * (1.0 - sigmoid)))


def product(left, right):
    return jnp.dot(left, right, preferred_element_type=F32)


def transpose_product(left, right):
    return lax.dot_general(left, right, (((0,), (0,)), ((), ())), preferred_element_type=F32)


def product_transposed(left, right):
    return lax.dot_general(left, right, (((1,), (1,)), ((), ())), preferred_element_type=F32)


def swap(values, axis):
    return lax.ppermute(values, axis, SWAP)


def exchange(values, axis):
    return lax.all_to_all(values, axis, 0, 0, tiled=True)


def spread(values, axis):
    count = lax.axis_size(axis)
    copies = jnp.broadcast_to(values[None], (count,) + values.shape)
    return exchange(copies.reshape((count * values.shape[0],) + values.shape[1:]), axis)


def sum_scatter(values, axis):
    count = lax.axis_size(axis)
    parts = exchange(values, axis)
    parts = parts.reshape((count, values.shape[0] // count) + values.shape[1:])
    return jnp.sum(parts.astype(F32), axis=0)


def group_sum(mine, other):
    received = swap(other.astype(BF16), "c")
    pair = (mine + received.astype(F32)).astype(BF16)
    total = sum_scatter(pair, "y")
    return total + swap(total.astype(BF16), "zh").astype(F32)


def group_rows(values):
    mine = spread(values, "y")
    return mine, swap(mine, "c")


def two_parts(values):
    high = lax.reduce_precision(values, 8, 7)
    return jnp.stack([high, values - high], axis=1).astype(BF16)


def widen(values, extra):
    rows = values.shape[0]
    left = LANES - values.shape[1] - extra.shape[1]
    return jnp.concatenate([values, extra, jnp.zeros((rows, left), BF16)], axis=1)


def shards(
    token_ids,
    page_ids,
    tap_layer,
    teacher_in,
    teacher_gain,
    teacher_gate,
    teacher_up,
    teacher_down,
    student_embed,
    student_gain,
    student_gate,
    student_up,
    student_down,
    projection,
):
    core = lax.axis_index("c")
    tokens, teacher_width = teacher_in.shape
    half = tokens // 2
    block = half // lax.axis_size("y")
    student_width = student_gain.shape[0]

    def halves_first(values):
        turned = jnp.concatenate([values[half:], values[:half]], axis=0)
        return jnp.where(core == 0, values, turned)

    ids = halves_first(token_ids)
    pages_of = halves_first(page_ids)
    teacher_rows = halves_first(teacher_in)
    row_start = lax.axis_index("y") * block

    pages = tap_layer.shape[0]
    member = pages_of[:, None] == jnp.arange(pages, dtype=jnp.int32)[None, :]
    counts = jnp.sum(member.astype(F32), axis=0)
    page_weight = 1.0 / (pages * counts)
    token_weight = jnp.sum(jnp.where(member, page_weight[None, :], 0.0), axis=1)
    token_tap = jnp.sum(jnp.where(member, tap_layer[None, :], 0), axis=1) == 1
    weight = lax.dynamic_slice_in_dim(token_weight, row_start, block, 0)[:, None]
    tap_scale = jnp.where(token_tap, 1.0, 0.0)[:, None]

    vocab_rows = student_embed.shape[0]
    local_ids = ids - lax.axis_index(MODEL) * vocab_rows
    inside = (local_ids >= 0) & (local_ids < vocab_rows)
    picked = jnp.take(student_embed, jnp.clip(local_ids, 0, vocab_rows - 1), axis=0)
    picked = jnp.where(inside[:, None], picked, jnp.zeros((), BF16))
    teacher_float = teacher_rows.astype(F32)
    teacher_square = jnp.sum(teacher_float * teacher_float, axis=1)
    first = sum_scatter(widen(picked, two_parts(teacher_square)), MODEL)
    student_in = first[:, :student_width]
    teacher_total = first[:, student_width] + first[:, student_width + 1]
    student_square = jnp.sum(student_in * student_in, axis=1)
    scaled = (student_in * student_gain.astype(F32)).astype(BF16)
    student_all = spread(
        widen(scaled, jnp.concatenate([two_parts(student_square), two_parts(teacher_total)], axis=1)),
        MODEL,
    )
    student_scaled = student_all[:, :student_width]
    teacher_square_all = student_all[:, student_width + 2].astype(F32) + student_all[
        :, student_width + 3
    ].astype(F32)

    teacher_scaled = (teacher_float * teacher_gain.astype(F32)).astype(BF16)
    teacher_both = jnp.concatenate([teacher_gate, teacher_up], axis=1)
    teacher_partial = product(teacher_scaled, teacher_both).astype(BF16)
    teacher_sums = sum_scatter(sum_scatter(teacher_partial, "x").astype(BF16), "zl")
    model_rows = tokens // lax.axis_size(MODEL)
    teacher_scale = lax.rsqrt(teacher_total / DT + EPS)[:, None]
    hidden_width = teacher_gate.shape[1]
    teacher_active, _ = silu_parts(teacher_sums[:, :hidden_width] * teacher_scale)
    teacher_share = (teacher_active * (teacher_sums[:, hidden_width:] * teacher_scale)).astype(BF16)
    teacher_hidden = spread(spread(teacher_share, "zl"), "x")

    columns = student_gate.shape[1]
    student_both = jnp.concatenate([student_gate, student_up], axis=1)
    depth = LANES - student_width
    carry = (jnp.arange(depth)[:, None] < 2) & (jnp.arange(128)[None, :] == 0)
    student_both = jnp.concatenate(
        [
            jnp.concatenate([student_both, jnp.zeros((student_width, 128), BF16)], axis=1),
            jnp.concatenate([jnp.zeros((depth, 2 * columns), BF16), carry.astype(BF16)], axis=1),
        ],
        axis=0,
    )
    sums = group_sum(
        product(student_all[:half], student_both), product(student_all[half:], student_both)
    )
    student_scale = lax.rsqrt(sums[:, 2 * columns : 2 * columns + 1] / DS + EPS)
    up_sum = sums[:, columns : 2 * columns] * student_scale
    active, slope = silu_parts(sums[:, :columns] * student_scale)
    hidden_mine, hidden_other = group_rows((active * up_sum).astype(BF16))

    down = jnp.concatenate(
        [product(hidden_mine, student_down), product(hidden_other, student_down)], axis=0
    ).astype(BF16)
    out_rows = (student_in + sum_scatter(down, MODEL)).astype(BF16)
    student_out = spread(out_rows, MODEL)

    def gap(rows):
        added = product(teacher_hidden[rows], teacher_down)
        return product(student_out[rows], projection) - tap_scale[rows] * added

    gap_sum = group_sum(gap(slice(0, half)), gap(slice(half, tokens)))
    base = lax.dynamic_slice_in_dim(teacher_in, core * half + row_start, block, 0)
    difference = gap_sum - base.astype(F32)
    loss_part = jnp.sum(weight * difference * difference) / DT
    pred_grad = (tokens / 16 * weight * difference).astype(BF16)
    pred_mine, pred_other = group_rows(pred_grad)
    pred_all = jnp.concatenate([pred_mine, pred_other], axis=0)
    grad_proj = transpose_product(student_out, pred_all)

    out_partial = jnp.concatenate(
        [product_transposed(pred_mine, projection), product_transposed(pred_other, projection)], axis=0
    ).astype(BF16)
    loss_columns = jnp.broadcast_to(two_parts(loss_part[None]), (tokens, 2))
    second = sum_scatter(widen(out_partial, loss_columns), MODEL)
    loss_sum = jnp.broadcast_to(second[0, student_width] + second[0, student_width + 1], (8, 128))
    loss_sum = loss_sum + lax.ppermute(loss_sum, "y", [(k, k ^ 1) for k in range(4)])
    loss_sum = loss_sum + lax.ppermute(loss_sum, "y", [(k, k ^ 2) for k in range(4)])
    loss_sum = loss_sum + swap(loss_sum, "c")
    loss = 0.5 * (loss_sum + swap(loss_sum, "zh"))[0, 0]
    out_grad = spread(second[:, :student_width].astype(BF16), MODEL)
    hidden_all = jnp.concatenate([hidden_mine, hidden_other], axis=0)
    grad_down = transpose_product(hidden_all, out_grad)

    hidden_grad = group_sum(
        product_transposed(out_grad[:half], student_down),
        product_transposed(out_grad[half:], student_down),
    )
    gate_grad = hidden_grad * up_sum * slope * student_scale
    up_grad = hidden_grad * active * student_scale
    both_mine, both_other = group_rows(jnp.concatenate([gate_grad, up_grad], axis=1).astype(BF16))
    both_grad = jnp.concatenate([both_mine, both_other], axis=0)
    grad_gate = transpose_product(student_scaled, both_grad[:, :columns])
    grad_up = transpose_product(student_scaled, both_grad[:, columns:])
    return (loss, grad_gate, grad_up, grad_down, grad_proj)


def solution(mesh):
    fine = Mesh(mesh.devices.reshape(2, 4, 2, 4, 4), ("zh", "y", "c", "x", "zl"))
    placed = (
        P(),
        P(),
        P(),
        P(None, MODEL),
        P(MODEL),
        P(MODEL, GROUP),
        P(MODEL, GROUP),
        P(GROUP, MODEL),
        P(MODEL, GROUP),
        P(GROUP),
        P(GROUP, MODEL),
        P(GROUP, MODEL),
        P(MODEL, GROUP),
        P(GROUP, MODEL),
    )
    return jax.shard_map(
        shards,
        mesh=fine,
        in_specs=placed,
        out_specs=(P(), P(GROUP, MODEL), P(GROUP, MODEL), P(MODEL, GROUP), P(GROUP, MODEL)),
        check_vma=False,
    )
```

time: 1130 us -> 311 us (0.28)
  waiting for transfers between devices: 784 us -> 120 us
  blocking collectives: 292 us -> 35.1 us
  starting transfers between devices: 0.37 us -> 101 us
  local copies, waits for them, and re-layouts: 7.31 us -> 21.1 us
    psum x3 -> x0, waiting for transfers between devices: 451 us -> none  [the longest x1 157 us: shards(): lax.psum(down_partial.astype(jnp.bfloat16), 'mp').astype(jnp.float32)]
    reduce_scatter x5 -> x0, waiting for transfers between devices: 251 us -> none  [the longest x1 84.6 us: shards(): lax.psum_scatter(jnp.dot(rows, projection, preferred_element_type=jnp.flo...]
    psum x3 -> x0, blocking collectives: 173 us -> none  [the longest x1 86.1 us: shards(): lax.psum(jnp.sum(weight[:, None] * difference * difference) / DT, ('group...]
    all_gather x4 -> x0, blocking collectives: 120 us -> none  [the longest x1 31 us: shards(): lax.all_gather(up_share, 'group', axis=0, tiled=True)]
    all_to_all x0 -> x13, waiting for transfers between devices: none -> 106 us  [exchange(): return lax.all_to_all(values, axis, 0, 0, tiled=True)]
    all_gather x1 -> x0, waiting for transfers between devices: 81.5 us -> none  [shards(): lax.all_gather(teacher_share, 'mp', axis=0, tiled=True)]
    all_to_all x0 -> x13, starting transfers between devices: none -> 54.7 us  [exchange(): return lax.all_to_all(values, axis, 0, 0, tiled=True)]
    ppermute x0 -> x13, starting transfers between devices: none -> 45.9 us  [the longest x11 41.7 us: swap(): return lax.ppermute(values, axis, SWAP)]
  transfers between devices with their start and end apart: 9 -> 26, of which waited for: 8 -> 21; matrix products, arithmetic and copies ran while one was open for 1% -> 5% of each run, Pallas kernels for 0% -> 0%
where the time goes in v1:
time: 311 us; the launch traced here: 309 us
  waiting for transfers between devices  120 us (39%)
  starting transfers between devices  101 us (32%)
  blocking collectives  35.1 us (11%)
  local copies, waits for them, and re-layouts  21.1 us (7%)
  matrix products  14.7 us (5%)
  other arithmetic  10.9 us (4%)
  between operations  6.86 us (2%)
    all_to_all x13, waiting for transfers between devices, exchange(): return lax.all_to_all(values, axis, 0, 0, tiled=True)  106 us
    all_to_all x13, starting transfers between devices, exchange(): return lax.all_to_all(values, axis, 0, 0, tiled=True)  54.7 us
    ppermute x11, starting transfers between devices, swap(): return lax.ppermute(values, axis, SWAP)  41.7 us
    all_to_all x3, blocking collectives, exchange(): return lax.all_to_all(values, axis, 0, 0, tiled=True)  35.1 us
    ppermute x11, waiting for transfers between devices, swap(): return lax.ppermute(values, axis, SWAP)  11.5 us
    dot_general x9, matrix products, product(): return jnp.dot(left, right, preferred_element_type=F32)  8.04 us
  transfers between devices with their start and end apart: 26, of which 21 were waited for; matrix products, arithmetic and copies ran while one was open for 5% of the time, Pallas kernels for 0%

profile of v1, /device:TPU:1, one launch (start us, length us, event | category | flops | bytes accessed | tf_op | source)
XLA Modules:
  0.0 309.1 jit_solution(15602413322600081831)
XLA Ops:
  5.6 3.6 %copy.48 = bf16[4752,224]{1,0:T(8,128)(2,1)S(1)} copy(bf16[4752,224]{0,1:T(8,128)(2,1)} %param.22) | data formatting | bytes 4257792 | tf_op args[8]
  14.8 9.1 %all-to-all-start = ((bf16[16,32,256]{2,1,0:T(8,128)(2,1)}), bf16[16,32,256]{2,1,0:T(8,128)(2,1)S(1)}, u32[]{:S(2)}, u32[]{:S(2)}) async-start(bf16[16,32,256]{2,1,0:T(8,128)(2,1)} %maximum_maximum_fusion), calls=%async_computation | async-start | bytes 524288 | tf_op jit(solution)/shard_map/all_to_all | solution.py:41
  24.0 8.5 %all-to-all-done = bf16[16,32,256]{2,1,0:T(8,128)(2,1)S(1)} async-done(((bf16[16,32,256]{2,1,0:T(8,128)(2,1)}), bf16[16,32,256]{2,1,0:T(8,128)(2,1)S(1)}, u32[]{:S(2)}, u32[]{:S(2)}) %all-to-all-start) | async-done | bytes 262176 | tf_op jit(solution)/shard_map/all_to_all | solution.py:41
  33.9 4.9 %all-to-all-start.1 = ((bf16[16,32,256]{2,1,0:T(8,128)(2,1)}), bf16[16,32,256]{2,1,0:T(8,128)(2,1)S(1)}, u32[]{:S(2)}, u32[]{:S(2)}) async-start(bf16[16,32,256]{2,1,0:T(8,128)(2,1)} %broadcast_in_dim.150), calls=%async_computation.1 | async-start | bytes 524288 | tf_op jit(solution)/shard_map/all_to_all | solution.py:41
  39.0 8.4 %all-to-all-done.1 = bf16[16,32,256]{2,1,0:T(8,128)(2,1)S(1)} async-done(((bf16[16,32,256]{2,1,0:T(8,128)(2,1)}), bf16[16,32,256]{2,1,0:T(8,128)(2,1)S(1)}, u32[]{:S(2)}, u32[]{:S(2)}) %all-to-all-start.1) | async-done | bytes 262176 | tf_op jit(solution)/shard_map/all_to_all | solution.py:41
  54.5 4.3 %all-to-all-start.2 = ((bf16[4,64,1408]{2,1,0:T(8,128)(2,1)}), bf16[4,64,1408]{2,1,0:T(8,128)(2,1)}, u32[]{:S(2)}, u32[]{:S(2)}) async-start(bf16[4,64,1408]{2,1,0:T(8,128)(2,1)} %bitcast.4), calls=%async_computation.2 | async-start | bytes 1441792 | tf_op jit(solution)/shard_map/all_to_all | solution.py:41
  58.9 3.8 %convolution_convert_fusion = bf16[512,2048]{1,0:T(8,128)(2,1)} fusion(bf16[512,1024]{1,0:T(8,128)(2,1)S(1)} %copy-done.19, bf16[512,1024]{1,0:T(8,128)(2,1)} %param.19, f32[512]{0:T(512)S(1)} %convert_element_type.146, bf16[512,512]{1,0:T(8,128)(2,1)S(1)} %copy-done.4, bf16[256,512]{1,0:T(8,128)(2,1)S(1)} %copy-done.13, ...), kind=kOutput, calls=%fused_computation.1 | convolution fusion | flops 1081081856 | bytes 5244929 | tf_op jit(solution)/shard_map/dot_general | solution.py:25
  62.7 7.2 %all-to-all-done.2 = bf16[4,64,1408]{2,1,0:T(8,128)(2,1)} async-done(((bf16[4,64,1408]{2,1,0:T(8,128)(2,1)}), bf16[4,64,1408]{2,1,0:T(8,128)(2,1)}, u32[]{:S(2)}, u32[]{:S(2)}) %all-to-all-start.2) | async-done | bytes 720928 | tf_op jit(solution)/shard_map/all_to_all | solution.py:41
  69.9 3.6 %all-to-all-start.6 = ((bf16[4,128,2048]{2,1,0:T(8,128)(2,1)}), bf16[4,128,2048]{2,1,0:T(8,128)(2,1)S(1)}, u32[]{:S(2)}, u32[]{:S(2)}) async-start(bf16[4,128,2048]{2,1,0:T(8,128)(2,1)} %bitcast.58), calls=%async_computation.6 | async-start | bytes 4194304 | tf_op jit(solution)/shard_map/all_to_all | solution.py:41
  75.5 4.2 %collective-permute-start.1 = (bf16[64,1408]{1,0:T(8,128)(2,1)}, bf16[64,1408]{1,0:T(8,128)(2,1)}, u32[]{:S(2)}, u32[]{:S(2)}) collective-permute-start(bf16[64,1408]{1,0:T(8,128)(2,1)} %convert_element_type.140), channel_id=1, source_target_pairs={{0,128},{128,0},{1,129},{129,1},{2,130},{130,2},{3,131},{131,3},{4... | collective-permute-start | bytes 540680 | tf_op jit(solution)/shard_map/ppermute | solution.py:37
  79.7 18.7 %all-to-all-done.6 = bf16[4,128,2048]{2,1,0:T(8,128)(2,1)S(1)} async-done(((bf16[4,128,2048]{2,1,0:T(8,128)(2,1)}), bf16[4,128,2048]{2,1,0:T(8,128)(2,1)S(1)}, u32[]{:S(2)}, u32[]{:S(2)}) %all-to-all-start.6) | async-done | bytes 2097184 | tf_op jit(solution)/shard_map/all_to_all | solution.py:41
  99.7 3.5 %all-to-all-start.7 = ((bf16[4,32,2048]{2,1,0:T(8,128)(2,1)}), bf16[4,32,2048]{2,1,0:T(8,128)(2,1)S(1)}, u32[]{:S(2)}, u32[]{:S(2)}) async-start(bf16[4,32,2048]{2,1,0:T(8,128)(2,1)} %bitcast.60), calls=%async_computation.7 | async-start | bytes 1048576 | tf_op jit(solution)/shard_map/all_to_all | solution.py:41
  104.4 11.9 %all-to-all-done.7 = bf16[4,32,2048]{2,1,0:T(8,128)(2,1)S(1)} async-done(((bf16[4,32,2048]{2,1,0:T(8,128)(2,1)}), bf16[4,32,2048]{2,1,0:T(8,128)(2,1)S(1)}, u32[]{:S(2)}, u32[]{:S(2)}) %all-to-all-start.7) | async-done | bytes 524320 | tf_op jit(solution)/shard_map/all_to_all | solution.py:41
  120.6 5.8 %all-to-all-done.3 = bf16[4,64,640]{2,1,0:T(8,128)(2,1)S(1)} async-done(((bf16[4,64,640]{2,1,0:T(8,128)(2,1)}), bf16[4,64,640]{2,1,0:T(8,128)(2,1)S(1)}, u32[]{:S(2)}, u32[]{:S(2)}) %all-to-all-start.3) | async-done | bytes 327712 | tf_op jit(solution)/shard_map/all_to_all | solution.py:41
  135.6 6.5 %all-to-all-done.8 = bf16[4,32,1024]{2,1,0:T(8,128)(2,1)S(1)} async-done(((bf16[4,32,1024]{2,1,0:T(8,128)(2,1)}), bf16[4,32,1024]{2,1,0:T(8,128)(2,1)S(1)}, u32[]{:S(2)}, u32[]{:S(2)}) %all-to-all-start.8) | async-done | bytes 262176 | tf_op jit(solution)/shard_map/all_to_all | solution.py:41
  142.0 4.2 %all-to-all-start.4 = ((bf16[16,32,224]{2,1,0:T(8,128)(2,1)}), bf16[16,32,224]{2,1,0:T(8,128)(2,1)S(1)}, u32[]{:S(2)}, u32[]{:S(2)}) async-start(bf16[16,32,224]{2,1,0:T(8,128)(2,1)} %bitcast.6), calls=%async_computation.4 | async-start | bytes 524288 | tf_op jit(solution)/shard_map/all_to_all | solution.py:41
  146.2 9.7 %all-to-all-done.4 = bf16[16,32,224]{2,1,0:T(8,128)(2,1)S(1)} async-done(((bf16[16,32,224]{2,1,0:T(8,128)(2,1)}), bf16[16,32,224]{2,1,0:T(8,128)(2,1)S(1)}, u32[]{:S(2)}, u32[]{:S(2)}) %all-to-all-start.4) | async-done | bytes 229408 | tf_op jit(solution)/shard_map/all_to_all | solution.py:41
  157.0 3.5 %all-to-all-start.9 = ((bf16[4,128,1024]{2,1,0:T(8,128)(2,1)}), bf16[4,128,1024]{2,1,0:T(8,128)(2,1)S(1)}, u32[]{:S(2)}, u32[]{:S(2)}) async-start(bf16[4,128,1024]{2,1,0:T(8,128)(2,1)} %broadcast_in_dim.160), calls=%async_computation.9 | async-start | bytes 2097152 | tf_op jit(solution)/shard_map/all_to_all | solution.py:41
  160.7 12.7 %all-to-all-done.9 = bf16[4,128,1024]{2,1,0:T(8,128)(2,1)S(1)} async-done(((bf16[4,128,1024]{2,1,0:T(8,128)(2,1)}), bf16[4,128,1024]{2,1,0:T(8,128)(2,1)S(1)}, u32[]{:S(2)}, u32[]{:S(2)}) %all-to-all-start.9) | async-done | bytes 1048608 | tf_op jit(solution)/shard_map/all_to_all | solution.py:41
  174.2 4.2 %all-to-all-start.5 = ((bf16[16,32,224]{2,1,0:T(8,128)(2,1)}), bf16[16,32,224]{2,1,0:T(8,128)(2,1)}, u32[]{:S(2)}, u32[]{:S(2)}) async-start(bf16[16,32,224]{2,1,0:T(8,128)(2,1)} %broadcast_in_dim.153), calls=%async_computation.5 | async-start | bytes 524288 | tf_op jit(solution)/shard_map/all_to_all | solution.py:41
  179.3 7.2 %all-to-all-done.5 = bf16[16,32,224]{2,1,0:T(8,128)(2,1)} async-done(((bf16[16,32,224]{2,1,0:T(8,128)(2,1)}), bf16[16,32,224]{2,1,0:T(8,128)(2,1)}, u32[]{:S(2)}, u32[]{:S(2)}) %all-to-all-start.5) | async-done | bytes 229408 | tf_op jit(solution)/shard_map/all_to_all | solution.py:41
  188.2 4.2 %collective-permute-start.3 = (bf16[256,512]{1,0:T(8,128)(2,1)S(1)}, bf16[256,512]{1,0:T(8,128)(2,1)S(1)}, u32[]{:S(2)}, u32[]{:S(2)}) collective-permute-start(bf16[256,512]{1,0:T(8,128)(2,1)S(1)} %fusion.5), channel_id=1, source_target_pairs={{0,16},{16,0},{1,17},{17,1},{2,18},{18,2},{3,19},{19,3},{4,20},{20... | collective-permute-start | bytes 786440 | tf_op jit(solution)/shard_map/ppermute | solution.py:37
  198.3 6.0 %all-to-all-done.10 = bf16[4,64,512]{2,1,0:T(8,128)(2,1)S(1)} async-done(((bf16[4,64,512]{2,1,0:T(8,128)(2,1)}), bf16[4,64,512]{2,1,0:T(8,128)(2,1)S(1)}, u32[]{:S(2)}, u32[]{:S(2)}) %all-to-all-start.10) | async-done | bytes 262176 | tf_op jit(solution)/shard_map/all_to_all | solution.py:41
  204.3 4.3 %collective-permute-start.4 = (bf16[64,512]{1,0:T(8,128)(2,1)S(1)}, bf16[64,512]{1,0:T(8,128)(2,1)S(1)}, u32[]{:S(2)}, u32[]{:S(2)}) collective-permute-start(bf16[64,512]{1,0:T(8,128)(2,1)S(1)} %convert_element_type.155), channel_id=1, source_target_pairs={{0,128},{128,0},{1,129},{129,1},{2,130},{130,2},{3,131},{131,3},{4... | collective-permute-start | bytes 196616 | tf_op jit(solution)/shard_map/ppermute | solution.py:37
  222.6 4.5 %collective-permute-start.5 = (bf16[256,512]{1,0:T(8,128)(2,1)S(1)}, bf16[256,512]{1,0:T(8,128)(2,1)S(1)}, u32[]{:S(2)}, u32[]{:S(2)}) collective-permute-start(bf16[256,512]{1,0:T(8,128)(2,1)S(1)} %bitcast.67), channel_id=1, source_target_pairs={{0,16},{16,0},{1,17},{17,1},{2,18},{18,2},{3,19},{19,3},{4,20},{20... | collective-permute-start | bytes 786440 | tf_op jit(solution)/shard_map/ppermute | solution.py:37
  228.7 12.6 %all_to_all.129 = bf16[16,32,256]{2,1,0:T(8,128)(2,1)S(1)} all-to-all(bf16[16,32,256]{2,1,0:T(8,128)(2,1)S(1)} %maximum_maximum_fusion.1), channel_id=1, replica_groups=mesh['zh'=2,'y'=4,'c'=2,'x'=4,'zl'=4] {'x','zl'}, dimensions={0} | all-to-all | bytes 524288 | tf_op jit(solution)/shard_map/all_to_all | solution.py:41
  241.4 13.3 %all_to_all.130 = bf16[16,32,224]{2,1,0:T(8,128)(2,1)S(1)} all-to-all(bf16[16,32,224]{2,1,0:T(8,128)(2,1)S(1)} %broadcast_in_dim.165), channel_id=1, replica_groups=mesh['zh'=2,'y'=4,'c'=2,'x'=4,'zl'=4] {'x','zl'}, dimensions={0} | all-to-all | bytes 458752 | tf_op jit(solution)/shard_map/all_to_all | solution.py:41
  258.8 9.2 %all_to_all.131 = bf16[4,64,640]{2,1,0:T(8,128)(2,1)S(1)} all-to-all(bf16[4,64,640]{2,1,0:T(8,128)(2,1)S(1)} %bitcast.65), channel_id=1, replica_groups=mesh['zh'=2,'y'=4,'c'=2,'x'=4,'zl'=4] {'y'}, dimensions={0} | all-to-all | bytes 655360 | tf_op jit(solution)/shard_map/all_to_all | solution.py:41
  268.0 4.5 %collective-permute-start.11 = (bf16[64,640]{1,0:T(8,128)(2,1)S(1)}, bf16[64,640]{1,0:T(8,128)(2,1)S(1)}, u32[]{:S(2)}, u32[]{:S(2)}) collective-permute-start(bf16[64,640]{1,0:T(8,128)(2,1)S(1)} %convert_element_type.165), channel_id=1, source_target_pairs={{0,128},{128,0},{1,129},{129,1},{2,130},{130,2},{3,131},{131,3},{4... | collective-permute-start | bytes 245768 | tf_op jit(solution)/shard_map/ppermute | solution.py:37
  276.5 3.6 %all-to-all-start.15 = ((bf16[4,64,1280]{2,1,0:T(8,128)(2,1)}), bf16[4,64,1280]{2,1,0:T(8,128)(2,1)S(1)}, u32[]{:S(2)}, u32[]{:S(2)}) async-start(bf16[4,64,1280]{2,1,0:T(8,128)(2,1)} %broadcast_in_dim.166), calls=%async_computation.15 | async-start | bytes 1310720 | tf_op jit(solution)/shard_map/all_to_all | solution.py:41
  288.9 4.6 %collective-permute-start.12 = (bf16[256,1280]{1,0:T(8,128)(2,1)S(1)}, bf16[256,1280]{1,0:T(8,128)(2,1)S(1)}, u32[]{:S(2)}, u32[]{:S(2)}) collective-permute-start(bf16[256,1280]{1,0:T(8,128)(2,1)S(1)} %bitcast.53), channel_id=1, source_target_pairs={{0,16},{16,0},{1,17},{17,1},{2,18},{18,2},{3,19},{19,3},{4,20},{20... | collective-permute-start | bytes 1966088 | tf_op jit(solution)/shard_map/ppermute | solution.py:37
  296.8 4.0 %collective-permute-start.9 = (f32[8,128]{1,0:T(8,128)S(1)}, f32[8,128]{1,0:T(8,128)S(1)}, u32[]{:S(2)}, u32[]{:S(2)}) collective-permute-start(f32[8,128]{1,0:T(8,128)S(1)} %add.106), channel_id=1, source_target_pairs={{0,128},{128,0},{1,129},{129,1},{2,130},{130,2},{3,131},{131,3},{4... | collective-permute-start | bytes 12296 | tf_op jit(solution)/shard_map/ppermute | solution.py:37
  (171 shorter events, 85.8 us)
Async XLA Ops:
  0.6 187.1 %copy-start = (bf16[1024,512]{1,0:T(8,128)(2,1)S(1)}, bf16[1024,512]{1,0:T(8,128)(2,1)}, u32[]{:S(2)}) copy-start(bf16[1024,512]{1,0:T(8,128)(2,1)} %param.21) | copy-start | bytes 3145732
  14.8 32.7 %copy-start.20 = (bf16[224,640]{1,0:T(8,128)(2,1)S(1)}, bf16[224,640]{1,0:T(8,128)(2,1)}, u32[]{:S(2)}) copy-start(bf16[224,640]{1,0:T(8,128)(2,1)} %param.25) | copy-start | bytes 860164
  14.8 32.7 %copy-start.21 = (bf16[224,640]{1,0:T(8,128)(2,1)S(1)}, bf16[224,640]{1,0:T(8,128)(2,1)}, u32[]{:S(2)}) copy-start(bf16[224,640]{1,0:T(8,128)(2,1)} %param.24) | copy-start | bytes 860164
  14.8 17.7 %all-to-all-start = ((bf16[16,32,256]{2,1,0:T(8,128)(2,1)}), bf16[16,32,256]{2,1,0:T(8,128)(2,1)S(1)}, u32[]{:S(2)}, u32[]{:S(2)}) async-start(bf16[16,32,256]{2,1,0:T(8,128)(2,1)} %maximum_maximum_fusion), calls=%async_computation | async-start | bytes 524288 | tf_op jit(solution)/shard_map/all_to_all | solution.py:41
  33.9 13.5 %all-to-all-start.1 = ((bf16[16,32,256]{2,1,0:T(8,128)(2,1)}), bf16[16,32,256]{2,1,0:T(8,128)(2,1)S(1)}, u32[]{:S(2)}, u32[]{:S(2)}) async-start(bf16[16,32,256]{2,1,0:T(8,128)(2,1)} %broadcast_in_dim.150), calls=%async_computation.1 | async-start | bytes 524288 | tf_op jit(solution)/shard_map/all_to_all | solution.py:41
  48.1 5.1 %collective-permute-start = (bf16[256,1408]{1,0:T(8,128)(2,1)S(1)}, bf16[256,1408]{1,0:T(8,128)(2,1)S(1)}, u32[]{:S(2)}, u32[]{:S(2)}) collective-permute-start(bf16[256,1408]{1,0:T(8,128)(2,1)S(1)} %convolution_convert_fusion.1), channel_id=1, source_target_pairs={{0,16},{16,0},{1,17},{17,1},{2,18},{18,2},{3,19},{19,3},{4,20},{20... | collective-permute-start | bytes 2162696 | tf_op jit(solution)/shard_map/ppermute | solution.py:37
  54.5 15.5 %all-to-all-start.2 = ((bf16[4,64,1408]{2,1,0:T(8,128)(2,1)}), bf16[4,64,1408]{2,1,0:T(8,128)(2,1)}, u32[]{:S(2)}, u32[]{:S(2)}) async-start(bf16[4,64,1408]{2,1,0:T(8,128)(2,1)} %bitcast.4), calls=%async_computation.2 | async-start | bytes 1441792 | tf_op jit(solution)/shard_map/all_to_all | solution.py:41
  69.9 28.4 %all-to-all-start.6 = ((bf16[4,128,2048]{2,1,0:T(8,128)(2,1)}), bf16[4,128,2048]{2,1,0:T(8,128)(2,1)S(1)}, u32[]{:S(2)}, u32[]{:S(2)}) async-start(bf16[4,128,2048]{2,1,0:T(8,128)(2,1)} %bitcast.58), calls=%async_computation.6 | async-start | bytes 4194304 | tf_op jit(solution)/shard_map/all_to_all | solution.py:41
  75.5 27.7 %collective-permute-start.1 = (bf16[64,1408]{1,0:T(8,128)(2,1)}, bf16[64,1408]{1,0:T(8,128)(2,1)}, u32[]{:S(2)}, u32[]{:S(2)}) collective-permute-start(bf16[64,1408]{1,0:T(8,128)(2,1)} %convert_element_type.140), channel_id=1, source_target_pairs={{0,128},{128,0},{1,129},{129,1},{2,130},{130,2},{3,131},{131,3},{4... | collective-permute-start | bytes 540680 | tf_op jit(solution)/shard_map/ppermute | solution.py:37
  99.7 16.6 %all-to-all-start.7 = ((bf16[4,32,2048]{2,1,0:T(8,128)(2,1)}), bf16[4,32,2048]{2,1,0:T(8,128)(2,1)S(1)}, u32[]{:S(2)}, u32[]{:S(2)}) async-start(bf16[4,32,2048]{2,1,0:T(8,128)(2,1)} %bitcast.60), calls=%async_computation.7 | async-start | bytes 1048576 | tf_op jit(solution)/shard_map/all_to_all | solution.py:41
  104.4 29.7 %copy-start.1 = (bf16[640,224]{0,1:T(8,128)(2,1)S(1)}, bf16[640,224]{0,1:T(8,128)(2,1)}, u32[]{:S(2)}) copy-start(bf16[640,224]{0,1:T(8,128)(2,1)} %param.26) | copy-start | bytes 860164
  117.1 9.3 %all-to-all-start.3 = ((bf16[4,64,640]{2,1,0:T(8,128)(2,1)}), bf16[4,64,640]{2,1,0:T(8,128)(2,1)S(1)}, u32[]{:S(2)}, u32[]{:S(2)}) async-start(bf16[4,64,640]{2,1,0:T(8,128)(2,1)} %broadcast_in_dim.152), calls=%async_computation.3 | async-start | bytes 655360 | tf_op jit(solution)/shard_map/all_to_all | solution.py:41
  126.4 8.0 %collective-permute-start.2 = (bf16[256,640]{1,0:T(8,128)(2,1)S(1)}, bf16[256,640]{1,0:T(8,128)(2,1)S(1)}, u32[]{:S(2)}, u32[]{:S(2)}) collective-permute-start(bf16[256,640]{1,0:T(8,128)(2,1)S(1)} %bitcast.62), channel_id=1, source_target_pairs={{0,16},{16,0},{1,17},{17,1},{2,18},{18,2},{3,19},{19,3},{4,20},{20... | collective-permute-start | bytes 983048 | tf_op jit(solution)/shard_map/ppermute | solution.py:37
  130.6 11.4 %all-to-all-start.8 = ((bf16[4,32,1024]{2,1,0:T(8,128)(2,1)}), bf16[4,32,1024]{2,1,0:T(8,128)(2,1)S(1)}, u32[]{:S(2)}, u32[]{:S(2)}) async-start(bf16[4,32,1024]{2,1,0:T(8,128)(2,1)} %broadcast_in_dim.158), calls=%async_computation.8 | async-start | bytes 524288 | tf_op jit(solution)/shard_map/all_to_all | solution.py:41
  142.0 13.9 %all-to-all-start.4 = ((bf16[16,32,224]{2,1,0:T(8,128)(2,1)}), bf16[16,32,224]{2,1,0:T(8,128)(2,1)S(1)}, u32[]{:S(2)}, u32[]{:S(2)}) async-start(bf16[16,32,224]{2,1,0:T(8,128)(2,1)} %bitcast.6), calls=%async_computation.4 | async-start | bytes 524288 | tf_op jit(solution)/shard_map/all_to_all | solution.py:41
  157.0 16.5 %all-to-all-start.9 = ((bf16[4,128,1024]{2,1,0:T(8,128)(2,1)}), bf16[4,128,1024]{2,1,0:T(8,128)(2,1)S(1)}, u32[]{:S(2)}, u32[]{:S(2)}) async-start(bf16[4,128,1024]{2,1,0:T(8,128)(2,1)} %broadcast_in_dim.160), calls=%async_computation.9 | async-start | bytes 2097152 | tf_op jit(solution)/shard_map/all_to_all | solution.py:41
  174.2 12.3 %all-to-all-start.5 = ((bf16[16,32,224]{2,1,0:T(8,128)(2,1)}), bf16[16,32,224]{2,1,0:T(8,128)(2,1)}, u32[]{:S(2)}, u32[]{:S(2)}) async-start(bf16[16,32,224]{2,1,0:T(8,128)(2,1)} %broadcast_in_dim.153), calls=%async_computation.5 | async-start | bytes 524288 | tf_op jit(solution)/shard_map/all_to_all | solution.py:41
  188.2 5.4 %collective-permute-start.3 = (bf16[256,512]{1,0:T(8,128)(2,1)S(1)}, bf16[256,512]{1,0:T(8,128)(2,1)S(1)}, u32[]{:S(2)}, u32[]{:S(2)}) collective-permute-start(bf16[256,512]{1,0:T(8,128)(2,1)S(1)} %fusion.5), channel_id=1, source_target_pairs={{0,16},{16,0},{1,17},{17,1},{2,18},{18,2},{3,19},{19,3},{4,20},{20... | collective-permute-start | bytes 786440 | tf_op jit(solution)/shard_map/ppermute | solution.py:37
  194.7 9.5 %all-to-all-start.10 = ((bf16[4,64,512]{2,1,0:T(8,128)(2,1)}), bf16[4,64,512]{2,1,0:T(8,128)(2,1)S(1)}, u32[]{:S(2)}, u32[]{:S(2)}) async-start(bf16[4,64,512]{2,1,0:T(8,128)(2,1)} %bitcast.14), calls=%async_computation.10 | async-start | bytes 524288 | tf_op jit(solution)/shard_map/all_to_all | solution.py:41
  204.3 7.1 %collective-permute-start.4 = (bf16[64,512]{1,0:T(8,128)(2,1)S(1)}, bf16[64,512]{1,0:T(8,128)(2,1)S(1)}, u32[]{:S(2)}, u32[]{:S(2)}) collective-permute-start(bf16[64,512]{1,0:T(8,128)(2,1)S(1)} %convert_element_type.155), channel_id=1, source_target_pairs={{0,128},{128,0},{1,129},{129,1},{2,130},{130,2},{3,131},{131,3},{4... | collective-permute-start | bytes 196616 | tf_op jit(solution)/shard_map/ppermute | solution.py:37
  213.7 8.9 %all-to-all-start.11 = ((bf16[4,64,512]{2,1,0:T(8,128)(2,1)}), bf16[4,64,512]{2,1,0:T(8,128)(2,1)S(1)}, u32[]{:S(2)}, u32[]{:S(2)}) async-start(bf16[4,64,512]{2,1,0:T(8,128)(2,1)} %broadcast_in_dim.161), calls=%async_computation.11 | async-start | bytes 524288 | tf_op jit(solution)/shard_map/all_to_all | solution.py:41
  222.6 5.6 %collective-permute-start.5 = (bf16[256,512]{1,0:T(8,128)(2,1)S(1)}, bf16[256,512]{1,0:T(8,128)(2,1)S(1)}, u32[]{:S(2)}, u32[]{:S(2)}) collective-permute-start(bf16[256,512]{1,0:T(8,128)(2,1)S(1)} %bitcast.67), channel_id=1, source_target_pairs={{0,16},{16,0},{1,17},{17,1},{2,18},{18,2},{3,19},{19,3},{4,20},{20... | collective-permute-start | bytes 786440 | tf_op jit(solution)/shard_map/ppermute | solution.py:37
  255.0 3.5 %collective-permute-start.10 = (bf16[256,640]{1,0:T(8,128)(2,1)S(1)}, bf16[256,640]{1,0:T(8,128)(2,1)S(1)}, u32[]{:S(2)}, u32[]{:S(2)}) collective-permute-start(bf16[256,640]{1,0:T(8,128)(2,1)S(1)} %convolution_convert_fusion.2), channel_id=1, source_target_pairs={{0,16},{16,0},{1,17},{17,1},{2,18},{18,2},{3,19},{19,3},{4,20},{20... | collective-permute-start | bytes 983048 | tf_op jit(solution)/shard_map/ppermute | solution.py:37
  268.0 7.4 %collective-permute-start.11 = (bf16[64,640]{1,0:T(8,128)(2,1)S(1)}, bf16[64,640]{1,0:T(8,128)(2,1)S(1)}, u32[]{:S(2)}, u32[]{:S(2)}) collective-permute-start(bf16[64,640]{1,0:T(8,128)(2,1)S(1)} %convert_element_type.165), channel_id=1, source_target_pairs={{0,128},{128,0},{1,129},{129,1},{2,130},{130,2},{3,131},{131,3},{4... | collective-permute-start | bytes 245768 | tf_op jit(solution)/shard_map/ppermute | solution.py:37
  276.5 27.9 %copy-start.9 = (bf16[4,64,640]{2,1,0:T(8,128)(2,1)S(1)}, bf16[4,64,640]{2,1,0:T(8,128)(2,1)}, u32[]{:S(2)}) copy-start(bf16[4,64,640]{2,1,0:T(8,128)(2,1)} %copy-done.8) | copy-start | bytes 983044
  276.5 27.9 %copy-start.15 = (bf16[256,640]{1,0:T(8,128)(2,1)S(1)}, bf16[256,640]{1,0:T(8,128)(2,1)}, u32[]{:S(2)}) copy-start(bf16[256,640]{1,0:T(8,128)(2,1)} %copy-done.14) | copy-start | bytes 983044
  276.5 12.5 %all-to-all-start.15 = ((bf16[4,64,1280]{2,1,0:T(8,128)(2,1)}), bf16[4,64,1280]{2,1,0:T(8,128)(2,1)S(1)}, u32[]{:S(2)}, u32[]{:S(2)}) async-start(bf16[4,64,1280]{2,1,0:T(8,128)(2,1)} %broadcast_in_dim.166), calls=%async_computation.15 | async-start | bytes 1310720 | tf_op jit(solution)/shard_map/all_to_all | solution.py:41
  282.0 4.2 %collective-permute-start.6 = (f32[8,128]{1,0:T(8,128)S(1)}, f32[8,128]{1,0:T(8,128)S(1)}, u32[]{:S(2)}, u32[]{:S(2)}) collective-permute-start(f32[8,128]{1,0:T(8,128)S(1)} %broadcast_in_dim.164), channel_id=1, source_target_pairs={{0,32},{32,0},{64,96},{96,64},{1,33},{33,1},{65,97},{97,65},{2,34}... | collective-permute-start | bytes 12296 | tf_op jit(solution)/shard_map/ppermute | solution.py:196
  286.3 7.3 %collective-permute-start.7 = (f32[8,128]{1,0:T(8,128)S(1)}, f32[8,128]{1,0:T(8,128)S(1)}, u32[]{:S(2)}, u32[]{:S(2)}) collective-permute-start(f32[8,128]{1,0:T(8,128)S(1)} %broadcast_add_fusion), channel_id=1, source_target_pairs={{0,64},{32,96},{64,0},{96,32},{1,65},{33,97},{65,1},{97,33},{2,66}... | collective-permute-start | bytes 12296 | tf_op jit(solution)/shard_map/ppermute | solution.py:197
  288.9 16.6 %collective-permute-start.12 = (bf16[256,1280]{1,0:T(8,128)(2,1)S(1)}, bf16[256,1280]{1,0:T(8,128)(2,1)S(1)}, u32[]{:S(2)}, u32[]{:S(2)}) collective-permute-start(bf16[256,1280]{1,0:T(8,128)(2,1)S(1)} %bitcast.53), channel_id=1, source_target_pairs={{0,16},{16,0},{1,17},{17,1},{2,18},{18,2},{3,19},{19,3},{4,20},{20... | collective-permute-start | bytes 1966088 | tf_op jit(solution)/shard_map/ppermute | solution.py:37
  293.6 3.2 %collective-permute-start.8 = (f32[8,128]{1,0:T(8,128)S(1)}, f32[8,128]{1,0:T(8,128)S(1)}, u32[]{:S(2)}, u32[]{:S(2)}) collective-permute-start(f32[8,128]{1,0:T(8,128)S(1)} %fusion.79), channel_id=1, source_target_pairs={{0,16},{16,0},{1,17},{17,1},{2,18},{18,2},{3,19},{19,3},{4,20},{20... | collective-permute-start | bytes 12296 | tf_op jit(solution)/shard_map/ppermute | solution.py:37
  296.8 6.4 %collective-permute-start.9 = (f32[8,128]{1,0:T(8,128)S(1)}, f32[8,128]{1,0:T(8,128)S(1)}, u32[]{:S(2)}, u32[]{:S(2)}) collective-permute-start(f32[8,128]{1,0:T(8,128)S(1)} %add.106), channel_id=1, source_target_pairs={{0,128},{128,0},{1,129},{129,1},{2,130},{130,2},{3,131},{131,3},{4... | collective-permute-start | bytes 12296 | tf_op jit(solution)/shard_map/ppermute | solution.py:37
  (17 other events, 95.4 us)

commit v2 on v1

v2 whole, which is shorter than its diff:
```python
import jax
import jax.numpy as jnp
from jax import lax
from jax.sharding import Mesh, PartitionSpec as P

DT = 8192
DS = 3584

EPS = 1e-06

F32 = jnp.float32
BF16 = jnp.bfloat16
GROUP = ("zh", "y", "c")
NEAR = ("y", "c")
MODEL = ("x", "zl")
SWAP = [(0, 1), (1, 0)]
LANES = 256


def silu_parts(values):
    sigmoid = jax.nn.sigmoid(values)
    return (values * sigmoid, sigmoid * (1.0 + values * (1.0 - sigmoid)))


def product(left, right):
    return jnp.dot(left, right, preferred_element_type=F32)


def transpose_product(left, right):
    return lax.dot_general(left, right, (((0,), (0,)), ((), ())), preferred_element_type=F32)


def product_transposed(left, right):
    return lax.dot_general(left, right, (((1,), (1,)), ((), ())), preferred_element_type=F32)


def swap(values, axis):
    return lax.ppermute(values, axis, SWAP)


def exchange(values, axis):
    return lax.all_to_all(values, axis, 0, 0, tiled=True)


def spread(values, axis):
    count = lax.axis_size(axis)
    copies = jnp.broadcast_to(values[None], (count,) + values.shape)
    return exchange(copies.reshape((count * values.shape[0],) + values.shape[1:]), axis)


def sum_scatter(values, axis):
    count = lax.axis_size(axis)
    parts = exchange(values, axis)
    parts = parts.reshape((count, values.shape[0] // count) + values.shape[1:])
    return jnp.sum(parts.astype(F32), axis=0)


def two_parts(values):
    high = lax.reduce_precision(values, 8, 7)
    return jnp.stack([high, values - high], axis=1).astype(BF16)


def widen(values, width, *extra):
    rows = values.shape[0]
    left = width - values.shape[1] - sum(part.shape[1] for part in extra)
    return jnp.concatenate([values, *extra, jnp.zeros((rows, left), BF16)], axis=1)


def shards(
    token_ids,
    page_ids,
    tap_layer,
    teacher_in,
    teacher_gain,
    teacher_gate,
    teacher_up,
    teacher_down,
    student_embed,
    student_gain,
    student_gate,
    student_up,
    student_down,
    projection,
):
    far = lax.axis_index("zh")
    near = lax.axis_index(NEAR)
    tokens = teacher_in.shape[0]
    half = tokens // 2
    models = lax.axis_size(MODEL)
    blocks = lax.axis_size(NEAR)
    block = half // blocks
    width = student_gain.shape[0]
    columns = student_gate.shape[1]

    def by_half(values):
        return jnp.swapaxes(values.reshape((models, 2, half // models) + values.shape[1:]), 0, 1)

    def of_half(values, which):
        rest = values.shape[1:]
        picked = lax.dynamic_index_in_dim(by_half(values), which, 0, keepdims=False)
        return picked.reshape((half,) + rest)

    def of_block(values):
        return lax.dynamic_slice_in_dim(of_half(values, far), near * block, block, 0)

    down_own = jnp.pad(student_down, ((0, 0), (0, LANES - width)))
    proj_own = jnp.pad(projection, ((0, LANES - width), (0, 0)))
    down_both = jnp.concatenate([down_own, swap(down_own, "zh")], axis=1)
    proj_both = jnp.concatenate([proj_own, swap(proj_own, "zh")], axis=0)

    pages = tap_layer.shape[0]
    member = page_ids[:, None] == jnp.arange(pages, dtype=jnp.int32)[None, :]
    counts = jnp.sum(member.astype(F32), axis=0)
    page_weight = 1.0 / (pages * counts)
    token_weight = jnp.sum(jnp.where(member, page_weight[None, :], 0.0), axis=1)
    token_tap = jnp.sum(jnp.where(member, tap_layer[None, :], 0), axis=1) == 1
    weight_half = of_half(token_weight, far)
    weight = lax.dynamic_slice_in_dim(weight_half, near * block, block, 0)[:, None]
    tap_half = of_half(jnp.where(token_tap, 1.0, 0.0), far)[:, None]
    base = of_block(teacher_in).astype(F32)

    vocab_rows = student_embed.shape[0]
    local_ids = token_ids - lax.axis_index(MODEL) * vocab_rows
    chosen = local_ids[:, None] == jnp.arange(vocab_rows, dtype=jnp.int32)[None, :]
    picked = product(chosen.astype(BF16), student_embed).astype(BF16)
    teacher_float = teacher_in.astype(F32)
    teacher_square = jnp.sum(teacher_float * teacher_float, axis=1)
    first = sum_scatter(widen(picked, LANES, two_parts(teacher_square)), MODEL)
    student_in = first[:, :width]
    teacher_total = first[:, width] + first[:, width + 1]
    student_square = jnp.sum(student_in * student_in, axis=1)
    scaled = (student_in * student_gain.astype(F32)).astype(BF16)
    student_all = spread(widen(scaled, LANES, two_parts(student_square)), MODEL)
    student_all = by_half(student_all).reshape(tokens, LANES)
    rows_here = jnp.pad(student_in, ((0, 0), (0, LANES - width))).astype(BF16)
    rows_here = rows_here.reshape(2, half // models, LANES)
    residual = jnp.concatenate(
        [
            lax.dynamic_index_in_dim(rows_here, far, 0, keepdims=False),
            swap(lax.dynamic_index_in_dim(rows_here, 1 - far, 0, keepdims=False), "zh"),
        ],
        axis=1,
    ).astype(F32)

    student_both = jnp.concatenate([student_gate, student_up], axis=1)
    depth = LANES - width
    carry = (jnp.arange(depth)[:, None] < 2) & (jnp.arange(128)[None, :] == jnp.arange(depth)[:, None])
    student_both = jnp.concatenate(
        [
            jnp.concatenate([student_both, jnp.zeros((width, 128), BF16)], axis=1),
            jnp.concatenate([jnp.zeros((depth, 2 * columns), BF16), carry.astype(BF16)], axis=1),
        ],
        axis=0,
    )
    sums = sum_scatter(product(student_all, student_both).astype(BF16), GROUP)
    student_square_sum = sums[:, 2 * columns : 2 * columns + 1] + sums[:, 2 * columns + 1 : 2 * columns + 2]
    student_scale = lax.rsqrt(student_square_sum / DS + EPS)
    up_sum = sums[:, columns : 2 * columns] * student_scale
    active, slope = silu_parts(sums[:, :columns] * student_scale)
    hidden = spread((active * up_sum).astype(BF16), NEAR)

    hidden_width = teacher_gate.shape[1]
    teacher_scaled = (teacher_float * teacher_gain.astype(F32)).astype(BF16)
    teacher_both = jnp.concatenate([teacher_gate, teacher_up], axis=1)
    teacher_partial = product(teacher_scaled, teacher_both).astype(BF16)
    teacher_sums = sum_scatter(sum_scatter(teacher_partial, "x").astype(BF16), "zl")
    teacher_scale = lax.rsqrt(teacher_total / DT + EPS)[:, None]
    teacher_active, _ = silu_parts(teacher_sums[:, :hidden_width] * teacher_scale)
    teacher_share = (teacher_active * (teacher_sums[:, hidden_width:] * teacher_scale)).astype(BF16)
    teacher_hidden = spread(spread(teacher_share, "zl"), "x")
    added = product(of_half(teacher_hidden, far), teacher_down)
    added = added + swap(
        product(of_half(teacher_hidden, 1 - far), teacher_down).astype(BF16), "zh"
    ).astype(F32)

    out_sum = sum_scatter(product(hidden, down_both).astype(BF16), MODEL)
    student_out = spread((residual + out_sum).astype(BF16), MODEL)

    gap = product(student_out, proj_both) - tap_half * added
    difference = sum_scatter(gap.astype(BF16), NEAR) - base
    pred_grad = (tokens / 16 * weight * difference).astype(BF16)
    pred = spread(pred_grad, NEAR)
    grad_proj = transpose_product(student_out[:, :width], pred) + swap(
        transpose_product(student_out[:, LANES : LANES + width], pred).astype(BF16), "zh"
    ).astype(F32)

    pred_float = pred.astype(F32)
    token_loss = jnp.sum(pred_float * pred_float, axis=1) / ((tokens / 16) ** 2 * DT * weight_half)
    out_partial = product_transposed(pred, proj_both).astype(BF16)
    spare = jnp.concatenate([out_partial[:, : 2 * LANES - 2], two_parts(token_loss)], axis=1)
    second = sum_scatter(spare, MODEL)
    loss_rows = two_parts(second[:, -2] + second[:, -1])
    out_grad = spread(jnp.concatenate([second[:, :-2].astype(BF16), loss_rows], axis=1), MODEL)
    half_loss = two_parts(jnp.sum(out_grad[:, -2:].astype(F32))[None])
    down_far = transpose_product(hidden, out_grad[:, LANES : LANES + width]).astype(BF16)
    down_far = widen(down_far, LANES, jnp.broadcast_to(half_loss, (down_far.shape[0], 2)))
    down_swapped = swap(down_far, "zh").astype(F32)
    grad_down = transpose_product(hidden, out_grad[:, :width]) + down_swapped[:, :width]
    own_loss = half_loss[0, 0].astype(F32) + half_loss[0, 1].astype(F32)
    loss = own_loss + (down_swapped[0, width] + down_swapped[0, width + 1])

    hidden_grad = sum_scatter(product_transposed(out_grad, down_both).astype(BF16), NEAR)
    gate_grad = hidden_grad * up_sum * slope * student_scale
    up_grad = hidden_grad * active * student_scale
    both_near = jnp.concatenate([gate_grad, up_grad], axis=1).astype(BF16)
    both_far = swap(both_near, "zh")
    student_rows = student_all.reshape(2, blocks // 2, 2, block, LANES)[..., :width]

    def grads(both, which):
        own = spread(both, "y")
        every = jnp.concatenate([own, swap(own, "c")], axis=0)
        rows = lax.dynamic_index_in_dim(student_rows, which, 0, keepdims=False)
        core = lax.axis_index("c")
        rows = jnp.concatenate(
            [lax.dynamic_index_in_dim(rows, k, 1, keepdims=False) for k in (core, 1 - core)], axis=0
        ).reshape(half, width)
        return (
            transpose_product(rows, every[:, :columns]),
            transpose_product(rows, every[:, columns:]),
        )

    gate_first, up_first = grads(both_near, far)
    gate_second, up_second = grads(both_far, 1 - far)
    return (loss, gate_first + gate_second, up_first + up_second, grad_down, grad_proj)


def solution(mesh):
    fine = Mesh(mesh.devices.reshape(2, 4, 2, 4, 4), ("zh", "y", "c", "x", "zl"))
    placed = (
        P(),
        P(),
        P(),
        P(None, MODEL),
        P(MODEL),
        P(MODEL, GROUP),
        P(MODEL, GROUP),
        P(GROUP, MODEL),
        P(MODEL, GROUP),
        P(GROUP),
        P(GROUP, MODEL),
        P(GROUP, MODEL),
        P(MODEL, GROUP),
        P(GROUP, MODEL),
    )
    return jax.shard_map(
        shards,
        mesh=fine,
        in_specs=placed,
        out_specs=(P(), P(GROUP, MODEL), P(GROUP, MODEL), P(MODEL, GROUP), P(GROUP, MODEL)),
        check_vma=False,
    )
```

time: 311 us -> 358 us (1.15)
  waiting for transfers between devices: 120 us -> 140 us
  matrix products: 14.7 us -> 31.4 us
  blocking collectives: 35.1 us -> 21.5 us
  starting transfers between devices: 101 us -> 112 us
  other arithmetic: 10.9 us -> 21.3 us
    all_to_all x13 -> x16, starting transfers between devices: 54.7 us -> 88.8 us  [exchange(): return lax.all_to_all(values, axis, 0, 0, tiled=True)]
    ppermute x11 -> x9, waiting for transfers between devices: 11.5 us -> 34.1 us  [swap(): return lax.ppermute(values, axis, SWAP)]
    ppermute x11 -> x9, starting transfers between devices: 41.7 us -> 22.8 us  [swap(): return lax.ppermute(values, axis, SWAP)]
    all_to_all x3 -> x1, blocking collectives: 35.1 us -> 21.5 us  [exchange(): return lax.all_to_all(values, axis, 0, 0, tiled=True)]
    dot_general x9 -> x7, matrix products: 8.04 us -> 16.5 us  [product(): return jnp.dot(left, right, preferred_element_type=F32)]
    dot_general x4 -> x8, matrix products: 5.63 us -> 11.4 us  [transpose_product(): lax.dot_general(left, right, (((0,), (0,)), ((), ())), preferred_element_...]
    unnamed x47, local copies, waits for them, and re-layouts: 4.7 us -> 0.19 us
    ppermute x2 -> x0, starting transfers between devices: 4.2 us -> none  [the longest x1 2.69 us: shards(): lax.ppermute(loss_sum, 'y', [(k, k ^ 2) for k in range(4)])]
  transfers between devices with their start and end apart: 26 -> 25, of which waited for: 21 -> 16; matrix products, arithmetic and copies ran while one was open for 5% -> 17% of each run, Pallas kernels for 0% -> 0%
where the time goes in v2:
time: 358 us; the launch traced here: 355 us
  waiting for transfers between devices  140 us (39%)
  starting transfers between devices  112 us (31%)
  matrix products  31.4 us (9%)
  local copies, waits for them, and re-layouts  22.9 us (6%)
  blocking collectives  21.5 us (6%)
  other arithmetic  21.3 us (6%)
  between operations  6.7 us (2%)
    all_to_all x16, waiting for transfers between devices, exchange(): return lax.all_to_all(values, axis, 0, 0, tiled=True)  106 us
    all_to_all x16, starting transfers between devices, exchange(): return lax.all_to_all(values, axis, 0, 0, tiled=True)  88.8 us
    ppermute x9, waiting for transfers between devices, swap(): return lax.ppermute(values, axis, SWAP)  34.1 us
    ppermute x9, starting transfers between devices, swap(): return lax.ppermute(values, axis, SWAP)  22.8 us
    all_to_all x1, blocking collectives, exchange(): return lax.all_to_all(values, axis, 0, 0, tiled=True)  21.5 us
    dot_general x7, matrix products, product(): return jnp.dot(left, right, preferred_element_type=F32)  16.5 us
    dot_general x8, matrix products, transpose_product(): lax.dot_general(left, right, (((0,), (0,)), ((), ())), preferred_element_...  11.4 us
  transfers between devices with their start and end apart: 25, of which 16 were waited for; matrix products, arithmetic and copies ran while one was open for 17% of the time, Pallas kernels for 0%

profile of v2, /device:TPU:1, one launch (start us, length us, event | category | flops | bytes accessed | tf_op | source)
XLA Modules:
  0.0 355.0 jit_solution(4475544851918069190)
XLA Ops:
  6.1 9.0 %all-to-all-start = ((bf16[16,32,256]{2,1,0:T(8,128)(2,1)}), bf16[16,32,256]{2,1,0:T(8,128)(2,1)S(1)}, u32[]{:S(2)}, u32[]{:S(2)}) async-start(bf16[16,32,256]{2,1,0:T(8,128)(2,1)} %bitcast.1), calls=%async_computation | async-start | bytes 524288 | tf_op jit(solution)/shard_map/all_to_all | solution.py:42
  15.2 4.1 %convolution_convert_fusion = bf16[512,2048]{1,0:T(8,128)(2,1)} fusion(bf16[512,1024]{1,0:T(8,128)(2,1)} %param.20, bf16[512,1024]{1,0:T(8,128)(2,1)} %param.19, bf16[512,512]{1,0:T(8,128)(2,1)S(1)} %copy-done.6, f32[512]{0:T(512)S(1)} %convert_element_type.167), kind=kOutput, calls=%fused_computation.3 | convolution fusion | flops 1079771136 | bytes 4720640 | tf_op jit(solution)/shard_map/dot_general | solution.py:26
  19.3 5.5 %all-to-all-done = bf16[16,32,256]{2,1,0:T(8,128)(2,1)S(1)} async-done(((bf16[16,32,256]{2,1,0:T(8,128)(2,1)}), bf16[16,32,256]{2,1,0:T(8,128)(2,1)S(1)}, u32[]{:S(2)}, u32[]{:S(2)}) %all-to-all-start) | async-done | bytes 262176 | tf_op jit(solution)/shard_map/all_to_all | solution.py:42
  24.9 4.6 %all-to-all-start.6 = ((bf16[4,128,2048]{2,1,0:T(8,128)(2,1)}), bf16[4,128,2048]{2,1,0:T(8,128)(2,1)}, u32[]{:S(2)}, u32[]{:S(2)}) async-start(bf16[4,128,2048]{2,1,0:T(8,128)(2,1)} %bitcast.79), calls=%async_computation.6 | async-start | bytes 4194304 | tf_op jit(solution)/shard_map/all_to_all | solution.py:42
  29.9 23.8 %all-to-all-done.6 = bf16[4,128,2048]{2,1,0:T(8,128)(2,1)} async-done(((bf16[4,128,2048]{2,1,0:T(8,128)(2,1)}), bf16[4,128,2048]{2,1,0:T(8,128)(2,1)}, u32[]{:S(2)}, u32[]{:S(2)}) %all-to-all-start.6) | async-done | bytes 2097184 | tf_op jit(solution)/shard_map/all_to_all | solution.py:42
  54.4 3.7 %all-to-all-start.1 = ((bf16[16,32,256]{2,1,0:T(8,128)(2,1)}), bf16[16,32,256]{2,1,0:T(8,128)(2,1)S(1)}, u32[]{:S(2)}, u32[]{:S(2)}) async-start(bf16[16,32,256]{2,1,0:T(8,128)(2,1)} %broadcast_in_dim.68), calls=%async_computation.1 | async-start | bytes 524288 | tf_op jit(solution)/shard_map/all_to_all | solution.py:42
  58.1 2.9 reduce_sum.157
  61.0 5.2 %all-to-all-done.1 = bf16[16,32,256]{2,1,0:T(8,128)(2,1)S(1)} async-done(((bf16[16,32,256]{2,1,0:T(8,128)(2,1)}), bf16[16,32,256]{2,1,0:T(8,128)(2,1)S(1)}, u32[]{:S(2)}, u32[]{:S(2)}) %all-to-all-start.1) | async-done | bytes 262176 | tf_op jit(solution)/shard_map/all_to_all | solution.py:42
  66.2 3.5 all-to-all-start.7
  72.6 7.8 %all-to-all-done.7 = bf16[4,32,2048]{2,1,0:T(8,128)(2,1)S(1)} async-done(((bf16[4,32,2048]{2,1,0:T(8,128)(2,1)}), bf16[4,32,2048]{2,1,0:T(8,128)(2,1)S(1)}, u32[]{:S(2)}, u32[]{:S(2)}) %all-to-all-start.7) | async-done | bytes 524320 | tf_op jit(solution)/shard_map/all_to_all | solution.py:42
  80.5 13.0 %all-to-all-start.2 = ((bf16[16,32,1408]{2,1,0:T(8,128)(2,1)}), bf16[16,32,1408]{2,1,0:T(8,128)(2,1)}, u32[]{:S(2)}, u32[]{:S(2)}) async-start(bf16[16,32,1408]{2,1,0:T(8,128)(2,1)} %bitcast.82), calls=%async_computation.2 | async-start | bytes 2883584 | tf_op jit(solution)/shard_map/all_to_all | solution.py:42
  93.9 36.6 %all-to-all-done.2 = bf16[16,32,1408]{2,1,0:T(8,128)(2,1)} async-done(((bf16[16,32,1408]{2,1,0:T(8,128)(2,1)}), bf16[16,32,1408]{2,1,0:T(8,128)(2,1)}, u32[]{:S(2)}, u32[]{:S(2)}) %all-to-all-start.2) | async-done | bytes 1441824 | tf_op jit(solution)/shard_map/all_to_all | solution.py:42
  131.2 3.4 all-to-all-start.8
  136.5 5.5 %all-to-all-done.8 = bf16[4,32,1024]{2,1,0:T(8,128)(2,1)S(1)} async-done(((bf16[4,32,1024]{2,1,0:T(8,128)(2,1)}), bf16[4,32,1024]{2,1,0:T(8,128)(2,1)S(1)}, u32[]{:S(2)}, u32[]{:S(2)}) %all-to-all-start.8) | async-done | bytes 262176 | tf_op jit(solution)/shard_map/all_to_all | solution.py:42
  142.8 6.3 %all-to-all-start.3 = ((bf16[8,32,640]{2,1,0:T(8,128)(2,1)}), bf16[8,32,640]{2,1,0:T(8,128)(2,1)S(1)}, u32[]{:S(2)}, u32[]{:S(2)}) async-start(bf16[8,32,640]{2,1,0:T(8,128)(2,1)} %broadcast_in_dim.70), calls=%async_computation.3 | async-start | bytes 655360 | tf_op jit(solution)/shard_map/all_to_all | solution.py:42
  157.8 4.2 %all-to-all-start.9 = ((bf16[4,128,1024]{2,1,0:T(8,128)(2,1)}), bf16[4,128,1024]{2,1,0:T(8,128)(2,1)}, u32[]{:S(2)}, u32[]{:S(2)}) async-start(bf16[4,128,1024]{2,1,0:T(8,128)(2,1)} %broadcast_in_dim.136), calls=%async_computation.9 | async-start | bytes 2097152 | tf_op jit(solution)/shard_map/all_to_all | solution.py:42
  163.2 12.2 %collective-permute-done.1 = bf16[640,256]{0,1:T(8,128)(2,1)} collective-permute-done((bf16[640,256]{0,1:T(8,128)(2,1)S(1)}, bf16[640,256]{0,1:T(8,128)(2,1)}, u32[]{:S(2)}, u32[]{:S(2)}) %collective-permute-start.1) | collective-permute-done | bytes 327712 | tf_op jit(solution)/shard_map/ppermute | solution.py:38
  177.5 4.3 %all-to-all-start.4 = ((bf16[16,16,512]{2,1,0:T(8,128)(2,1)}), bf16[16,16,512]{2,1,0:T(8,128)(2,1)}, u32[]{:S(2)}, u32[]{:S(2)}) async-start(bf16[16,16,512]{2,1,0:T(8,128)(2,1)} %bitcast.100), calls=%async_computation.4 | async-start | bytes 524288 | tf_op jit(solution)/shard_map/all_to_all | solution.py:42
  200.9 6.9 %all-to-all-start.5 = ((bf16[16,16,512]{2,1,0:T(8,128)(2,1)}), bf16[16,16,512]{2,1,0:T(8,128)(2,1)}, u32[]{:S(2)}, u32[]{:S(2)}) async-start(bf16[16,16,512]{2,1,0:T(8,128)(2,1)} %broadcast_in_dim.71), calls=%async_computation.5 | async-start | bytes 524288 | tf_op jit(solution)/shard_map/all_to_all | solution.py:42
  209.4 2.8 collective-permute-start.3
  213.5 6.2 %collective-permute-done.3 = bf16[256,512]{1,0:T(8,128)(2,1)} collective-permute-done((bf16[256,512]{1,0:T(8,128)(2,1)S(1)}, bf16[256,512]{1,0:T(8,128)(2,1)}, u32[]{:S(2)}, u32[]{:S(2)}) %collective-permute-start.3) | collective-permute-done | bytes 262176 | tf_op jit(solution)/shard_map/ppermute | solution.py:38
  222.1 7.3 %all-to-all-start.10 = ((bf16[8,32,512]{2,1,0:T(8,128)(2,1)}), bf16[8,32,512]{2,1,0:T(8,128)(2,1)S(1)}, u32[]{:S(2)}, u32[]{:S(2)}) async-start(bf16[8,32,512]{2,1,0:T(8,128)(2,1)} %bitcast.19), calls=%async_computation.10 | async-start | bytes 524288 | tf_op jit(solution)/shard_map/all_to_all | solution.py:42
  230.0 5.9 %all-to-all-done.10 = bf16[8,32,512]{2,1,0:T(8,128)(2,1)S(1)} async-done(((bf16[8,32,512]{2,1,0:T(8,128)(2,1)}), bf16[8,32,512]{2,1,0:T(8,128)(2,1)S(1)}, u32[]{:S(2)}, u32[]{:S(2)}) %all-to-all-start.10) | async-done | bytes 262176 | tf_op jit(solution)/shard_map/all_to_all | solution.py:42
  237.4 4.4 %all-to-all-start.11 = ((bf16[8,32,512]{2,1,0:T(8,128)(2,1)}), bf16[8,32,512]{2,1,0:T(8,128)(2,1)S(1)}, u32[]{:S(2)}, u32[]{:S(2)}) async-start(bf16[8,32,512]{2,1,0:T(8,128)(2,1)} %broadcast_in_dim.137), calls=%async_computation.11 | async-start | bytes 524288 | tf_op jit(solution)/shard_map/all_to_all | solution.py:42
  242.5 5.7 %all-to-all-done.11 = bf16[8,32,512]{2,1,0:T(8,128)(2,1)S(1)} async-done(((bf16[8,32,512]{2,1,0:T(8,128)(2,1)}), bf16[8,32,512]{2,1,0:T(8,128)(2,1)S(1)}, u32[]{:S(2)}, u32[]{:S(2)}) %all-to-all-start.11) | async-done | bytes 262176 | tf_op jit(solution)/shard_map/all_to_all | solution.py:42
  250.3 21.5 %all_to_all.144 = bf16[16,16,512]{2,1,0:T(8,128)(2,1)S(1)} all-to-all(bf16[16,16,512]{2,1,0:T(8,128)(2,1)S(1)} %bitcast.96), channel_id=1, replica_groups=mesh['zh'=2,'y'=4,'c'=2,'x'=4,'zl'=4] {'x','zl'}, dimensions={0} | all-to-all | bytes 524288 | tf_op jit(solution)/shard_map/all_to_all | solution.py:42
  272.7 3.9 %all-to-all-start.13 = ((bf16[16,16,512]{2,1,0:T(8,128)(2,1)}), bf16[16,16,512]{2,1,0:T(8,128)(2,1)S(1)}, u32[]{:S(2)}, u32[]{:S(2)}) async-start(bf16[16,16,512]{2,1,0:T(8,128)(2,1)} %broadcast_in_dim.138), calls=%async_computation.13 | async-start | bytes 524288 | tf_op jit(solution)/shard_map/all_to_all | solution.py:42
  292.3 6.7 %all-to-all-start.14 = ((bf16[8,32,640]{2,1,0:T(8,128)(2,1)}), bf16[8,32,640]{2,1,0:T(8,128)(2,1)S(1)}, u32[]{:S(2)}, u32[]{:S(2)}) async-start(bf16[8,32,640]{2,1,0:T(8,128)(2,1)} %bitcast.99), calls=%async_computation.14 | async-start | bytes 655360 | tf_op jit(solution)/shard_map/all_to_all | solution.py:42
  310.0 14.9 %collective-permute-done.6 = bf16[32,1280]{1,0:T(8,128)(2,1)S(1)} collective-permute-done((bf16[32,1280]{1,0:T(8,128)(2,1)S(1)}, bf16[32,1280]{1,0:T(8,128)(2,1)S(1)}, u32[]{:S(2)}, u32[]{:S(2)}) %collective-permute-start.6) | collective-permute-done | bytes 81952 | tf_op jit(solution)/shard_map/ppermute | solution.py:38
  325.7 4.1 %all-to-all-start.16 = ((bf16[4,32,1280]{2,1,0:T(8,128)(2,1)}), bf16[4,32,1280]{2,1,0:T(8,128)(2,1)S(1)}, u32[]{:S(2)}, u32[]{:S(2)}) async-start(bf16[4,32,1280]{2,1,0:T(8,128)(2,1)} %broadcast_in_dim.143), calls=%async_computation.16 | async-start | bytes 655360 | tf_op jit(solution)/shard_map/all_to_all | solution.py:42
  331.8 4.0 %all-to-all-done.16 = bf16[4,32,1280]{2,1,0:T(8,128)(2,1)S(1)} async-done(((bf16[4,32,1280]{2,1,0:T(8,128)(2,1)}), bf16[4,32,1280]{2,1,0:T(8,128)(2,1)S(1)}, u32[]{:S(2)}, u32[]{:S(2)}) %all-to-all-start.16) | async-done | bytes 327712 | tf_op jit(solution)/shard_map/all_to_all | solution.py:42
  336.5 3.5 all-to-all-start.15
  (165 shorter events, 94.8 us)
Async XLA Ops:
  5.2 24.7 %copy-start.15 = (bf16[256]{0:T(256)(128)(2,1)}, bf16[256]{0:T(256)(128)(2,1)S(1)}, u32[]{:S(2)}) copy-start(bf16[256]{0:T(256)(128)(2,1)S(1)} %pad.57.clone) | copy-start | bytes 1540
  6.1 18.7 %all-to-all-start = ((bf16[16,32,256]{2,1,0:T(8,128)(2,1)}), bf16[16,32,256]{2,1,0:T(8,128)(2,1)S(1)}, u32[]{:S(2)}, u32[]{:S(2)}) async-start(bf16[16,32,256]{2,1,0:T(8,128)(2,1)} %bitcast.1), calls=%async_computation | async-start | bytes 524288 | tf_op jit(solution)/shard_map/all_to_all | solution.py:42
  24.9 28.9 %all-to-all-start.6 = ((bf16[4,128,2048]{2,1,0:T(8,128)(2,1)}), bf16[4,128,2048]{2,1,0:T(8,128)(2,1)}, u32[]{:S(2)}, u32[]{:S(2)}) async-start(bf16[4,128,2048]{2,1,0:T(8,128)(2,1)} %bitcast.79), calls=%async_computation.6 | async-start | bytes 4194304 | tf_op jit(solution)/shard_map/all_to_all | solution.py:42
  29.5 64.0 %copy-start.11 = (f32[32,256]{1,0:T(8,128)}, f32[32,256]{1,0:T(8,128)S(1)}, u32[]{:S(2)}) copy-start(f32[32,256]{1,0:T(8,128)S(1)} %convert_reduce_fusion.6) | copy-start | bytes 98308
  54.4 11.7 %all-to-all-start.1 = ((bf16[16,32,256]{2,1,0:T(8,128)(2,1)}), bf16[16,32,256]{2,1,0:T(8,128)(2,1)S(1)}, u32[]{:S(2)}, u32[]{:S(2)}) async-start(bf16[16,32,256]{2,1,0:T(8,128)(2,1)} %broadcast_in_dim.68), calls=%async_computation.1 | async-start | bytes 524288 | tf_op jit(solution)/shard_map/all_to_all | solution.py:42
  66.2 14.3 %all-to-all-start.7 = ((bf16[4,32,2048]{2,1,0:T(8,128)(2,1)}), bf16[4,32,2048]{2,1,0:T(8,128)(2,1)S(1)}, u32[]{:S(2)}, u32[]{:S(2)}) async-start(bf16[4,32,2048]{2,1,0:T(8,128)(2,1)} %bitcast.14), calls=%async_computation.7 | async-start | bytes 1048576 | tf_op jit(solution)/shard_map/all_to_all | solution.py:42
  80.5 50.0 %all-to-all-start.2 = ((bf16[16,32,1408]{2,1,0:T(8,128)(2,1)}), bf16[16,32,1408]{2,1,0:T(8,128)(2,1)}, u32[]{:S(2)}, u32[]{:S(2)}) async-start(bf16[16,32,1408]{2,1,0:T(8,128)(2,1)} %bitcast.82), calls=%async_computation.2 | async-start | bytes 2883584 | tf_op jit(solution)/shard_map/all_to_all | solution.py:42
  93.8 55.4 %copy-start.13 = (bf16[640,224]{0,1:T(8,128)(2,1)S(1)}, bf16[640,224]{0,1:T(8,128)(2,1)}, u32[]{:S(2)}) copy-start(bf16[640,224]{0,1:T(8,128)(2,1)} %param.26) | copy-start | bytes 860164
  131.2 10.9 %all-to-all-start.8 = ((bf16[4,32,1024]{2,1,0:T(8,128)(2,1)}), bf16[4,32,1024]{2,1,0:T(8,128)(2,1)S(1)}, u32[]{:S(2)}, u32[]{:S(2)}) async-start(bf16[4,32,1024]{2,1,0:T(8,128)(2,1)} %broadcast_in_dim.76), calls=%async_computation.8 | async-start | bytes 524288 | tf_op jit(solution)/shard_map/all_to_all | solution.py:42
  142.8 13.8 %all-to-all-start.3 = ((bf16[8,32,640]{2,1,0:T(8,128)(2,1)}), bf16[8,32,640]{2,1,0:T(8,128)(2,1)S(1)}, u32[]{:S(2)}, u32[]{:S(2)}) async-start(bf16[8,32,640]{2,1,0:T(8,128)(2,1)} %broadcast_in_dim.70), calls=%async_computation.3 | async-start | bytes 655360 | tf_op jit(solution)/shard_map/all_to_all | solution.py:42
  149.2 26.3 %copy-start.12 = (bf16[640,256]{0,1:T(8,128)(2,1)}, bf16[640,256]{0,1:T(8,128)(2,1)S(1)}, u32[]{:S(2)}) copy-start(bf16[640,256]{0,1:T(8,128)(2,1)S(1)} %pad.15) | copy-start | bytes 983044
  149.2 26.3 %collective-permute-start.1 = (bf16[640,256]{0,1:T(8,128)(2,1)S(1)}, bf16[640,256]{0,1:T(8,128)(2,1)}, u32[]{:S(2)}, u32[]{:S(2)}) collective-permute-start(bf16[640,256]{0,1:T(8,128)(2,1)S(1)} %pad.15), channel_id=1, source_target_pairs={{0,128},{128,0},{1,129},{129,1},{2,130},{130,2},{3,131},{131,3},{4... | collective-permute-start | bytes 983048 | tf_op jit(solution)/shard_map/ppermute | solution.py:38
  153.6 59.8 %collective-permute-start.2 = (bf16[256,512]{1,0:T(8,128)(2,1)}, bf16[256,512]{1,0:T(8,128)(2,1)}, u32[]{:S(2)}, u32[]{:S(2)}) collective-permute-start(bf16[256,512]{1,0:T(8,128)(2,1)} %pad.16), channel_id=1, source_target_pairs={{0,128},{128,0},{1,129},{129,1},{2,130},{130,2},{3,131},{131,3},{4... | collective-permute-start | bytes 786440 | tf_op jit(solution)/shard_map/ppermute | solution.py:38
  157.8 19.8 %all-to-all-start.9 = ((bf16[4,128,1024]{2,1,0:T(8,128)(2,1)}), bf16[4,128,1024]{2,1,0:T(8,128)(2,1)}, u32[]{:S(2)}, u32[]{:S(2)}) async-start(bf16[4,128,1024]{2,1,0:T(8,128)(2,1)} %broadcast_in_dim.136), calls=%async_computation.9 | async-start | bytes 2097152 | tf_op jit(solution)/shard_map/all_to_all | solution.py:42
  177.5 30.3 %copy-start.1 = (bf16[1024,512]{1,0:T(8,128)(2,1)S(1)}, bf16[1024,512]{1,0:T(8,128)(2,1)}, u32[]{:S(2)}) copy-start(bf16[1024,512]{1,0:T(8,128)(2,1)} %param.21) | copy-start | bytes 3145732
  177.5 20.2 %all-to-all-start.4 = ((bf16[16,16,512]{2,1,0:T(8,128)(2,1)}), bf16[16,16,512]{2,1,0:T(8,128)(2,1)}, u32[]{:S(2)}, u32[]{:S(2)}) async-start(bf16[16,16,512]{2,1,0:T(8,128)(2,1)} %bitcast.100), calls=%async_computation.4 | async-start | bytes 524288 | tf_op jit(solution)/shard_map/all_to_all | solution.py:42
  192.8 6.7 %collective-permute-start = (bf16[16,256]{1,0:T(8,128)(2,1)}, bf16[16,256]{1,0:T(8,128)(2,1)}, u32[]{:S(2)}, u32[]{:S(2)}) collective-permute-start(bf16[16,256]{1,0:T(8,128)(2,1)} %get-tuple-element.24), channel_id=1, source_target_pairs={{0,128},{128,0},{1,129},{129,1},{2,130},{130,2},{3,131},{131,3},{4... | collective-permute-start | bytes 24584 | tf_op jit(solution)/shard_map/ppermute | solution.py:38
  200.9 18.8 %all-to-all-start.5 = ((bf16[16,16,512]{2,1,0:T(8,128)(2,1)}), bf16[16,16,512]{2,1,0:T(8,128)(2,1)}, u32[]{:S(2)}, u32[]{:S(2)}) async-start(bf16[16,16,512]{2,1,0:T(8,128)(2,1)} %broadcast_in_dim.71), calls=%async_computation.5 | async-start | bytes 524288 | tf_op jit(solution)/shard_map/all_to_all | solution.py:42
  209.4 10.3 %collective-permute-start.3 = (bf16[256,512]{1,0:T(8,128)(2,1)S(1)}, bf16[256,512]{1,0:T(8,128)(2,1)}, u32[]{:S(2)}, u32[]{:S(2)}) collective-permute-start(bf16[256,512]{1,0:T(8,128)(2,1)S(1)} %convolution_convert_fusion.4), channel_id=1, source_target_pairs={{0,128},{128,0},{1,129},{129,1},{2,130},{130,2},{3,131},{131,3},{4... | collective-permute-start | bytes 786440 | tf_op jit(solution)/shard_map/ppermute | solution.py:38
  222.1 13.8 %all-to-all-start.10 = ((bf16[8,32,512]{2,1,0:T(8,128)(2,1)}), bf16[8,32,512]{2,1,0:T(8,128)(2,1)S(1)}, u32[]{:S(2)}, u32[]{:S(2)}) async-start(bf16[8,32,512]{2,1,0:T(8,128)(2,1)} %bitcast.19), calls=%async_computation.10 | async-start | bytes 524288 | tf_op jit(solution)/shard_map/all_to_all | solution.py:42
  237.4 10.9 %all-to-all-start.11 = ((bf16[8,32,512]{2,1,0:T(8,128)(2,1)}), bf16[8,32,512]{2,1,0:T(8,128)(2,1)S(1)}, u32[]{:S(2)}, u32[]{:S(2)}) async-start(bf16[8,32,512]{2,1,0:T(8,128)(2,1)} %broadcast_in_dim.137), calls=%async_computation.11 | async-start | bytes 524288 | tf_op jit(solution)/shard_map/all_to_all | solution.py:42
  242.5 34.1 %copy-start.10 = (bf16[2,16,16,256]{3,2,1,0:T(8,128)(2,1)S(1)}, bf16[2,16,16,256]{3,2,1,0:T(8,128)(2,1)}, u32[]{:S(2)}) copy-start(bf16[2,16,16,256]{3,2,1,0:T(8,128)(2,1)} %copy-done.9) | copy-start | bytes 786436
  272.7 12.5 %all-to-all-start.13 = ((bf16[16,16,512]{2,1,0:T(8,128)(2,1)}), bf16[16,16,512]{2,1,0:T(8,128)(2,1)S(1)}, u32[]{:S(2)}, u32[]{:S(2)}) async-start(bf16[16,16,512]{2,1,0:T(8,128)(2,1)} %broadcast_in_dim.138), calls=%async_computation.13 | async-start | bytes 524288 | tf_op jit(solution)/shard_map/all_to_all | solution.py:42
  277.4 21.7 %copy-start.16 = (bf16[256]{0:T(256)(128)(2,1)S(1)}, bf16[256]{0:T(256)(128)(2,1)}, u32[]{:S(2)}) copy-start(bf16[256]{0:T(256)(128)(2,1)} %copy-done.15) | copy-start | bytes 1540
  279.9 49.9 %collective-permute-start.8 = (bf16[224,512]{1,0:T(8,128)(2,1)}, bf16[224,512]{1,0:T(8,128)(2,1)}, u32[]{:S(2)}, u32[]{:S(2)}) collective-permute-start(bf16[224,512]{1,0:T(8,128)(2,1)} %convolution_convert_fusion.6), channel_id=1, source_target_pairs={{0,128},{128,0},{1,129},{129,1},{2,130},{130,2},{3,131},{131,3},{4... | collective-permute-start | bytes 688136 | tf_op jit(solution)/shard_map/ppermute | solution.py:38
  292.3 13.9 %all-to-all-start.14 = ((bf16[8,32,640]{2,1,0:T(8,128)(2,1)}), bf16[8,32,640]{2,1,0:T(8,128)(2,1)S(1)}, u32[]{:S(2)}, u32[]{:S(2)}) async-start(bf16[8,32,640]{2,1,0:T(8,128)(2,1)} %bitcast.99), calls=%async_computation.14 | async-start | bytes 655360 | tf_op jit(solution)/shard_map/all_to_all | solution.py:42
  300.9 41.5 %collective-permute-start.4 = (bf16[640,256]{0,1:T(8,128)(2,1)}, bf16[640,256]{0,1:T(8,128)(2,1)}, u32[]{:S(2)}, u32[]{:S(2)}) collective-permute-start(bf16[640,256]{0,1:T(8,128)(2,1)} %maximum_maximum_fusion), channel_id=1, source_target_pairs={{0,128},{128,0},{1,129},{129,1},{2,130},{130,2},{3,131},{131,3},{4... | collective-permute-start | bytes 983048 | tf_op jit(solution)/shard_map/ppermute | solution.py:38
  306.4 18.5 %collective-permute-start.6 = (bf16[32,1280]{1,0:T(8,128)(2,1)S(1)}, bf16[32,1280]{1,0:T(8,128)(2,1)S(1)}, u32[]{:S(2)}, u32[]{:S(2)}) collective-permute-start(bf16[32,1280]{1,0:T(8,128)(2,1)S(1)} %pad_maximum_fusion.13), channel_id=1, source_target_pairs={{0,128},{128,0},{1,129},{129,1},{2,130},{130,2},{3,131},{131,3},{4... | collective-permute-start | bytes 245768 | tf_op jit(solution)/shard_map/ppermute | solution.py:38
  325.7 10.1 %all-to-all-start.16 = ((bf16[4,32,1280]{2,1,0:T(8,128)(2,1)}), bf16[4,32,1280]{2,1,0:T(8,128)(2,1)S(1)}, u32[]{:S(2)}, u32[]{:S(2)}) async-start(bf16[4,32,1280]{2,1,0:T(8,128)(2,1)} %broadcast_in_dim.143), calls=%async_computation.16 | async-start | bytes 655360 | tf_op jit(solution)/shard_map/all_to_all | solution.py:42
  336.5 11.5 %all-to-all-start.15 = ((bf16[4,32,1280]{2,1,0:T(8,128)(2,1)}), bf16[4,32,1280]{2,1,0:T(8,128)(2,1)S(1)}, u32[]{:S(2)}, u32[]{:S(2)}) async-start(bf16[4,32,1280]{2,1,0:T(8,128)(2,1)} %broadcast_in_dim.142), calls=%async_computation.15 | async-start | bytes 655360 | tf_op jit(solution)/shard_map/all_to_all | solution.py:42
  340.0 9.3 %collective-permute-start.7 = (bf16[128,1280]{1,0:T(8,128)(2,1)S(1)}, bf16[128,1280]{1,0:T(8,128)(2,1)}, u32[]{:S(2)}, u32[]{:S(2)}) collective-permute-start(bf16[128,1280]{1,0:T(8,128)(2,1)S(1)} %bitcast.73), channel_id=1, source_target_pairs={{0,16},{16,0},{1,17},{17,1},{2,18},{18,2},{3,19},{19,3},{4,20},{20... | collective-permute-start | bytes 983048 | tf_op jit(solution)/shard_map/ppermute | solution.py:38
  348.0 3.7 %collective-permute-start.5 = (bf16[128,1280]{1,0:T(8,128)(2,1)S(1)}, bf16[128,1280]{1,0:T(8,128)(2,1)S(1)}, u32[]{:S(2)}, u32[]{:S(2)}) collective-permute-start(bf16[128,1280]{1,0:T(8,128)(2,1)S(1)} %bitcast.76), channel_id=1, source_target_pairs={{0,16},{16,0},{1,17},{17,1},{2,18},{18,2},{3,19},{19,3},{4,20},{20... | collective-permute-start | bytes 983048 | tf_op jit(solution)/shard_map/ppermute | solution.py:38
  (16 other events, 199.8 us)

commit v3 on v1

v3 whole, which is shorter than its diff:
```python
import jax
import jax.numpy as jnp
from jax import lax
from jax.sharding import Mesh, PartitionSpec as P

DT = 8192
DS = 3584

EPS = 1e-06

F32 = jnp.float32
BF16 = jnp.bfloat16
GROUP = ("zh", "y", "c")
MODEL = ("x", "zl")
SWAP = [(0, 1), (1, 0)]
LANES = 256
PAIRS = {step: [(at, at ^ step) for at in range(4)] for step in (1, 2, 3)}


def silu_parts(values):
    sigmoid = jax.nn.sigmoid(values)
    return (values * sigmoid, sigmoid * (1.0 + values * (1.0 - sigmoid)))


def product(left, right):
    return jnp.dot(left, right, preferred_element_type=F32)


def transpose_product(left, right):
    return lax.dot_general(left, right, (((0,), (0,)), ((), ())), preferred_element_type=F32)


def product_transposed(left, right):
    return lax.dot_general(left, right, (((1,), (1,)), ((), ())), preferred_element_type=F32)


def swap(values, axis):
    return lax.ppermute(values, axis, SWAP)


def exchange(values, axis):
    return lax.all_to_all(values, axis, 0, 0, tiled=True)


def copies(values, axis):
    count = lax.axis_size(axis)
    many = jnp.broadcast_to(values[None], (count,) + values.shape)
    return many.reshape((count * values.shape[0],) + values.shape[1:])


def spread(values, axis):
    return exchange(copies(values, axis), axis)


def sum_scatter(values, axis):
    count = lax.axis_size(axis)
    parts = exchange(values, axis)
    parts = parts.reshape((count, values.shape[0] // count) + values.shape[1:])
    return jnp.sum(parts.astype(F32), axis=0)


def group_sum(mine, other):
    received = swap(other.astype(BF16), "c")
    pair = (mine + received.astype(F32)).astype(BF16)
    total = lax.reduce_precision(sum_scatter(pair, "y"), 8, 7)
    return total + swap(total.astype(BF16), "zh").astype(F32)


def group_rows(values):
    mine = spread(values, "y")
    return mine, swap(mine, "c")


def after(values, earlier):
    return lax.optimization_barrier((values, earlier))[0]


def with_parts(values, column, place):
    high = lax.reduce_precision(column, 8, 7)
    at = lax.broadcasted_iota(jnp.int32, values.shape, 1)
    spare = jnp.where(at == place, high, column - high)
    return jnp.where((at == place) | (at == place + 1), spare, values).astype(BF16)


def column_sum(values, place):
    return values[:, place : place + 1] + values[:, place + 1 : place + 2]


def shards(
    token_ids,
    page_ids,
    tap_layer,
    teacher_in,
    teacher_gain,
    teacher_gate,
    teacher_up,
    teacher_down,
    student_embed,
    student_gain,
    student_gate,
    student_up,
    student_down,
    projection,
):
    core = lax.axis_index("c")
    tokens, teacher_width = teacher_in.shape
    half = tokens // 2
    block = half // lax.axis_size("y")
    student_width = student_gain.shape[0]

    def halves_first(values):
        turned = jnp.concatenate([values[half:], values[:half]], axis=0)
        return jnp.where(core == 0, values, turned)

    def rows_at(values, start, count):
        return lax.dynamic_slice_in_dim(values, start, count, 0)

    row_start = lax.axis_index("y") * block

    pages = tap_layer.shape[0]
    member = page_ids[:, None] == jnp.arange(pages, dtype=jnp.int32)[None, :]
    counts = jnp.sum(member.astype(F32), axis=0)
    page_weight = 1.0 / (pages * counts)
    token_weight = jnp.sum(jnp.where(member, page_weight[None, :], 0.0), axis=1, keepdims=True)
    token_tap = jnp.sum(jnp.where(member, tap_layer[None, :], 0), axis=1, keepdims=True)
    weight = rows_at(token_weight, core * half + row_start, block)

    vocab_rows = student_embed.shape[0]
    local_ids = token_ids - lax.axis_index(MODEL) * vocab_rows
    chosen = local_ids[:, None] == jnp.arange(vocab_rows, dtype=jnp.int32)[None, :]
    picked = product(chosen.astype(BF16), student_embed).astype(BF16)
    teacher_square = jnp.sum(jnp.square(teacher_in.astype(F32)), axis=1, keepdims=True)
    spare = LANES - student_width
    picked = jnp.pad(picked, ((0, 0), (0, spare)))
    payload = halves_first(with_parts(picked.astype(F32), teacher_square, student_width))
    first = sum_scatter(payload, MODEL)

    teacher_scaled = after(teacher_in, payload).astype(F32) * teacher_gain.astype(F32)
    teacher_scaled = halves_first(teacher_scaled.astype(BF16))
    teacher_both = jnp.concatenate([teacher_gate, teacher_up], axis=1)
    teacher_partial = product(teacher_scaled, teacher_both).astype(BF16)
    gain = jnp.pad(student_gain, (0, spare)).astype(F32)
    down_wide = jnp.pad(after(student_down, payload), ((0, 0), (0, spare)))
    proj_wide = jnp.pad(after(projection, payload), ((0, spare), (0, 0)))
    first = after(first, (teacher_partial, down_wide, proj_wide))
    quarter = tokens // 4
    part_rows = quarter // 4
    x_at = lax.axis_index("x")
    z_at = lax.axis_index("zl")

    def x_block(which):
        return rows_at(teacher_partial, which * quarter, quarter)

    teacher_total = column_sum(first, student_width)
    student_in = jnp.where(jnp.arange(LANES) < student_width, first, 0.0)
    student_square = jnp.sum(student_in * student_in, axis=1, keepdims=True)
    share_rows = with_parts(student_in * gain, student_square, student_width)
    teacher_partial = after(teacher_partial, share_rows)
    sent = {step: lax.ppermute(x_block(x_at ^ step), "x", PAIRS[step]) for step in (2, 1, 3)}
    student_all = spread(share_rows, MODEL)
    student_scaled = student_all[:, :student_width]

    columns = student_gate.shape[1]
    student_both = jnp.concatenate([student_gate, student_up], axis=1)
    depth = spare
    carry = (jnp.arange(depth)[:, None] < 2) & (jnp.arange(128)[None, :] == jnp.arange(depth)[:, None])
    student_both = jnp.concatenate(
        [
            jnp.concatenate([student_both, jnp.zeros((student_width, 128), BF16)], axis=1),
            jnp.concatenate([jnp.zeros((depth, 2 * columns), BF16), carry.astype(BF16)], axis=1),
        ],
        axis=0,
    )
    sums_other = swap(product(student_all[half:], student_both).astype(BF16), "c")
    pair = (product(student_all[:half], student_both) + sums_other.astype(F32)).astype(BF16)
    x_sums = x_block(x_at).astype(F32) + after(sent[2], pair).astype(F32)
    pair = after(pair, x_sums)
    y_sums = sum_scatter(pair, "y")
    x_sums = x_sums + after(sent[1], y_sums).astype(F32)
    y_sums = after(y_sums, x_sums)
    sums = y_sums + swap(y_sums.astype(BF16), "zh").astype(F32)
    student_scale = lax.rsqrt(column_sum(sums, 2 * columns) / DS + EPS)
    up_sum = sums[:, columns : 2 * columns] * student_scale
    active, slope = silu_parts(sums[:, :columns] * student_scale)
    hidden_share = (active * up_sum).astype(BF16)
    hidden_copies = copies(hidden_share, "y")
    hidden_mine = exchange(hidden_copies, "y")
    hidden_other = swap(hidden_mine, "c")

    hidden_width = teacher_gate.shape[1]
    x_sums = x_sums + after(sent[3], hidden_copies).astype(F32)
    arrived = [
        lax.ppermute(
            rows_at(x_sums, (z_at ^ step) * part_rows, part_rows).astype(BF16), "zl", PAIRS[step]
        )
        for step in (3, 2, 1)
    ]
    down = jnp.concatenate(
        [product(hidden_mine, down_wide), product(hidden_other, down_wide)], axis=0
    ).astype(BF16)
    teacher_sums = rows_at(x_sums, z_at * part_rows, part_rows)
    for part in after(arrived, down):
        teacher_sums = teacher_sums + part.astype(F32)
    teacher_scale = lax.rsqrt(teacher_total / DT + EPS)
    teacher_active, _ = silu_parts(teacher_sums[:, :hidden_width] * teacher_scale)
    teacher_share = (teacher_active * (teacher_sums[:, hidden_width:] * teacher_scale)).astype(BF16)
    arrived = [lax.ppermute(teacher_share, "zl", PAIRS[step]) for step in (1, 2, 3)]

    out_rows = (student_in + sum_scatter(down, MODEL)).astype(BF16)
    out_copies = copies(out_rows, MODEL)
    z_all = jnp.concatenate([teacher_share] + after(arrived, out_copies), axis=0)
    arrived = [lax.ppermute(z_all, "x", PAIRS[step]) for step in (1, 2, 3)]
    student_out = exchange(out_copies, MODEL)
    teacher_held = jnp.concatenate([z_all] + after(arrived, student_out), axis=0)

    held = jnp.arange(tokens, dtype=jnp.int32)
    held_model = ((held // quarter) ^ x_at) * 4 + ((held // part_rows % 4) ^ z_at)
    held_token = held_model * part_rows + held % part_rows
    order = (held[:, None] == held_token[None, :]) & (halves_first(token_tap) == 1)
    teacher_hidden = product(order.astype(BF16), teacher_held).astype(BF16)

    def gap(rows):
        added = product(teacher_hidden[rows], teacher_down)
        return product(student_out[rows], proj_wide) - added

    gap_sum = group_sum(gap(slice(0, half)), gap(slice(half, tokens)))
    base = rows_at(teacher_in, core * half + row_start, block)
    difference = gap_sum - base.astype(F32)
    pred_grad = (tokens / 16 * weight * difference).astype(BF16)
    pred_mine, pred_other = group_rows(pred_grad)
    pred_all = jnp.concatenate([pred_mine, pred_other], axis=0)
    grad_proj = transpose_product(student_out[:, :student_width], pred_all)

    pred_float = pred_all.astype(F32)
    token_loss = jnp.sum(pred_float * pred_float, axis=1, keepdims=True)
    token_loss = token_loss / ((tokens / 16) ** 2 * DT * halves_first(token_weight))
    out_partial = with_parts(product_transposed(pred_all, proj_wide), token_loss, student_width)
    second = sum_scatter(out_partial, MODEL)
    out_all = spread(with_parts(second, column_sum(second, student_width), student_width), MODEL)
    out_grad = out_all[:, :student_width]
    loss_terms = column_sum(out_all.astype(F32), student_width)
    loss_halves = jnp.sum(loss_terms.reshape(2, half), axis=1)
    loss = loss_halves[0] + loss_halves[1]
    hidden_all = jnp.concatenate([hidden_mine, hidden_other], axis=0)
    grad_down = transpose_product(hidden_all, out_grad)

    hidden_grad = group_sum(
        product_transposed(out_all[:half], down_wide), product_transposed(out_all[half:], down_wide)
    )
    gate_grad = hidden_grad * up_sum * slope * student_scale
    up_grad = hidden_grad * active * student_scale
    both_mine, both_other = group_rows(jnp.concatenate([gate_grad, up_grad], axis=1).astype(BF16))
    mine_scaled, other_scaled = student_scaled[:half], student_scaled[half:]

    def weight_grad(part):
        return transpose_product(mine_scaled, both_mine[:, part]) + transpose_product(
            other_scaled, both_other[:, part]
        )

    grad_gate = weight_grad(slice(0, columns))
    grad_up = weight_grad(slice(columns, 2 * columns))
    return (loss, grad_gate, grad_up, grad_down, grad_proj)


def solution(mesh):
    fine = Mesh(mesh.devices.reshape(2, 4, 2, 4, 4), ("zh", "y", "c", "x", "zl"))
    placed = (
        P(),
        P(),
        P(),
        P(None, MODEL),
        P(MODEL),
        P(MODEL, GROUP),
        P(MODEL, GROUP),
        P(GROUP, MODEL),
        P(MODEL, GROUP),
        P(GROUP),
        P(GROUP, MODEL),
        P(GROUP, MODEL),
        P(MODEL, GROUP),
        P(GROUP, MODEL),
    )
    return jax.shard_map(
        shards,
        mesh=fine,
        in_specs=placed,
        out_specs=(P(), P(GROUP, MODEL), P(GROUP, MODEL), P(MODEL, GROUP), P(GROUP, MODEL)),
        check_vma=False,
    )
```

time: 311 us -> 276 us (0.89)
  waiting for transfers between devices: 120 us -> 78.6 us
  starting transfers between devices: 101 us -> 87.6 us
  blocking collectives: 35.1 us -> 45.5 us
  matrix products: 14.7 us -> 24.1 us
  other arithmetic: 10.9 us -> 15.5 us
  between operations: 6.86 us -> 3.73 us
    all_to_all x13 -> x8, waiting for transfers between devices: 106 us -> 25.9 us  [exchange(): return lax.all_to_all(values, axis, 0, 0, tiled=True)]
    ppermute x2 -> x12, waiting for transfers between devices: 2.73 us -> 37 us  [the longest x3 25.3 us: shards(): lax.ppermute(x_block(x_at ^ step), 'x', PAIRS[step])]
    all_to_all x13 -> x8, starting transfers between devices: 54.7 us -> 37.9 us  [exchange(): return lax.all_to_all(values, axis, 0, 0, tiled=True)]
    all_to_all x3 -> x4, blocking collectives: 35.1 us -> 45.5 us  [exchange(): return lax.all_to_all(values, axis, 0, 0, tiled=True)]
    ppermute x2 -> x12, starting transfers between devices: 4.2 us -> 14.4 us  [the longest x3 6.06 us: shards(): lax.ppermute(rows_at(x_sums, (z_at ^ step) * part_rows, part_rows).astype...]
    dot_general x9 -> x11, matrix products: 8.04 us -> 15.4 us  [product(): return jnp.dot(left, right, preferred_element_type=F32)]
    ppermute x11 -> x9, starting transfers between devices: 41.7 us -> 35.3 us  [swap(): return lax.ppermute(values, axis, SWAP)]
    add x5 -> x6, other arithmetic: 0.97 us -> 5.26 us  [the longest x1 2.37 us: shards(): x_sums = x_sums + after(sent[3], hidden_copies).astype(F32)]
  transfers between devices with their start and end apart: 26 -> 29, of which waited for: 21 -> 15; matrix products, arithmetic and copies ran while one was open for 5% -> 9% of each run, Pallas kernels for 0% -> 0%
where the time goes in v3:
time: 276 us; the launch traced here: 274 us
  starting transfers between devices  87.6 us (32%)
  waiting for transfers between devices  78.6 us (28%)
  blocking collectives  45.5 us (16%)
  matrix products  24.1 us (9%)
  local copies, waits for them, and re-layouts  19.3 us (7%)
  other arithmetic  15.5 us (6%)
  between operations  3.73 us (1%)
    all_to_all x4, blocking collectives, exchange(): return lax.all_to_all(values, axis, 0, 0, tiled=True)  45.5 us
    all_to_all x8, starting transfers between devices, exchange(): return lax.all_to_all(values, axis, 0, 0, tiled=True)  37.9 us
    ppermute x9, starting transfers between devices, swap(): return lax.ppermute(values, axis, SWAP)  35.3 us
    all_to_all x8, waiting for transfers between devices, exchange(): return lax.all_to_all(values, axis, 0, 0, tiled=True)  25.9 us
    ppermute x3, waiting for transfers between devices, shards(): lax.ppermute(x_block(x_at ^ step), 'x', PAIRS[step])  25.3 us
    ppermute x9, waiting for transfers between devices, swap(): return lax.ppermute(values, axis, SWAP)  15.8 us
    dot_general x11, matrix products, product(): return jnp.dot(left, right, preferred_element_type=F32)  15.4 us
    unnamed x49, local copies, waits for them, and re-layouts  8.42 us
  transfers between devices with their start and end apart: 29, of which 15 were waited for; matrix products, arithmetic and copies ran while one was open for 9% of the time, Pallas kernels for 0%

profile of v3, /device:TPU:1, one launch (start us, length us, event | category | flops | bytes accessed | tf_op | source)
XLA Modules:
  0.0 274.4 jit_solution(13171479759369773215)
XLA Ops:
  6.3 9.2 %all-to-all-start = ((bf16[16,32,256]{2,1,0:T(8,128)(2,1)}), bf16[16,32,256]{2,1,0:T(8,128)(2,1)S(1)}, u32[]{:S(2)}, u32[]{:S(2)}) async-start(bf16[16,32,256]{2,1,0:T(8,128)(2,1)} %bitcast), calls=%async_computation | async-start | bytes 524288 | tf_op jit(solution)/shard_map/all_to_all | solution.py:42
  19.7 5.5 %all-to-all-done = bf16[16,32,256]{2,1,0:T(8,128)(2,1)S(1)} async-done(((bf16[16,32,256]{2,1,0:T(8,128)(2,1)}), bf16[16,32,256]{2,1,0:T(8,128)(2,1)S(1)}, u32[]{:S(2)}, u32[]{:S(2)}) %all-to-all-start) | async-done | bytes 262176 | tf_op jit(solution)/shard_map/all_to_all | solution.py:42
  26.2 4.0 %all-to-all-start.1 = ((bf16[16,32,256]{2,1,0:T(8,128)(2,1)}), bf16[16,32,256]{2,1,0:T(8,128)(2,1)S(1)}, u32[]{:S(2)}, u32[]{:S(2)}) async-start(bf16[16,32,256]{2,1,0:T(8,128)(2,1)} %broadcast_in_dim.154), calls=%async_computation.1 | async-start | bytes 524288 | tf_op jit(solution)/shard_map/all_to_all | solution.py:42
  30.3 8.5 %all-to-all-done.1 = bf16[16,32,256]{2,1,0:T(8,128)(2,1)S(1)} async-done(((bf16[16,32,256]{2,1,0:T(8,128)(2,1)}), bf16[16,32,256]{2,1,0:T(8,128)(2,1)S(1)}, u32[]{:S(2)}, u32[]{:S(2)}) %all-to-all-start.1) | async-done | bytes 262176 | tf_op jit(solution)/shard_map/all_to_all | solution.py:42
  41.1 3.2 %collective-permute-start = (bf16[256,1408]{1,0:T(8,128)(2,1)}, bf16[256,1408]{1,0:T(8,128)(2,1)}, u32[]{:S(2)}, u32[]{:S(2)}) collective-permute-start(bf16[256,1408]{1,0:T(8,128)(2,1)} %convolution_convert_fusion.1), channel_id=1, source_target_pairs={{0,16},{16,0},{1,17},{17,1},{2,18},{18,2},{3,19},{19,3},{4,20},{20... | collective-permute-start | bytes 2162696 | tf_op jit(solution)/shard_map/ppermute | solution.py:38
  49.9 12.0 %collective-permute-done.1 = bf16[128,2048]{1,0:T(8,128)(2,1)} collective-permute-done((bf16[128,2048]{1,0:T(8,128)(2,1)S(1)}, bf16[128,2048]{1,0:T(8,128)(2,1)}, u32[]{:S(2)}, u32[]{:S(2)}) %collective-permute-start.1) | collective-permute-done | bytes 524320 | tf_op jit(solution)/shard_map/ppermute | solution.py:159
  63.3 4.2 %all-to-all-start.2 = ((bf16[4,64,1408]{2,1,0:T(8,128)(2,1)}), bf16[4,64,1408]{2,1,0:T(8,128)(2,1)}, u32[]{:S(2)}, u32[]{:S(2)}) async-start(bf16[4,64,1408]{2,1,0:T(8,128)(2,1)} %bitcast.51), calls=%async_computation.2 | async-start | bytes 1441792 | tf_op jit(solution)/shard_map/all_to_all | solution.py:42
  68.2 13.3 %collective-permute-done.5 = bf16[128,2048]{1,0:T(8,128)(2,1)} collective-permute-done((bf16[128,2048]{1,0:T(8,128)(2,1)}, bf16[128,2048]{1,0:T(8,128)(2,1)}, u32[]{:S(2)}, u32[]{:S(2)}) %collective-permute-start.5) | collective-permute-done | bytes 524320 | tf_op jit(solution)/shard_map/ppermute | solution.py:159
  85.2 4.3 %collective-permute-start.3 = (bf16[64,1408]{1,0:T(8,128)(2,1)S(1)}, bf16[64,1408]{1,0:T(8,128)(2,1)S(1)}, u32[]{:S(2)}, u32[]{:S(2)}) collective-permute-start(bf16[64,1408]{1,0:T(8,128)(2,1)S(1)} %convert_element_type.200), channel_id=1, source_target_pairs={{0,128},{128,0},{1,129},{129,1},{2,130},{130,2},{3,131},{131,3},{4... | collective-permute-start | bytes 540680 | tf_op jit(solution)/shard_map/ppermute | solution.py:38
  89.5 5.7 %collective-permute-done.3 = bf16[64,1408]{1,0:T(8,128)(2,1)S(1)} collective-permute-done((bf16[64,1408]{1,0:T(8,128)(2,1)S(1)}, bf16[64,1408]{1,0:T(8,128)(2,1)S(1)}, u32[]{:S(2)}, u32[]{:S(2)}) %collective-permute-start.3) | collective-permute-done | bytes 180256 | tf_op jit(solution)/shard_map/ppermute | solution.py:38
  96.3 3.5 %all-to-all-start.3 = ((bf16[4,64,640]{2,1,0:T(8,128)(2,1)}), bf16[4,64,640]{2,1,0:T(8,128)(2,1)S(1)}, u32[]{:S(2)}, u32[]{:S(2)}) async-start(bf16[4,64,640]{2,1,0:T(8,128)(2,1)} %broadcast_in_dim.156), calls=%async_computation.3 | async-start | bytes 655360 | tf_op jit(solution)/shard_map/all_to_all | solution.py:42
  101.6 4.0 %collective-permute-start.8 = (bf16[32,2048]{1,0:T(8,128)(2,1)}, bf16[32,2048]{1,0:T(8,128)(2,1)}, u32[]{:S(2)}, u32[]{:S(2)}) collective-permute-start(bf16[32,2048]{1,0:T(8,128)(2,1)} %get-tuple-element.52), channel_id=1, source_target_pairs={{0,1},{1,0},{2,3},{3,2},{4,5},{5,4},{6,7},{7,6},{8,9},{9,8},{10,11... | collective-permute-start | bytes 393224 | tf_op jit(solution)/shard_map/ppermute | solution.py:193
  107.7 3.1 %collective-permute-start.4 = (bf16[256,640]{1,0:T(8,128)(2,1)S(1)}, bf16[256,640]{1,0:T(8,128)(2,1)S(1)}, u32[]{:S(2)}, u32[]{:S(2)}) collective-permute-start(bf16[256,640]{1,0:T(8,128)(2,1)S(1)} %bitcast.40), channel_id=1, source_target_pairs={{0,16},{16,0},{1,17},{17,1},{2,18},{18,2},{3,19},{19,3},{4,20},{20... | collective-permute-start | bytes 983048 | tf_op jit(solution)/shard_map/ppermute | solution.py:38
  111.0 5.8 %collective-permute-done.7 = bf16[32,2048]{1,0:T(8,128)(2,1)} collective-permute-done((bf16[32,2048]{1,0:T(8,128)(2,1)}, bf16[32,2048]{1,0:T(8,128)(2,1)}, u32[]{:S(2)}, u32[]{:S(2)}) %collective-permute-start.7) | collective-permute-done | bytes 131104 | tf_op jit(solution)/shard_map/ppermute | solution.py:193
  118.2 4.8 %all-to-all-start.4 = ((bf16[16,32,256]{2,1,0:T(8,128)(2,1)}), bf16[16,32,256]{2,1,0:T(8,128)(2,1)}, u32[]{:S(2)}, u32[]{:S(2)}) async-start(bf16[16,32,256]{2,1,0:T(8,128)(2,1)} %bitcast.49), calls=%async_computation.4 | async-start | bytes 524288 | tf_op jit(solution)/shard_map/all_to_all | solution.py:42
  124.9 3.1 %collective-permute-start.11 = (bf16[32,1024]{1,0:T(8,128)(2,1)}, bf16[32,1024]{1,0:T(8,128)(2,1)S(1)}, u32[]{:S(2)}, u32[]{:S(2)}) collective-permute-start(bf16[32,1024]{1,0:T(8,128)(2,1)} %get-tuple-element.46), channel_id=1, source_target_pairs={{0,3},{1,2},{2,1},{3,0},{4,7},{5,6},{6,5},{7,4},{8,11},{9,10},{10,... | collective-permute-start | bytes 196616 | tf_op jit(solution)/shard_map/ppermute | solution.py:207
  133.3 5.5 %all-to-all-start.5 = ((bf16[16,32,256]{2,1,0:T(8,128)(2,1)}), bf16[16,32,256]{2,1,0:T(8,128)(2,1)S(1)}, u32[]{:S(2)}, u32[]{:S(2)}) async-start(bf16[16,32,256]{2,1,0:T(8,128)(2,1)} %broadcast_in_dim.157), calls=%async_computation.5 | async-start | bytes 524288 | tf_op jit(solution)/shard_map/all_to_all | solution.py:42
  145.7 5.9 %collective-permute-done.14 = bf16[128,1024]{1,0:T(8,128)(2,1)S(1)} collective-permute-done((bf16[128,1024]{1,0:T(8,128)(2,1)S(1)}, bf16[128,1024]{1,0:T(8,128)(2,1)S(1)}, u32[]{:S(2)}, u32[]{:S(2)}) %collective-permute-start.14) | collective-permute-done | bytes 262176 | tf_op jit(solution)/shard_map/ppermute | solution.py:212
  160.0 6.2 %collective-permute-start.15 = (bf16[256,512]{1,0:T(8,128)(2,1)S(1)}, bf16[256,512]{1,0:T(8,128)(2,1)S(1)}, u32[]{:S(2)}, u32[]{:S(2)}) collective-permute-start(bf16[256,512]{1,0:T(8,128)(2,1)S(1)} %fusion.5), channel_id=1, source_target_pairs={{0,16},{16,0},{1,17},{17,1},{2,18},{18,2},{3,19},{19,3},{4,20},{20... | collective-permute-start | bytes 786440 | tf_op jit(solution)/shard_map/ppermute | solution.py:38
  168.5 3.4 %all-to-all-start.6 = ((bf16[4,64,512]{2,1,0:T(8,128)(2,1)}), bf16[4,64,512]{2,1,0:T(8,128)(2,1)S(1)}, u32[]{:S(2)}, u32[]{:S(2)}) async-start(bf16[4,64,512]{2,1,0:T(8,128)(2,1)} %bitcast.9), calls=%async_computation.6 | async-start | bytes 524288 | tf_op jit(solution)/shard_map/all_to_all | solution.py:42
  172.1 6.0 %all-to-all-done.6 = bf16[4,64,512]{2,1,0:T(8,128)(2,1)S(1)} async-done(((bf16[4,64,512]{2,1,0:T(8,128)(2,1)}), bf16[4,64,512]{2,1,0:T(8,128)(2,1)S(1)}, u32[]{:S(2)}, u32[]{:S(2)}) %all-to-all-start.6) | async-done | bytes 262176 | tf_op jit(solution)/shard_map/all_to_all | solution.py:42
  178.1 3.2 %collective-permute-start.16 = (bf16[64,512]{1,0:T(8,128)(2,1)S(1)}, bf16[64,512]{1,0:T(8,128)(2,1)S(1)}, u32[]{:S(2)}, u32[]{:S(2)}) collective-permute-start(bf16[64,512]{1,0:T(8,128)(2,1)S(1)} %reduce-precision_convert_fusion.1), channel_id=1, source_target_pairs={{0,128},{128,0},{1,129},{129,1},{2,130},{130,2},{3,131},{131,3},{4... | collective-permute-start | bytes 196616 | tf_op jit(solution)/shard_map/ppermute | solution.py:38
  181.4 3.9 %collective-permute-done.16 = bf16[64,512]{1,0:T(8,128)(2,1)S(1)} collective-permute-done((bf16[64,512]{1,0:T(8,128)(2,1)S(1)}, bf16[64,512]{1,0:T(8,128)(2,1)S(1)}, u32[]{:S(2)}, u32[]{:S(2)}) %collective-permute-start.16) | collective-permute-done | bytes 65568 | tf_op jit(solution)/shard_map/ppermute | solution.py:38
  186.3 7.9 %all_to_all.105 = bf16[4,64,512]{2,1,0:T(8,128)(2,1)S(1)} all-to-all(bf16[4,64,512]{2,1,0:T(8,128)(2,1)S(1)} %broadcast_in_dim.160), channel_id=1, replica_groups=mesh['zh'=2,'y'=4,'c'=2,'x'=4,'zl'=4] {'y'}, dimensions={0} | all-to-all | bytes 524288 | tf_op jit(solution)/shard_map/all_to_all | solution.py:42
  194.2 3.8 %collective-permute-start.17 = (bf16[256,512]{1,0:T(8,128)(2,1)S(1)}, bf16[256,512]{1,0:T(8,128)(2,1)S(1)}, u32[]{:S(2)}, u32[]{:S(2)}) collective-permute-start(bf16[256,512]{1,0:T(8,128)(2,1)S(1)} %bitcast.45), channel_id=1, source_target_pairs={{0,16},{16,0},{1,17},{17,1},{2,18},{18,2},{3,19},{19,3},{4,20},{20... | collective-permute-start | bytes 786440 | tf_op jit(solution)/shard_map/ppermute | solution.py:38
  202.0 15.2 %all_to_all.106 = bf16[16,32,256]{2,1,0:T(8,128)(2,1)S(1)} all-to-all(bf16[16,32,256]{2,1,0:T(8,128)(2,1)S(1)} %bitcast.50), channel_id=1, replica_groups=mesh['zh'=2,'y'=4,'c'=2,'x'=4,'zl'=4] {'x','zl'}, dimensions={0} | all-to-all | bytes 524288 | tf_op jit(solution)/shard_map/all_to_all | solution.py:42
  217.6 13.1 %all_to_all.107 = bf16[16,32,256]{2,1,0:T(8,128)(2,1)S(1)} all-to-all(bf16[16,32,256]{2,1,0:T(8,128)(2,1)S(1)} %broadcast_in_dim.167), channel_id=1, replica_groups=mesh['zh'=2,'y'=4,'c'=2,'x'=4,'zl'=4] {'x','zl'}, dimensions={0} | all-to-all | bytes 524288 | tf_op jit(solution)/shard_map/all_to_all | solution.py:42
  234.8 9.2 %all_to_all.108 = bf16[4,64,640]{2,1,0:T(8,128)(2,1)S(1)} all-to-all(bf16[4,64,640]{2,1,0:T(8,128)(2,1)S(1)} %bitcast.43), channel_id=1, replica_groups=mesh['zh'=2,'y'=4,'c'=2,'x'=4,'zl'=4] {'y'}, dimensions={0} | all-to-all | bytes 655360 | tf_op jit(solution)/shard_map/all_to_all | solution.py:42
  244.1 4.4 %collective-permute-start.19 = (bf16[64,640]{1,0:T(8,128)(2,1)S(1)}, bf16[64,640]{1,0:T(8,128)(2,1)S(1)}, u32[]{:S(2)}, u32[]{:S(2)}) collective-permute-start(bf16[64,640]{1,0:T(8,128)(2,1)S(1)} %reduce-precision_convert_fusion), channel_id=1, source_target_pairs={{0,128},{128,0},{1,129},{129,1},{2,130},{130,2},{3,131},{131,3},{4... | collective-permute-start | bytes 245768 | tf_op jit(solution)/shard_map/ppermute | solution.py:38
  252.6 3.5 %all-to-all-start.11 = ((bf16[4,64,1280]{2,1,0:T(8,128)(2,1)}), bf16[4,64,1280]{2,1,0:T(8,128)(2,1)S(1)}, u32[]{:S(2)}, u32[]{:S(2)}) async-start(bf16[4,64,1280]{2,1,0:T(8,128)(2,1)} %broadcast_in_dim.168), calls=%async_computation.11 | async-start | bytes 1310720 | tf_op jit(solution)/shard_map/all_to_all | solution.py:42
  260.6 3.0 %all-to-all-done.11 = bf16[4,64,1280]{2,1,0:T(8,128)(2,1)S(1)} async-done(((bf16[4,64,1280]{2,1,0:T(8,128)(2,1)}), bf16[4,64,1280]{2,1,0:T(8,128)(2,1)S(1)}, u32[]{:S(2)}, u32[]{:S(2)}) %all-to-all-start.11) | async-done | bytes 655392 | tf_op jit(solution)/shard_map/all_to_all | solution.py:42
  263.7 4.6 %collective-permute-start.20 = (bf16[256,1280]{1,0:T(8,128)(2,1)S(1)}, bf16[256,1280]{1,0:T(8,128)(2,1)S(1)}, u32[]{:S(2)}, u32[]{:S(2)}) collective-permute-start(bf16[256,1280]{1,0:T(8,128)(2,1)S(1)} %bitcast.35), channel_id=1, source_target_pairs={{0,16},{16,0},{1,17},{17,1},{2,18},{18,2},{3,19},{19,3},{4,20},{20... | collective-permute-start | bytes 1966088 | tf_op jit(solution)/shard_map/ppermute | solution.py:38
  (174 shorter events, 77.6 us)
Async XLA Ops:
  6.3 18.9 %all-to-all-start = ((bf16[16,32,256]{2,1,0:T(8,128)(2,1)}), bf16[16,32,256]{2,1,0:T(8,128)(2,1)S(1)}, u32[]{:S(2)}, u32[]{:S(2)}) async-start(bf16[16,32,256]{2,1,0:T(8,128)(2,1)} %bitcast), calls=%async_computation | async-start | bytes 524288 | tf_op jit(solution)/shard_map/all_to_all | solution.py:42
  19.7 19.2 %copy-start.20 = (bf16[224,640]{1,0:T(8,128)(2,1)S(1)}, bf16[224,640]{1,0:T(8,128)(2,1)}, u32[]{:S(2)}) copy-start(bf16[224,640]{1,0:T(8,128)(2,1)} %param.25) | copy-start | bytes 860164
  26.2 12.6 %all-to-all-start.1 = ((bf16[16,32,256]{2,1,0:T(8,128)(2,1)}), bf16[16,32,256]{2,1,0:T(8,128)(2,1)S(1)}, u32[]{:S(2)}, u32[]{:S(2)}) async-start(bf16[16,32,256]{2,1,0:T(8,128)(2,1)} %broadcast_in_dim.154), calls=%async_computation.1 | async-start | bytes 524288 | tf_op jit(solution)/shard_map/all_to_all | solution.py:42
  41.1 6.3 %collective-permute-start = (bf16[256,1408]{1,0:T(8,128)(2,1)}, bf16[256,1408]{1,0:T(8,128)(2,1)}, u32[]{:S(2)}, u32[]{:S(2)}) collective-permute-start(bf16[256,1408]{1,0:T(8,128)(2,1)} %convolution_convert_fusion.1), channel_id=1, source_target_pairs={{0,16},{16,0},{1,17},{17,1},{2,18},{18,2},{3,19},{19,3},{4,20},{20... | collective-permute-start | bytes 2162696 | tf_op jit(solution)/shard_map/ppermute | solution.py:38
  46.8 15.2 %collective-permute-start.1 = (bf16[128,2048]{1,0:T(8,128)(2,1)S(1)}, bf16[128,2048]{1,0:T(8,128)(2,1)}, u32[]{:S(2)}, u32[]{:S(2)}) collective-permute-start(bf16[128,2048]{1,0:T(8,128)(2,1)S(1)} %get-tuple-element.51), channel_id=1, source_target_pairs={{0,8},{4,12},{8,0},{12,4},{1,9},{5,13},{9,1},{13,5},{2,10},{6,14},... | collective-permute-start | bytes 1572872 | tf_op jit(solution)/shard_map/ppermute | solution.py:159
  63.3 18.2 %all-to-all-start.2 = ((bf16[4,64,1408]{2,1,0:T(8,128)(2,1)}), bf16[4,64,1408]{2,1,0:T(8,128)(2,1)}, u32[]{:S(2)}, u32[]{:S(2)}) async-start(bf16[4,64,1408]{2,1,0:T(8,128)(2,1)} %bitcast.51), calls=%async_computation.2 | async-start | bytes 1441792 | tf_op jit(solution)/shard_map/all_to_all | solution.py:42
  67.5 14.1 %collective-permute-start.5 = (bf16[128,2048]{1,0:T(8,128)(2,1)}, bf16[128,2048]{1,0:T(8,128)(2,1)}, u32[]{:S(2)}, u32[]{:S(2)}) collective-permute-start(bf16[128,2048]{1,0:T(8,128)(2,1)} %get-tuple-element.50), channel_id=1, source_target_pairs={{0,12},{4,8},{8,4},{12,0},{1,13},{5,9},{9,5},{13,1},{2,14},{6,10},... | collective-permute-start | bytes 1572872 | tf_op jit(solution)/shard_map/ppermute | solution.py:159
  68.1 14.6 %collective-permute-start.2 = (bf16[128,2048]{1,0:T(8,128)(2,1)}, bf16[128,2048]{1,0:T(8,128)(2,1)}, u32[]{:S(2)}, u32[]{:S(2)}) collective-permute-start(bf16[128,2048]{1,0:T(8,128)(2,1)} %get-tuple-element.49), channel_id=1, source_target_pairs={{0,4},{4,0},{8,12},{12,8},{1,5},{5,1},{9,13},{13,9},{2,6},{6,2},{1... | collective-permute-start | bytes 1572872 | tf_op jit(solution)/shard_map/ppermute | solution.py:159
  85.2 10.0 %collective-permute-start.3 = (bf16[64,1408]{1,0:T(8,128)(2,1)S(1)}, bf16[64,1408]{1,0:T(8,128)(2,1)S(1)}, u32[]{:S(2)}, u32[]{:S(2)}) collective-permute-start(bf16[64,1408]{1,0:T(8,128)(2,1)S(1)} %convert_element_type.200), channel_id=1, source_target_pairs={{0,128},{128,0},{1,129},{129,1},{2,130},{130,2},{3,131},{131,3},{4... | collective-permute-start | bytes 540680 | tf_op jit(solution)/shard_map/ppermute | solution.py:38
  89.5 27.4 %copy-start.1 = (bf16[640,224]{0,1:T(8,128)(2,1)S(1)}, bf16[640,224]{0,1:T(8,128)(2,1)}, u32[]{:S(2)}) copy-start(bf16[640,224]{0,1:T(8,128)(2,1)} %param.26) | copy-start | bytes 860164
  96.3 11.4 %all-to-all-start.3 = ((bf16[4,64,640]{2,1,0:T(8,128)(2,1)}), bf16[4,64,640]{2,1,0:T(8,128)(2,1)S(1)}, u32[]{:S(2)}, u32[]{:S(2)}) async-start(bf16[4,64,640]{2,1,0:T(8,128)(2,1)} %broadcast_in_dim.156), calls=%async_computation.3 | async-start | bytes 655360 | tf_op jit(solution)/shard_map/all_to_all | solution.py:42
  101.6 9.4 %collective-permute-start.8 = (bf16[32,2048]{1,0:T(8,128)(2,1)}, bf16[32,2048]{1,0:T(8,128)(2,1)}, u32[]{:S(2)}, u32[]{:S(2)}) collective-permute-start(bf16[32,2048]{1,0:T(8,128)(2,1)} %get-tuple-element.52), channel_id=1, source_target_pairs={{0,1},{1,0},{2,3},{3,2},{4,5},{5,4},{6,7},{7,6},{8,9},{9,8},{10,11... | collective-permute-start | bytes 393224 | tf_op jit(solution)/shard_map/ppermute | solution.py:193
  105.6 11.2 %collective-permute-start.7 = (bf16[32,2048]{1,0:T(8,128)(2,1)}, bf16[32,2048]{1,0:T(8,128)(2,1)}, u32[]{:S(2)}, u32[]{:S(2)}) collective-permute-start(bf16[32,2048]{1,0:T(8,128)(2,1)} %get-tuple-element.53), channel_id=1, source_target_pairs={{0,2},{1,3},{2,0},{3,1},{4,6},{5,7},{6,4},{7,5},{8,10},{9,11},{10,... | collective-permute-start | bytes 393224 | tf_op jit(solution)/shard_map/ppermute | solution.py:193
  105.6 11.2 %collective-permute-start.6 = (bf16[32,2048]{1,0:T(8,128)(2,1)}, bf16[32,2048]{1,0:T(8,128)(2,1)}, u32[]{:S(2)}, u32[]{:S(2)}) collective-permute-start(bf16[32,2048]{1,0:T(8,128)(2,1)} %get-tuple-element.54), channel_id=1, source_target_pairs={{0,3},{1,2},{2,1},{3,0},{4,7},{5,6},{6,5},{7,4},{8,11},{9,10},{10,... | collective-permute-start | bytes 393224 | tf_op jit(solution)/shard_map/ppermute | solution.py:193
  107.7 9.4 %collective-permute-start.4 = (bf16[256,640]{1,0:T(8,128)(2,1)S(1)}, bf16[256,640]{1,0:T(8,128)(2,1)S(1)}, u32[]{:S(2)}, u32[]{:S(2)}) collective-permute-start(bf16[256,640]{1,0:T(8,128)(2,1)S(1)} %bitcast.40), channel_id=1, source_target_pairs={{0,16},{16,0},{1,17},{17,1},{2,18},{18,2},{3,19},{19,3},{4,20},{20... | collective-permute-start | bytes 983048 | tf_op jit(solution)/shard_map/ppermute | solution.py:38
  118.2 13.4 %all-to-all-start.4 = ((bf16[16,32,256]{2,1,0:T(8,128)(2,1)}), bf16[16,32,256]{2,1,0:T(8,128)(2,1)}, u32[]{:S(2)}, u32[]{:S(2)}) async-start(bf16[16,32,256]{2,1,0:T(8,128)(2,1)} %bitcast.49), calls=%async_computation.4 | async-start | bytes 524288 | tf_op jit(solution)/shard_map/all_to_all | solution.py:42
  124.9 13.8 %collective-permute-start.11 = (bf16[32,1024]{1,0:T(8,128)(2,1)}, bf16[32,1024]{1,0:T(8,128)(2,1)S(1)}, u32[]{:S(2)}, u32[]{:S(2)}) collective-permute-start(bf16[32,1024]{1,0:T(8,128)(2,1)} %get-tuple-element.46), channel_id=1, source_target_pairs={{0,3},{1,2},{2,1},{3,0},{4,7},{5,6},{6,5},{7,4},{8,11},{9,10},{10,... | collective-permute-start | bytes 196616 | tf_op jit(solution)/shard_map/ppermute | solution.py:207
  128.0 10.7 %collective-permute-start.10 = (bf16[32,1024]{1,0:T(8,128)(2,1)}, bf16[32,1024]{1,0:T(8,128)(2,1)S(1)}, u32[]{:S(2)}, u32[]{:S(2)}) collective-permute-start(bf16[32,1024]{1,0:T(8,128)(2,1)} %get-tuple-element.46), channel_id=1, source_target_pairs={{0,2},{1,3},{2,0},{3,1},{4,6},{5,7},{6,4},{7,5},{8,10},{9,11},{10,... | collective-permute-start | bytes 196616 | tf_op jit(solution)/shard_map/ppermute | solution.py:207
  128.7 10.1 %collective-permute-start.9 = (bf16[32,1024]{1,0:T(8,128)(2,1)}, bf16[32,1024]{1,0:T(8,128)(2,1)}, u32[]{:S(2)}, u32[]{:S(2)}) collective-permute-start(bf16[32,1024]{1,0:T(8,128)(2,1)} %get-tuple-element.46), channel_id=1, source_target_pairs={{0,1},{1,0},{2,3},{3,2},{4,5},{5,4},{6,7},{7,6},{8,9},{9,8},{10,11... | collective-permute-start | bytes 196616 | tf_op jit(solution)/shard_map/ppermute | solution.py:207
  133.3 19.7 %all-to-all-start.5 = ((bf16[16,32,256]{2,1,0:T(8,128)(2,1)}), bf16[16,32,256]{2,1,0:T(8,128)(2,1)S(1)}, u32[]{:S(2)}, u32[]{:S(2)}) async-start(bf16[16,32,256]{2,1,0:T(8,128)(2,1)} %broadcast_in_dim.157), calls=%async_computation.5 | async-start | bytes 524288 | tf_op jit(solution)/shard_map/all_to_all | solution.py:42
  139.7 11.9 %collective-permute-start.14 = (bf16[128,1024]{1,0:T(8,128)(2,1)S(1)}, bf16[128,1024]{1,0:T(8,128)(2,1)S(1)}, u32[]{:S(2)}, u32[]{:S(2)}) collective-permute-start(bf16[128,1024]{1,0:T(8,128)(2,1)S(1)} %pad_maximum_fusion.3), channel_id=1, source_target_pairs={{0,12},{4,8},{8,4},{12,0},{1,13},{5,9},{9,5},{13,1},{2,14},{6,10},... | collective-permute-start | bytes 786440 | tf_op jit(solution)/shard_map/ppermute | solution.py:212
  142.3 9.3 %collective-permute-start.13 = (bf16[128,1024]{1,0:T(8,128)(2,1)S(1)}, bf16[128,1024]{1,0:T(8,128)(2,1)S(1)}, u32[]{:S(2)}, u32[]{:S(2)}) collective-permute-start(bf16[128,1024]{1,0:T(8,128)(2,1)S(1)} %pad_maximum_fusion.3), channel_id=1, source_target_pairs={{0,8},{4,12},{8,0},{12,4},{1,9},{5,13},{9,1},{13,5},{2,10},{6,14},... | collective-permute-start | bytes 786440 | tf_op jit(solution)/shard_map/ppermute | solution.py:212
  142.9 10.1 %collective-permute-start.12 = (bf16[128,1024]{1,0:T(8,128)(2,1)S(1)}, bf16[128,1024]{1,0:T(8,128)(2,1)}, u32[]{:S(2)}, u32[]{:S(2)}) collective-permute-start(bf16[128,1024]{1,0:T(8,128)(2,1)S(1)} %pad_maximum_fusion.3), channel_id=1, source_target_pairs={{0,4},{4,0},{8,12},{12,8},{1,5},{5,1},{9,13},{13,9},{2,6},{6,2},{1... | collective-permute-start | bytes 786440 | tf_op jit(solution)/shard_map/ppermute | solution.py:212
  160.0 7.4 %collective-permute-start.15 = (bf16[256,512]{1,0:T(8,128)(2,1)S(1)}, bf16[256,512]{1,0:T(8,128)(2,1)S(1)}, u32[]{:S(2)}, u32[]{:S(2)}) collective-permute-start(bf16[256,512]{1,0:T(8,128)(2,1)S(1)} %fusion.5), channel_id=1, source_target_pairs={{0,16},{16,0},{1,17},{17,1},{2,18},{18,2},{3,19},{19,3},{4,20},{20... | collective-permute-start | bytes 786440 | tf_op jit(solution)/shard_map/ppermute | solution.py:38
  168.5 9.5 %all-to-all-start.6 = ((bf16[4,64,512]{2,1,0:T(8,128)(2,1)}), bf16[4,64,512]{2,1,0:T(8,128)(2,1)S(1)}, u32[]{:S(2)}, u32[]{:S(2)}) async-start(bf16[4,64,512]{2,1,0:T(8,128)(2,1)} %bitcast.9), calls=%async_computation.6 | async-start | bytes 524288 | tf_op jit(solution)/shard_map/all_to_all | solution.py:42
  178.0 21.8 %copy-start.8 = (bf16[224,512]{1,0:T(8,128)(2,1)S(1)}, bf16[224,512]{1,0:T(8,128)(2,1)}, u32[]{:S(2)}) copy-start(bf16[224,512]{1,0:T(8,128)(2,1)} %param.27) | copy-start | bytes 688132
  178.1 7.2 %collective-permute-start.16 = (bf16[64,512]{1,0:T(8,128)(2,1)S(1)}, bf16[64,512]{1,0:T(8,128)(2,1)S(1)}, u32[]{:S(2)}, u32[]{:S(2)}) collective-permute-start(bf16[64,512]{1,0:T(8,128)(2,1)S(1)} %reduce-precision_convert_fusion.1), channel_id=1, source_target_pairs={{0,128},{128,0},{1,129},{129,1},{2,130},{130,2},{3,131},{131,3},{4... | collective-permute-start | bytes 196616 | tf_op jit(solution)/shard_map/ppermute | solution.py:38
  194.2 5.0 %collective-permute-start.17 = (bf16[256,512]{1,0:T(8,128)(2,1)S(1)}, bf16[256,512]{1,0:T(8,128)(2,1)S(1)}, u32[]{:S(2)}, u32[]{:S(2)}) collective-permute-start(bf16[256,512]{1,0:T(8,128)(2,1)S(1)} %bitcast.45), channel_id=1, source_target_pairs={{0,16},{16,0},{1,17},{17,1},{2,18},{18,2},{3,19},{19,3},{4,20},{20... | collective-permute-start | bytes 786440 | tf_op jit(solution)/shard_map/ppermute | solution.py:38
  231.0 3.6 %collective-permute-start.18 = (bf16[256,640]{1,0:T(8,128)(2,1)S(1)}, bf16[256,640]{1,0:T(8,128)(2,1)S(1)}, u32[]{:S(2)}, u32[]{:S(2)}) collective-permute-start(bf16[256,640]{1,0:T(8,128)(2,1)S(1)} %convolution_convert_fusion.3), channel_id=1, source_target_pairs={{0,16},{16,0},{1,17},{17,1},{2,18},{18,2},{3,19},{19,3},{4,20},{20... | collective-permute-start | bytes 983048 | tf_op jit(solution)/shard_map/ppermute | solution.py:38
  244.1 7.4 %collective-permute-start.19 = (bf16[64,640]{1,0:T(8,128)(2,1)S(1)}, bf16[64,640]{1,0:T(8,128)(2,1)S(1)}, u32[]{:S(2)}, u32[]{:S(2)}) collective-permute-start(bf16[64,640]{1,0:T(8,128)(2,1)S(1)} %reduce-precision_convert_fusion), channel_id=1, source_target_pairs={{0,128},{128,0},{1,129},{129,1},{2,130},{130,2},{3,131},{131,3},{4... | collective-permute-start | bytes 245768 | tf_op jit(solution)/shard_map/ppermute | solution.py:38
  252.6 11.1 %all-to-all-start.11 = ((bf16[4,64,1280]{2,1,0:T(8,128)(2,1)}), bf16[4,64,1280]{2,1,0:T(8,128)(2,1)S(1)}, u32[]{:S(2)}, u32[]{:S(2)}) async-start(bf16[4,64,1280]{2,1,0:T(8,128)(2,1)} %broadcast_in_dim.168), calls=%async_computation.11 | async-start | bytes 1310720 | tf_op jit(solution)/shard_map/all_to_all | solution.py:42
  263.7 7.4 %collective-permute-start.20 = (bf16[256,1280]{1,0:T(8,128)(2,1)S(1)}, bf16[256,1280]{1,0:T(8,128)(2,1)S(1)}, u32[]{:S(2)}, u32[]{:S(2)}) collective-permute-start(bf16[256,1280]{1,0:T(8,128)(2,1)S(1)} %bitcast.35), channel_id=1, source_target_pairs={{0,16},{16,0},{1,17},{17,1},{2,18},{18,2},{3,19},{19,3},{4,20},{20... | collective-permute-start | bytes 1966088 | tf_op jit(solution)/shard_map/ppermute | solution.py:38
  (19 other events, 116.4 us)

commit v4 on v3

v4 whole, which is shorter than its diff:
```python
import jax
import jax.numpy as jnp
from jax import lax
from jax.sharding import Mesh, PartitionSpec as P

DT = 8192
DS = 3584

EPS = 1e-06

F32 = jnp.float32
BF16 = jnp.bfloat16
GROUP = ("zh", "y", "c")
MODEL = ("x", "zl")
SWAP = [(0, 1), (1, 0)]
LANES = 256
PAIRS = {step: [(at, at ^ step) for at in range(4)] for step in (1, 2, 3)}


def silu_parts(values):
    sigmoid = jax.nn.sigmoid(values)
    return (values * sigmoid, sigmoid * (1.0 + values * (1.0 - sigmoid)))


def product(left, right):
    return jnp.dot(left, right, preferred_element_type=F32)


def transpose_product(left, right):
    return lax.dot_general(left, right, (((0,), (0,)), ((), ())), preferred_element_type=F32)


def product_transposed(left, right):
    return lax.dot_general(left, right, (((1,), (1,)), ((), ())), preferred_element_type=F32)


def swap(values, axis):
    return lax.ppermute(values, axis, SWAP)


def exchange(values, axis):
    return lax.all_to_all(values, axis, 0, 0, tiled=True)


def copies(values, axis):
    count = lax.axis_size(axis)
    many = jnp.broadcast_to(values[None], (count,) + values.shape)
    return many.reshape((count * values.shape[0],) + values.shape[1:])


def spread(values, axis):
    return exchange(copies(values, axis), axis)


def sum_scatter(values, axis):
    count = lax.axis_size(axis)
    parts = exchange(values, axis)
    parts = parts.reshape((count, values.shape[0] // count) + values.shape[1:])
    return jnp.sum(parts.astype(F32), axis=0)


def pair_sum(values):
    values = lax.reduce_precision(values, 8, 7)
    return values + swap(values.astype(BF16), "zh").astype(F32)


def after(values, earlier):
    return lax.optimization_barrier((values, earlier))[0]


def with_parts(values, column, place):
    high = lax.reduce_precision(column, 8, 7)
    at = lax.broadcasted_iota(jnp.int32, values.shape, 1)
    spare = jnp.where(at == place, high, column - high)
    return jnp.where((at == place) | (at == place + 1), spare, values).astype(BF16)


def column_sum(values, place):
    return values[:, place : place + 1] + values[:, place + 1 : place + 2]


def shards(
    token_ids,
    page_ids,
    tap_layer,
    teacher_in,
    teacher_gain,
    teacher_gate,
    teacher_up,
    teacher_down,
    student_embed,
    student_gain,
    student_gate,
    student_up,
    student_down,
    projection,
):
    core = lax.axis_index("c")
    x_at = lax.axis_index("x")
    z_at = lax.axis_index("zl")
    tokens = teacher_in.shape[0]
    half = tokens // 2
    models = lax.axis_size(MODEL)
    share = half // models
    block = half // lax.axis_size("y")
    width = student_gain.shape[0]
    columns = student_gate.shape[1]
    spare = LANES - width
    place = width

    def rows_at(values, start, count):
        return lax.dynamic_slice_in_dim(values, start, count, 0)

    def by_model(values):
        parts = values.reshape(2, models, share, values.shape[1])
        return jnp.swapaxes(parts, 0, 1).reshape(values.shape)

    def of_core(values, which):
        return rows_at(values, which * share, share)

    def both_cores(values, axis):
        return jnp.concatenate([values, swap(values, "c")], axis=axis)

    pages = tap_layer.shape[0]
    member = page_ids[:, None] == jnp.arange(pages, dtype=jnp.int32)[None, :]
    counts = jnp.sum(member.astype(F32), axis=0)
    page_weight = 1.0 / (pages * counts)
    token_weight = jnp.sum(jnp.where(member, page_weight[None, :], 0.0), axis=1, keepdims=True)
    token_tap = jnp.sum(jnp.where(member, tap_layer[None, :], 0), axis=1, keepdims=True)
    weight_half = rows_at(token_weight, core * half, half)
    row_start = core * half + lax.axis_index("y") * block
    weight = rows_at(token_weight, row_start, block)
    base = rows_at(teacher_in, row_start, block)

    vocab_rows = student_embed.shape[0]
    local_ids = token_ids - lax.axis_index(MODEL) * vocab_rows
    chosen = local_ids[:, None] == jnp.arange(vocab_rows, dtype=jnp.int32)[None, :]
    picked = product(chosen.astype(BF16), student_embed).astype(BF16)
    teacher_square = jnp.sum(jnp.square(teacher_in.astype(F32)), axis=1, keepdims=True)
    picked = jnp.pad(picked, ((0, 0), (0, spare)))
    payload = by_model(with_parts(picked.astype(F32), teacher_square, place))
    first = sum_scatter(payload, MODEL)

    teacher_scaled = by_model(after(teacher_in, payload) * teacher_gain)
    teacher_both = jnp.concatenate([teacher_gate, teacher_up], axis=1)
    teacher_partial = product(teacher_scaled, teacher_both).astype(BF16)
    x_sums = lax.psum_scatter(teacher_partial, "x", scatter_dimension=0, tiled=True)
    gain = jnp.pad(student_gain, (0, spare)).astype(F32)
    down_wide = jnp.pad(after(student_down, payload), ((0, 0), (0, spare)))
    proj_wide = jnp.pad(after(projection, payload), ((0, spare), (0, 0)))
    student_both = jnp.concatenate([student_gate, student_up], axis=1)
    carry = (jnp.arange(spare)[:, None] < 2) & (jnp.arange(128)[None, :] == jnp.arange(spare)[:, None])
    student_both = jnp.concatenate(
        [
            jnp.concatenate([student_both, jnp.zeros((width, 128), BF16)], axis=1),
            jnp.concatenate([jnp.zeros((spare, 2 * columns), BF16), carry.astype(BF16)], axis=1),
        ],
        axis=0,
    )
    first = after(first, (teacher_partial, down_wide, proj_wide, student_both))
    quarter = tokens // 4
    part_rows = quarter // 4

    teacher_total = column_sum(first, place)
    student_in = jnp.where(jnp.arange(LANES) < width, first, 0.0)
    student_square = jnp.sum(student_in * student_in, axis=1, keepdims=True)
    share_rows = with_parts(student_in * gain, student_square, place)
    both_rows = jnp.concatenate([share_rows, student_in.astype(BF16)], axis=1)
    rows_mine, rows_far = of_core(both_rows, core), swap(of_core(both_rows, 1 - core), "c")
    student_all = spread(jnp.concatenate([rows_mine[:, :LANES], rows_far[:, :LANES]], axis=1), MODEL)
    residual = jnp.concatenate([rows_mine[:, LANES:], rows_far[:, LANES:]], axis=1).astype(F32)

    weights_all = both_cores(student_both, 0)
    y_sums = sum_scatter(product(student_all, weights_all).astype(BF16), "y")
    y_sums = after(y_sums, x_sums)
    sums = y_sums + swap(y_sums.astype(BF16), "zh").astype(F32)
    student_scale = lax.rsqrt(column_sum(sums, 2 * columns) / DS + EPS)
    up_sum = sums[:, columns : 2 * columns] * student_scale
    active, slope = silu_parts(sums[:, :columns] * student_scale)
    hidden_copies = copies((active * up_sum).astype(BF16), "y")

    hidden_width = teacher_gate.shape[1]
    arrived = [
        lax.ppermute(rows_at(x_sums, (z_at ^ step) * part_rows, part_rows), "zl", PAIRS[step])
        for step in (3, 2, 1)
    ]
    teacher_sums = rows_at(x_sums, z_at * part_rows, part_rows).astype(F32)
    for part in after(arrived, hidden_copies):
        teacher_sums = teacher_sums + part.astype(F32)
    teacher_scale = lax.rsqrt(teacher_total / DT + EPS)
    teacher_active, _ = silu_parts(teacher_sums[:, :hidden_width] * teacher_scale)
    teacher_share = (teacher_active * (teacher_sums[:, hidden_width:] * teacher_scale)).astype(BF16)
    arrived = [lax.ppermute(teacher_share, "zl", PAIRS[step]) for step in (1, 2, 3)]

    hidden = exchange(hidden_copies, "y")
    down_all = both_cores(down_wide, 1)
    down = product(hidden, down_all).astype(BF16)
    z_all = jnp.concatenate([teacher_share] + arrived, axis=0)
    arrived = [lax.ppermute(z_all, "x", PAIRS[step]) for step in (1, 2, 3)]
    down = after(down, z_all)

    out_rows = (residual + sum_scatter(down, MODEL)).astype(BF16)
    student_out = spread(out_rows, MODEL)

    added_held = jnp.concatenate(
        [product(part, teacher_down).astype(BF16) for part in [z_all] + arrived], axis=0
    )
    held = jnp.arange(tokens, dtype=jnp.int32)
    held_model = ((held // quarter) ^ x_at) * 4 + ((held // part_rows % 4) ^ z_at)
    held_token = (held // share % 2) * half + held_model * share + held % share
    wanted = (held + core * half) % tokens
    tapped = jnp.concatenate(
        [rows_at(token_tap, core * half, half), rows_at(token_tap, (1 - core) * half, half)], axis=0
    )
    order = ((wanted[:, None] == held_token[None, :]) & (tapped == 1)).astype(BF16)
    added_far = swap(product(order[half:], added_held).astype(BF16), "c")
    added = product(order[:half], added_held) + added_far.astype(F32)

    proj_all = both_cores(proj_wide, 0)
    gap = (product(student_out, proj_all) - added).astype(BF16)
    difference = pair_sum(sum_scatter(gap, "y")) - base.astype(F32)
    pred_grad = (tokens / 16 * weight * difference).astype(BF16)
    pred = spread(pred_grad, "y")
    other_scaled = swap(student_all[:, LANES:], "c")[:, :width]
    pred, other_scaled = lax.optimization_barrier((pred, other_scaled))

    pred_float = pred.astype(F32)
    token_loss = jnp.sum(pred_float * pred_float, axis=1, keepdims=True)
    token_loss = token_loss / ((tokens / 16) ** 2 * DT * weight_half)
    out_partial = with_parts(product_transposed(pred, proj_all), token_loss, place)
    second = sum_scatter(out_partial, MODEL)
    out_all = spread(with_parts(second, column_sum(second, place), place), MODEL)

    far_at = slice(LANES, LANES + width)
    proj_far = swap(transpose_product(student_out[:, far_at], pred).astype(BF16), "c")
    out_all = after(out_all, proj_far)

    hidden_partial = product_transposed(out_all, down_all).astype(BF16)
    grad_proj = transpose_product(student_out[:, :width], after(pred, hidden_partial)) + proj_far.astype(F32)
    out_later = after(out_all, hidden_partial)
    at = lax.broadcasted_iota(jnp.int32, (half, LANES), 1)
    own_terms = out_later[:, place : place + 2]
    terms = jnp.where(at == place, own_terms[:, :1], jnp.where(at == place + 1, own_terms[:, 1:], 0))
    terms = jnp.pad(terms, ((0, hidden.shape[1] - half), (0, 0))).astype(F32)
    down_far = swap((transpose_product(hidden, out_later[:, LANES:]) + terms).astype(BF16), "c")
    grad_down = transpose_product(hidden, out_later[:, :width]) + down_far[:, :width].astype(F32)
    y_sums = after(sum_scatter(hidden_partial, "y"), down_far)
    hidden_grad, grad_down = lax.optimization_barrier((pair_sum(y_sums), grad_down))
    gate_grad = hidden_grad * up_sum * slope * student_scale
    up_grad = hidden_grad * active * student_scale
    both_copies = copies(jnp.concatenate([gate_grad, up_grad], axis=1).astype(BF16), "y")
    both_mine = exchange(both_copies, "y")

    loss_terms = jnp.stack([own_terms, down_far[:half, place : place + 2]])
    core_loss = jnp.sum(loss_terms.astype(F32), axis=(1, 2))
    loss = core_loss[0] + core_loss[1]
    both_mine, grad_proj, loss = lax.optimization_barrier((both_mine, grad_proj, loss))
    both_other = swap(both_mine, "c")
    parts = (slice(0, columns), slice(columns, 2 * columns))
    mine_grads = [transpose_product(student_all[:, :width], both_mine[:, part]) for part in parts]
    both_other, mine_grads = lax.optimization_barrier((both_other, mine_grads))
    grad_gate, grad_up = [
        mine + transpose_product(other_scaled, both_other[:, part]) for mine, part in zip(mine_grads, parts)
    ]
    return (loss, grad_gate, grad_up, grad_down, grad_proj)


def solution(mesh):
    fine = Mesh(mesh.devices.reshape(2, 4, 2, 4, 4), ("zh", "y", "c", "x", "zl"))
    placed = (
        P(),
        P(),
        P(),
        P(None, MODEL),
        P(MODEL),
        P(MODEL, GROUP),
        P(MODEL, GROUP),
        P(GROUP, MODEL),
        P(MODEL, GROUP),
        P(GROUP),
        P(GROUP, MODEL),
        P(GROUP, MODEL),
        P(MODEL, GROUP),
        P(GROUP, MODEL),
    )
    return jax.shard_map(
        shards,
        mesh=fine,
        in_specs=placed,
        out_specs=(P(), P(GROUP, MODEL), P(GROUP, MODEL), P(MODEL, GROUP), P(GROUP, MODEL)),
        check_vma=False,
    )
```

time: 276 us -> 253 us (0.917)
  waiting for transfers between devices: 78.6 us -> 37.2 us
  blocking collectives: 45.5 us -> 11 us
  starting transfers between devices: 87.6 us -> 117 us
  between operations: 3.73 us -> 17.1 us
  matrix products: 24.1 us -> 37.1 us
    all_to_all x4 -> x1, blocking collectives: 45.5 us -> 11 us  [exchange(): return lax.all_to_all(values, axis, 0, 0, tiled=True)]
    ppermute x6 -> x3, waiting for transfers between devices: 31.1 us -> 2.42 us  [shards(): lax.ppermute(rows_at(x_sums, (z_at ^ step) * part_rows, part_rows), 'zl',...]
    all_to_all x8 -> x11, starting transfers between devices: 37.9 us -> 54.4 us  [exchange(): return lax.all_to_all(values, axis, 0, 0, tiled=True)]
    ppermute x9 -> x12, starting transfers between devices: 35.3 us -> 49.7 us  [swap(): return lax.ppermute(values, axis, SWAP)]
    dot_general x11, matrix products: 15.4 us -> 22.8 us  [product(): return jnp.dot(left, right, preferred_element_type=F32)]
    ppermute x9 -> x12, waiting for transfers between devices: 15.8 us -> 8.67 us  [swap(): return lax.ppermute(values, axis, SWAP)]
    ppermute x3, waiting for transfers between devices: 5.86 us -> 0.01 us  [shards(): arrived = [lax.ppermute(z_all, 'x', PAIRS[step]) for step in (1, 2, 3)]]
    unnamed x49 -> x61, local copies, waits for them, and re-layouts: 8.42 us -> 3.63 us
  transfers between devices with their start and end apart: 29 -> 33, of which waited for: 15 -> 14; matrix products, arithmetic and copies ran while one was open for 9% -> 17% of each run, Pallas kernels for 0% -> 0%
where the time goes in v4:
time: 253 us; the launch traced here: 251 us
  starting transfers between devices  117 us (46%)
  waiting for transfers between devices  37.2 us (15%)
  matrix products  37.1 us (15%)
  between operations  17.1 us (7%)
  local copies, waits for them, and re-layouts  16.6 us (7%)
  other arithmetic  15 us (6%)
  blocking collectives  11 us (4%)
    all_to_all x11, starting transfers between devices, exchange(): return lax.all_to_all(values, axis, 0, 0, tiled=True)  54.4 us
    ppermute x12, starting transfers between devices, swap(): return lax.ppermute(values, axis, SWAP)  49.7 us
    all_to_all x11, waiting for transfers between devices, exchange(): return lax.all_to_all(values, axis, 0, 0, tiled=True)  26.1 us
    dot_general x11, matrix products, product(): return jnp.dot(left, right, preferred_element_type=F32)  22.8 us
    all_to_all x1, blocking collectives, exchange(): return lax.all_to_all(values, axis, 0, 0, tiled=True)  11 us
    dot_general x8, matrix products, transpose_product(): lax.dot_general(left, right, (((0,), (0,)), ((), ())), preferred_element_...  10.7 us
    ppermute x12, waiting for transfers between devices, swap(): return lax.ppermute(values, axis, SWAP)  8.67 us
    ppermute x3, starting transfers between devices, shards(): arrived = [lax.ppermute(z_all, 'x', PAIRS[step]) for step in (1, 2, 3)]  5.16 us
  transfers between devices with their start and end apart: 33, of which 14 were waited for; matrix products, arithmetic and copies ran while one was open for 17% of the time, Pallas kernels for 0%

profile of v4, /device:TPU:1, one launch (start us, length us, event | category | flops | bytes accessed | tf_op | source)
XLA Modules:
  0.0 251.4 jit_solution(10967857232427334261)
XLA Ops:
  9.3 2.4 fusion.17
  13.6 2.6 %convolution_convert_fusion = bf16[512,2048]{1,0:T(8,128)(2,1)} fusion(bf16[512,512]{1,0:T(8,128)(2,1)S(1)} %bitcast.65, bf16[512,1024]{1,0:T(8,128)(2,1)S(1)} %copy-done.27, bf16[512,1024]{1,0:T(8,128)(2,1)S(1)} %copy-done.28), kind=kOutput, calls=%fused_computation.3 | convolution fusion | flops 1078984704 | bytes 4718592 | tf_op jit(solution)/shard_map/dot_general | solution.py:26
  16.3 9.2 %all-to-all-start = ((bf16[16,32,256]{2,1,0:T(8,128)(2,1)}), bf16[16,32,256]{2,1,0:T(8,128)(2,1)S(1)}, u32[]{:S(2)}, u32[]{:S(2)}) async-start(bf16[16,32,256]{2,1,0:T(8,128)(2,1)} %bitcast.2), calls=%async_computation | async-start | bytes 524288 | tf_op jit(solution)/shard_map/all_to_all | solution.py:42
  30.8 4.3 %all-to-all-done = bf16[16,32,256]{2,1,0:T(8,128)(2,1)S(1)} async-done(((bf16[16,32,256]{2,1,0:T(8,128)(2,1)}), bf16[16,32,256]{2,1,0:T(8,128)(2,1)S(1)}, u32[]{:S(2)}, u32[]{:S(2)}) %all-to-all-start) | async-done | bytes 262176 | tf_op jit(solution)/shard_map/all_to_all | solution.py:42
  35.4 2.3 collective-permute-start
  39.9 3.5 %all-to-all-start.1 = ((bf16[16,16,512]{2,1,0:T(8,128)(2,1)}), bf16[16,16,512]{2,1,0:T(8,128)(2,1)S(1)}, u32[]{:S(2)}, u32[]{:S(2)}) async-start(bf16[16,16,512]{2,1,0:T(8,128)(2,1)} %broadcast_in_dim.191), calls=%async_computation.1 | async-start | bytes 524288 | tf_op jit(solution)/shard_map/all_to_all | solution.py:42
  44.3 9.2 %all-to-all-done.1 = bf16[16,16,512]{2,1,0:T(8,128)(2,1)S(1)} async-done(((bf16[16,16,512]{2,1,0:T(8,128)(2,1)}), bf16[16,16,512]{2,1,0:T(8,128)(2,1)S(1)}, u32[]{:S(2)}, u32[]{:S(2)}) %all-to-all-start.1) | async-done | bytes 262176 | tf_op jit(solution)/shard_map/all_to_all | solution.py:42
  53.4 2.9 %convolution_convert_fusion.1 = bf16[256,1408]{1,0:T(8,128)(2,1)} fusion(bf16[256,512]{1,0:T(8,128)(2,1)S(1)} %bitcast.54, bf16[256,1408]{1,0:T(8,128)(2,1)} %collective-permute-done.1, bf16[32,1408]{1,0:T(8,128)(2,1)} %copy-done.11, bf16[224,128]{1,0:T(8,128)(2,1)S(1)} %broadcast_in_dim.187, bf16[224,640]{1,0:T(8,128)(2,1)} %param.25, ...), kind=kOutput, calls=%fused_computation.4 | convolution fusion | flops 376668160 | bytes 2424832 | tf_op jit(solution)/shard_map/dot_general | solution.py:26
  56.3 4.2 %all-to-all-start.2 = ((bf16[4,64,1408]{2,1,0:T(8,128)(2,1)}), bf16[4,64,1408]{2,1,0:T(8,128)(2,1)S(1)}, u32[]{:S(2)}, u32[]{:S(2)}) async-start(bf16[4,64,1408]{2,1,0:T(8,128)(2,1)} %bitcast.64), calls=%async_computation.2 | async-start | bytes 1441792 | tf_op jit(solution)/shard_map/all_to_all | solution.py:42
  70.1 4.2 %collective-permute-start.2 = (bf16[64,1408]{1,0:T(8,128)(2,1)S(1)}, bf16[64,1408]{1,0:T(8,128)(2,1)S(1)}, u32[]{:S(2)}, u32[]{:S(2)}) collective-permute-start(bf16[64,1408]{1,0:T(8,128)(2,1)S(1)} %convert_element_type.195), channel_id=1, source_target_pairs={{0,128},{128,0},{1,129},{129,1},{2,130},{130,2},{3,131},{131,3},{4... | collective-permute-start | bytes 540680 | tf_op jit(solution)/shard_map/ppermute | solution.py:38
  77.9 2.8 %collective-permute-start.8 = (bf16[32,1024]{1,0:T(8,128)(2,1)S(1)}, bf16[32,1024]{1,0:T(8,128)(2,1)}, u32[]{:S(2)}, u32[]{:S(2)}) collective-permute-start(bf16[32,1024]{1,0:T(8,128)(2,1)S(1)} %fusion.36), channel_id=1, source_target_pairs={{0,2},{1,3},{2,0},{3,1},{4,6},{5,7},{6,4},{7,5},{8,10},{9,11},{10,... | collective-permute-start | bytes 196616 | tf_op jit(solution)/shard_map/ppermute | solution.py:193
  84.5 4.1 %all-to-all-start.3 = ((bf16[4,64,640]{2,1,0:T(8,128)(2,1)}), bf16[4,64,640]{2,1,0:T(8,128)(2,1)}, u32[]{:S(2)}, u32[]{:S(2)}) async-start(bf16[4,64,640]{2,1,0:T(8,128)(2,1)} %broadcast_in_dim.192), calls=%async_computation.4 | async-start | bytes 655360 | tf_op jit(solution)/shard_map/all_to_all | solution.py:42
  90.3 4.6 %collective-permute-start.13 = (bf16[128,1024]{1,0:T(8,128)(2,1)}, bf16[128,1024]{1,0:T(8,128)(2,1)}, u32[]{:S(2)}, u32[]{:S(2)}) collective-permute-start(bf16[128,1024]{1,0:T(8,128)(2,1)} %pad_maximum_fusion.8), channel_id=1, source_target_pairs={{0,12},{4,8},{8,4},{12,0},{1,13},{5,9},{9,5},{13,1},{2,14},{6,10},... | collective-permute-start | bytes 786440 | tf_op jit(solution)/shard_map/ppermute | solution.py:199
  99.6 8.3 %all-to-all-start.4 = ((bf16[16,16,512]{2,1,0:T(8,128)(2,1)}), bf16[16,16,512]{2,1,0:T(8,128)(2,1)}, u32[]{:S(2)}, u32[]{:S(2)}) async-start(bf16[16,16,512]{2,1,0:T(8,128)(2,1)} %bitcast.68), calls=%async_computation.5 | async-start | bytes 524288 | tf_op jit(solution)/shard_map/all_to_all | solution.py:42
  117.7 4.9 %all-to-all-start.5 = ((bf16[16,16,512]{2,1,0:T(8,128)(2,1)}), bf16[16,16,512]{2,1,0:T(8,128)(2,1)S(1)}, u32[]{:S(2)}, u32[]{:S(2)}) async-start(bf16[16,16,512]{2,1,0:T(8,128)(2,1)} %broadcast_in_dim.193), calls=%async_computation.6 | async-start | bytes 524288 | tf_op jit(solution)/shard_map/all_to_all | solution.py:42
  124.2 5.1 %collective-permute-start.14 = (bf16[256,512]{1,0:T(8,128)(2,1)S(1)}, bf16[256,512]{1,0:T(8,128)(2,1)S(1)}, u32[]{:S(2)}, u32[]{:S(2)}) collective-permute-start(bf16[256,512]{1,0:T(8,128)(2,1)S(1)} %convolution_convert_fusion.3), channel_id=1, source_target_pairs={{0,16},{16,0},{1,17},{17,1},{2,18},{18,2},{3,19},{19,3},{4,20},{20... | collective-permute-start | bytes 786440 | tf_op jit(solution)/shard_map/ppermute | solution.py:38
  133.1 4.5 %all-to-all-start.6 = ((bf16[4,64,512]{2,1,0:T(8,128)(2,1)}), bf16[4,64,512]{2,1,0:T(8,128)(2,1)S(1)}, u32[]{:S(2)}, u32[]{:S(2)}) async-start(bf16[4,64,512]{2,1,0:T(8,128)(2,1)} %bitcast.13), calls=%async_computation.7 | async-start | bytes 524288 | tf_op jit(solution)/shard_map/all_to_all | solution.py:42
  137.7 5.4 %all-to-all-done.6 = bf16[4,64,512]{2,1,0:T(8,128)(2,1)S(1)} async-done(((bf16[4,64,512]{2,1,0:T(8,128)(2,1)}), bf16[4,64,512]{2,1,0:T(8,128)(2,1)S(1)}, u32[]{:S(2)}, u32[]{:S(2)}) %all-to-all-start.6) | async-done | bytes 262176 | tf_op jit(solution)/shard_map/all_to_all | solution.py:42
  143.2 3.5 %collective-permute-start.15 = (bf16[64,512]{1,0:T(8,128)(2,1)S(1)}, bf16[64,512]{1,0:T(8,128)(2,1)S(1)}, u32[]{:S(2)}, u32[]{:S(2)}) collective-permute-start(bf16[64,512]{1,0:T(8,128)(2,1)S(1)} %reduce-precision_convert_fusion.1), channel_id=1, source_target_pairs={{0,128},{128,0},{1,129},{129,1},{2,130},{130,2},{3,131},{131,3},{4... | collective-permute-start | bytes 196616 | tf_op jit(solution)/shard_map/ppermute | solution.py:38
  146.7 3.6 %collective-permute-done.15 = bf16[64,512]{1,0:T(8,128)(2,1)S(1)} collective-permute-done((bf16[64,512]{1,0:T(8,128)(2,1)S(1)}, bf16[64,512]{1,0:T(8,128)(2,1)S(1)}, u32[]{:S(2)}, u32[]{:S(2)}) %collective-permute-start.15) | collective-permute-done | bytes 65568 | tf_op jit(solution)/shard_map/ppermute | solution.py:38
  151.9 3.4 %all-to-all-start.7 = ((bf16[4,64,512]{2,1,0:T(8,128)(2,1)}), bf16[4,64,512]{2,1,0:T(8,128)(2,1)S(1)}, u32[]{:S(2)}, u32[]{:S(2)}) async-start(bf16[4,64,512]{2,1,0:T(8,128)(2,1)} %broadcast_in_dim.196), calls=%async_computation.8 | async-start | bytes 524288 | tf_op jit(solution)/shard_map/all_to_all | solution.py:42
  155.4 8.6 %collective-permute-start.16 = (bf16[256,256]{1,0:T(8,128)(2,1)S(1)}, bf16[256,256]{1,0:T(8,128)(2,1)S(1)}, u32[]{:S(2)}, u32[]{:S(2)}) collective-permute-start(bf16[256,256]{1,0:T(8,128)(2,1)S(1)} %slice.151), channel_id=1, source_target_pairs={{0,16},{16,0},{1,17},{17,1},{2,18},{18,2},{3,19},{19,3},{4,20},{20... | collective-permute-start | bytes 393224 | tf_op jit(solution)/shard_map/ppermute | solution.py:38
  166.6 11.0 %all_to_all.108 = bf16[16,16,512]{2,1,0:T(8,128)(2,1)S(1)} all-to-all(bf16[16,16,512]{2,1,0:T(8,128)(2,1)S(1)} %bitcast.69), channel_id=1, replica_groups=mesh['zh'=2,'y'=4,'c'=2,'x'=4,'zl'=4] {'x','zl'}, dimensions={0} | all-to-all | bytes 524288 | tf_op jit(solution)/shard_map/all_to_all | solution.py:42
  178.6 3.5 %all-to-all-start.9 = ((bf16[16,16,512]{2,1,0:T(8,128)(2,1)}), bf16[16,16,512]{2,1,0:T(8,128)(2,1)S(1)}, u32[]{:S(2)}, u32[]{:S(2)}) async-start(bf16[16,16,512]{2,1,0:T(8,128)(2,1)} %broadcast_in_dim.203), calls=%async_computation.10 | async-start | bytes 524288 | tf_op jit(solution)/shard_map/all_to_all | solution.py:42
  182.4 7.1 %collective-permute-start.17 = (bf16[224,512]{1,0:T(8,128)(2,1)S(1)}, bf16[224,512]{1,0:T(8,128)(2,1)S(1)}, u32[]{:S(2)}, u32[]{:S(2)}) collective-permute-start(bf16[224,512]{1,0:T(8,128)(2,1)S(1)} %convolution_convert_fusion.5), channel_id=1, source_target_pairs={{0,16},{16,0},{1,17},{17,1},{2,18},{18,2},{3,19},{19,3},{4,20},{20... | collective-permute-start | bytes 688136 | tf_op jit(solution)/shard_map/ppermute | solution.py:38
  193.1 4.1 %all-to-all-start.10 = ((bf16[4,64,640]{2,1,0:T(8,128)(2,1)}), bf16[4,64,640]{2,1,0:T(8,128)(2,1)}, u32[]{:S(2)}, u32[]{:S(2)}) async-start(bf16[4,64,640]{2,1,0:T(8,128)(2,1)} %bitcast.17), calls=%async_computation.11 | async-start | bytes 655360 | tf_op jit(solution)/shard_map/all_to_all | solution.py:42
  199.4 7.6 %collective-permute-start.18 = (bf16[640,256]{1,0:T(8,128)(2,1)}, bf16[640,256]{1,0:T(8,128)(2,1)}, u32[]{:S(2)}, u32[]{:S(2)}) collective-permute-start(bf16[640,256]{1,0:T(8,128)(2,1)} %fusion.14), channel_id=1, source_target_pairs={{0,16},{16,0},{1,17},{17,1},{2,18},{18,2},{3,19},{19,3},{4,20},{20... | collective-permute-start | bytes 983048 | tf_op jit(solution)/shard_map/ppermute | solution.py:38
  208.5 3.5 %collective-permute-start.19 = (bf16[64,640]{1,0:T(8,128)(2,1)S(1)}, bf16[64,640]{1,0:T(8,128)(2,1)S(1)}, u32[]{:S(2)}, u32[]{:S(2)}) collective-permute-start(bf16[64,640]{1,0:T(8,128)(2,1)S(1)} %reduce-precision_convert_fusion), channel_id=1, source_target_pairs={{0,128},{128,0},{1,129},{129,1},{2,130},{130,2},{3,131},{131,3},{4... | collective-permute-start | bytes 245768 | tf_op jit(solution)/shard_map/ppermute | solution.py:38
  213.4 2.4 collective-permute-done.19
  217.0 4.6 %all-to-all-start.11 = ((bf16[4,64,1280]{2,1,0:T(8,128)(2,1)}), bf16[4,64,1280]{2,1,0:T(8,128)(2,1)}, u32[]{:S(2)}, u32[]{:S(2)}) async-start(bf16[4,64,1280]{2,1,0:T(8,128)(2,1)} %broadcast_in_dim.209), calls=%async_computation.12 | async-start | bytes 1310720 | tf_op jit(solution)/shard_map/all_to_all | solution.py:42
  226.7 2.7 %all-to-all-done.11 = bf16[4,64,1280]{2,1,0:T(8,128)(2,1)} async-done(((bf16[4,64,1280]{2,1,0:T(8,128)(2,1)}), bf16[4,64,1280]{2,1,0:T(8,128)(2,1)}, u32[]{:S(2)}, u32[]{:S(2)}) %all-to-all-start.11) | async-done | bytes 655392 | tf_op jit(solution)/shard_map/all_to_all | solution.py:42
  229.4 6.3 %collective-permute-start.20 = (bf16[256,1280]{1,0:T(8,128)(2,1)}, bf16[256,1280]{1,0:T(8,128)(2,1)}, u32[]{:S(2)}, u32[]{:S(2)}) collective-permute-start(bf16[256,1280]{1,0:T(8,128)(2,1)} %bitcast.18), channel_id=1, source_target_pairs={{0,16},{16,0},{1,17},{17,1},{2,18},{18,2},{3,19},{19,3},{4,20},{20... | collective-permute-start | bytes 1966088 | tf_op jit(solution)/shard_map/ppermute | solution.py:38
  (198 shorter events, 78.0 us)
Async XLA Ops:
  7.2 55.0 %reduce-scatter.2.cloned.1.call-start = ((), (), s32[]{:S(2)}) async-start(), calls=%async_computation.13 | async-start | bytes 2621440 | tf_op jit(solution)/shard_map/reduce_scatter | solution.py:147
  16.3 18.9 %all-to-all-start = ((bf16[16,32,256]{2,1,0:T(8,128)(2,1)}), bf16[16,32,256]{2,1,0:T(8,128)(2,1)S(1)}, u32[]{:S(2)}, u32[]{:S(2)}) async-start(bf16[16,32,256]{2,1,0:T(8,128)(2,1)} %bitcast.2), calls=%async_computation | async-start | bytes 524288 | tf_op jit(solution)/shard_map/all_to_all | solution.py:42
  27.3 16.9 %collective-permute-start.1 = (bf16[256,1408]{1,0:T(8,128)(2,1)S(1)}, bf16[256,1408]{1,0:T(8,128)(2,1)}, u32[]{:S(2)}, u32[]{:S(2)}) collective-permute-start(bf16[256,1408]{1,0:T(8,128)(2,1)S(1)} %pad_maximum_fusion), channel_id=1, source_target_pairs={{0,16},{16,0},{1,17},{17,1},{2,18},{18,2},{3,19},{19,3},{4,20},{20... | collective-permute-start | bytes 2162696 | tf_op jit(solution)/shard_map/ppermute | solution.py:38
  39.9 13.5 %all-to-all-start.1 = ((bf16[16,16,512]{2,1,0:T(8,128)(2,1)}), bf16[16,16,512]{2,1,0:T(8,128)(2,1)S(1)}, u32[]{:S(2)}, u32[]{:S(2)}) async-start(bf16[16,16,512]{2,1,0:T(8,128)(2,1)} %broadcast_in_dim.191), calls=%async_computation.1 | async-start | bytes 524288 | tf_op jit(solution)/shard_map/all_to_all | solution.py:42
  43.5 53.8 %collective-permute-start.3 = (bf16[640,256]{0,1:T(8,128)(2,1)}, bf16[640,256]{0,1:T(8,128)(2,1)}, u32[]{:S(2)}, u32[]{:S(2)}) collective-permute-start(bf16[640,256]{0,1:T(8,128)(2,1)} %pad.23), channel_id=1, source_target_pairs={{0,16},{16,0},{1,17},{17,1},{2,18},{18,2},{3,19},{19,3},{4,20},{20... | collective-permute-start | bytes 983048 | tf_op jit(solution)/shard_map/ppermute | solution.py:38
  43.9 87.0 %collective-permute-start.10 = (bf16[256,512]{1,0:T(8,128)(2,1)}, bf16[256,512]{1,0:T(8,128)(2,1)}, u32[]{:S(2)}, u32[]{:S(2)}) collective-permute-start(bf16[256,512]{1,0:T(8,128)(2,1)} %pad.24), channel_id=1, source_target_pairs={{0,16},{16,0},{1,17},{17,1},{2,18},{18,2},{3,19},{19,3},{4,20},{20... | collective-permute-start | bytes 786440 | tf_op jit(solution)/shard_map/ppermute | solution.py:38
  56.3 13.4 %all-to-all-start.2 = ((bf16[4,64,1408]{2,1,0:T(8,128)(2,1)}), bf16[4,64,1408]{2,1,0:T(8,128)(2,1)S(1)}, u32[]{:S(2)}, u32[]{:S(2)}) async-start(bf16[4,64,1408]{2,1,0:T(8,128)(2,1)} %bitcast.64), calls=%async_computation.2 | async-start | bytes 1441792 | tf_op jit(solution)/shard_map/all_to_all | solution.py:42
  64.0 6.1 %collective-permute-start.4 = (bf16[32,2048]{1,0:T(8,128)(2,1)}, bf16[32,2048]{1,0:T(8,128)(2,1)}, u32[]{:S(2)}, u32[]{:S(2)}) collective-permute-start(bf16[32,2048]{1,0:T(8,128)(2,1)} %get-tuple-element.91), channel_id=1, source_target_pairs={{0,3},{1,2},{2,1},{3,0},{4,7},{5,6},{6,5},{7,4},{8,11},{9,10},{10,... | collective-permute-start | bytes 393224 | tf_op jit(solution)/shard_map/ppermute | solution.py:184
  64.7 11.8 %collective-permute-start.5 = (bf16[32,2048]{1,0:T(8,128)(2,1)}, bf16[32,2048]{1,0:T(8,128)(2,1)}, u32[]{:S(2)}, u32[]{:S(2)}) collective-permute-start(bf16[32,2048]{1,0:T(8,128)(2,1)} %get-tuple-element.90), channel_id=1, source_target_pairs={{0,2},{1,3},{2,0},{3,1},{4,6},{5,7},{6,4},{7,5},{8,10},{9,11},{10,... | collective-permute-start | bytes 393224 | tf_op jit(solution)/shard_map/ppermute | solution.py:184
  65.3 11.2 %collective-permute-start.6 = (bf16[32,2048]{1,0:T(8,128)(2,1)}, bf16[32,2048]{1,0:T(8,128)(2,1)}, u32[]{:S(2)}, u32[]{:S(2)}) collective-permute-start(bf16[32,2048]{1,0:T(8,128)(2,1)} %get-tuple-element.89), channel_id=1, source_target_pairs={{0,1},{1,0},{2,3},{3,2},{4,5},{5,4},{6,7},{7,6},{8,9},{9,8},{10,11... | collective-permute-start | bytes 393224 | tf_op jit(solution)/shard_map/ppermute | solution.py:184
  70.1 10.6 %collective-permute-start.2 = (bf16[64,1408]{1,0:T(8,128)(2,1)S(1)}, bf16[64,1408]{1,0:T(8,128)(2,1)S(1)}, u32[]{:S(2)}, u32[]{:S(2)}) collective-permute-start(bf16[64,1408]{1,0:T(8,128)(2,1)S(1)} %convert_element_type.195), channel_id=1, source_target_pairs={{0,128},{128,0},{1,129},{129,1},{2,130},{130,2},{3,131},{131,3},{4... | collective-permute-start | bytes 540680 | tf_op jit(solution)/shard_map/ppermute | solution.py:38
  77.7 10.9 %collective-permute-start.7 = (bf16[32,1024]{1,0:T(8,128)(2,1)S(1)}, bf16[32,1024]{1,0:T(8,128)(2,1)}, u32[]{:S(2)}, u32[]{:S(2)}) collective-permute-start(bf16[32,1024]{1,0:T(8,128)(2,1)S(1)} %fusion.36), channel_id=1, source_target_pairs={{0,1},{1,0},{2,3},{3,2},{4,5},{5,4},{6,7},{7,6},{8,9},{9,8},{10,11... | collective-permute-start | bytes 196616 | tf_op jit(solution)/shard_map/ppermute | solution.py:193
  77.9 10.8 %collective-permute-start.8 = (bf16[32,1024]{1,0:T(8,128)(2,1)S(1)}, bf16[32,1024]{1,0:T(8,128)(2,1)}, u32[]{:S(2)}, u32[]{:S(2)}) collective-permute-start(bf16[32,1024]{1,0:T(8,128)(2,1)S(1)} %fusion.36), channel_id=1, source_target_pairs={{0,2},{1,3},{2,0},{3,1},{4,6},{5,7},{6,4},{7,5},{8,10},{9,11},{10,... | collective-permute-start | bytes 196616 | tf_op jit(solution)/shard_map/ppermute | solution.py:193
  80.7 7.9 %collective-permute-start.9 = (bf16[32,1024]{1,0:T(8,128)(2,1)S(1)}, bf16[32,1024]{1,0:T(8,128)(2,1)}, u32[]{:S(2)}, u32[]{:S(2)}) collective-permute-start(bf16[32,1024]{1,0:T(8,128)(2,1)S(1)} %fusion.36), channel_id=1, source_target_pairs={{0,3},{1,2},{2,1},{3,0},{4,7},{5,6},{6,5},{7,4},{8,11},{9,10},{10,... | collective-permute-start | bytes 196616 | tf_op jit(solution)/shard_map/ppermute | solution.py:193
  84.5 12.8 %all-to-all-start.3 = ((bf16[4,64,640]{2,1,0:T(8,128)(2,1)}), bf16[4,64,640]{2,1,0:T(8,128)(2,1)}, u32[]{:S(2)}, u32[]{:S(2)}) async-start(bf16[4,64,640]{2,1,0:T(8,128)(2,1)} %broadcast_in_dim.192), calls=%async_computation.4 | async-start | bytes 655360 | tf_op jit(solution)/shard_map/all_to_all | solution.py:42
  90.3 17.7 %collective-permute-start.13 = (bf16[128,1024]{1,0:T(8,128)(2,1)}, bf16[128,1024]{1,0:T(8,128)(2,1)}, u32[]{:S(2)}, u32[]{:S(2)}) collective-permute-start(bf16[128,1024]{1,0:T(8,128)(2,1)} %pad_maximum_fusion.8), channel_id=1, source_target_pairs={{0,12},{4,8},{8,4},{12,0},{1,13},{5,9},{9,5},{13,1},{2,14},{6,10},... | collective-permute-start | bytes 786440 | tf_op jit(solution)/shard_map/ppermute | solution.py:199
  94.8 15.0 %collective-permute-start.12 = (bf16[128,1024]{1,0:T(8,128)(2,1)}, bf16[128,1024]{1,0:T(8,128)(2,1)}, u32[]{:S(2)}, u32[]{:S(2)}) collective-permute-start(bf16[128,1024]{1,0:T(8,128)(2,1)} %pad_maximum_fusion.8), channel_id=1, source_target_pairs={{0,8},{4,12},{8,0},{12,4},{1,9},{5,13},{9,1},{13,5},{2,10},{6,14},... | collective-permute-start | bytes 786440 | tf_op jit(solution)/shard_map/ppermute | solution.py:199
  94.9 16.9 %collective-permute-start.11 = (bf16[128,1024]{1,0:T(8,128)(2,1)}, bf16[128,1024]{1,0:T(8,128)(2,1)}, u32[]{:S(2)}, u32[]{:S(2)}) collective-permute-start(bf16[128,1024]{1,0:T(8,128)(2,1)} %pad_maximum_fusion.8), channel_id=1, source_target_pairs={{0,4},{4,0},{8,12},{12,8},{1,5},{5,1},{9,13},{13,9},{2,6},{6,2},{1... | collective-permute-start | bytes 786440 | tf_op jit(solution)/shard_map/ppermute | solution.py:199
  99.6 16.4 %all-to-all-start.4 = ((bf16[16,16,512]{2,1,0:T(8,128)(2,1)}), bf16[16,16,512]{2,1,0:T(8,128)(2,1)}, u32[]{:S(2)}, u32[]{:S(2)}) async-start(bf16[16,16,512]{2,1,0:T(8,128)(2,1)} %bitcast.68), calls=%async_computation.5 | async-start | bytes 524288 | tf_op jit(solution)/shard_map/all_to_all | solution.py:42
  117.7 13.2 %all-to-all-start.5 = ((bf16[16,16,512]{2,1,0:T(8,128)(2,1)}), bf16[16,16,512]{2,1,0:T(8,128)(2,1)S(1)}, u32[]{:S(2)}, u32[]{:S(2)}) async-start(bf16[16,16,512]{2,1,0:T(8,128)(2,1)} %broadcast_in_dim.193), calls=%async_computation.6 | async-start | bytes 524288 | tf_op jit(solution)/shard_map/all_to_all | solution.py:42
  124.2 6.7 %collective-permute-start.14 = (bf16[256,512]{1,0:T(8,128)(2,1)S(1)}, bf16[256,512]{1,0:T(8,128)(2,1)S(1)}, u32[]{:S(2)}, u32[]{:S(2)}) collective-permute-start(bf16[256,512]{1,0:T(8,128)(2,1)S(1)} %convolution_convert_fusion.3), channel_id=1, source_target_pairs={{0,16},{16,0},{1,17},{17,1},{2,18},{18,2},{3,19},{19,3},{4,20},{20... | collective-permute-start | bytes 786440 | tf_op jit(solution)/shard_map/ppermute | solution.py:38
  133.1 10.0 %all-to-all-start.6 = ((bf16[4,64,512]{2,1,0:T(8,128)(2,1)}), bf16[4,64,512]{2,1,0:T(8,128)(2,1)S(1)}, u32[]{:S(2)}, u32[]{:S(2)}) async-start(bf16[4,64,512]{2,1,0:T(8,128)(2,1)} %bitcast.13), calls=%async_computation.7 | async-start | bytes 524288 | tf_op jit(solution)/shard_map/all_to_all | solution.py:42
  143.2 7.1 %collective-permute-start.15 = (bf16[64,512]{1,0:T(8,128)(2,1)S(1)}, bf16[64,512]{1,0:T(8,128)(2,1)S(1)}, u32[]{:S(2)}, u32[]{:S(2)}) collective-permute-start(bf16[64,512]{1,0:T(8,128)(2,1)S(1)} %reduce-precision_convert_fusion.1), channel_id=1, source_target_pairs={{0,128},{128,0},{1,129},{129,1},{2,130},{130,2},{3,131},{131,3},{4... | collective-permute-start | bytes 196616 | tf_op jit(solution)/shard_map/ppermute | solution.py:38
  151.9 13.0 %all-to-all-start.7 = ((bf16[4,64,512]{2,1,0:T(8,128)(2,1)}), bf16[4,64,512]{2,1,0:T(8,128)(2,1)S(1)}, u32[]{:S(2)}, u32[]{:S(2)}) async-start(bf16[4,64,512]{2,1,0:T(8,128)(2,1)} %broadcast_in_dim.196), calls=%async_computation.8 | async-start | bytes 524288 | tf_op jit(solution)/shard_map/all_to_all | solution.py:42
  155.4 9.5 %collective-permute-start.16 = (bf16[256,256]{1,0:T(8,128)(2,1)S(1)}, bf16[256,256]{1,0:T(8,128)(2,1)S(1)}, u32[]{:S(2)}, u32[]{:S(2)}) collective-permute-start(bf16[256,256]{1,0:T(8,128)(2,1)S(1)} %slice.151), channel_id=1, source_target_pairs={{0,16},{16,0},{1,17},{17,1},{2,18},{18,2},{3,19},{19,3},{4,20},{20... | collective-permute-start | bytes 393224 | tf_op jit(solution)/shard_map/ppermute | solution.py:38
  178.6 12.0 %all-to-all-start.9 = ((bf16[16,16,512]{2,1,0:T(8,128)(2,1)}), bf16[16,16,512]{2,1,0:T(8,128)(2,1)S(1)}, u32[]{:S(2)}, u32[]{:S(2)}) async-start(bf16[16,16,512]{2,1,0:T(8,128)(2,1)} %broadcast_in_dim.203), calls=%async_computation.10 | async-start | bytes 524288 | tf_op jit(solution)/shard_map/all_to_all | solution.py:42
  182.4 8.2 %collective-permute-start.17 = (bf16[224,512]{1,0:T(8,128)(2,1)S(1)}, bf16[224,512]{1,0:T(8,128)(2,1)S(1)}, u32[]{:S(2)}, u32[]{:S(2)}) collective-permute-start(bf16[224,512]{1,0:T(8,128)(2,1)S(1)} %convolution_convert_fusion.5), channel_id=1, source_target_pairs={{0,16},{16,0},{1,17},{17,1},{2,18},{18,2},{3,19},{19,3},{4,20},{20... | collective-permute-start | bytes 688136 | tf_op jit(solution)/shard_map/ppermute | solution.py:38
  193.1 14.0 %all-to-all-start.10 = ((bf16[4,64,640]{2,1,0:T(8,128)(2,1)}), bf16[4,64,640]{2,1,0:T(8,128)(2,1)}, u32[]{:S(2)}, u32[]{:S(2)}) async-start(bf16[4,64,640]{2,1,0:T(8,128)(2,1)} %bitcast.17), calls=%async_computation.11 | async-start | bytes 655360 | tf_op jit(solution)/shard_map/all_to_all | solution.py:42
  199.4 9.2 %collective-permute-start.18 = (bf16[640,256]{1,0:T(8,128)(2,1)}, bf16[640,256]{1,0:T(8,128)(2,1)}, u32[]{:S(2)}, u32[]{:S(2)}) collective-permute-start(bf16[640,256]{1,0:T(8,128)(2,1)} %fusion.14), channel_id=1, source_target_pairs={{0,16},{16,0},{1,17},{17,1},{2,18},{18,2},{3,19},{19,3},{4,20},{20... | collective-permute-start | bytes 983048 | tf_op jit(solution)/shard_map/ppermute | solution.py:38
  208.5 7.3 %collective-permute-start.19 = (bf16[64,640]{1,0:T(8,128)(2,1)S(1)}, bf16[64,640]{1,0:T(8,128)(2,1)S(1)}, u32[]{:S(2)}, u32[]{:S(2)}) collective-permute-start(bf16[64,640]{1,0:T(8,128)(2,1)S(1)} %reduce-precision_convert_fusion), channel_id=1, source_target_pairs={{0,128},{128,0},{1,129},{129,1},{2,130},{130,2},{3,131},{131,3},{4... | collective-permute-start | bytes 245768 | tf_op jit(solution)/shard_map/ppermute | solution.py:38
  217.0 12.4 %all-to-all-start.11 = ((bf16[4,64,1280]{2,1,0:T(8,128)(2,1)}), bf16[4,64,1280]{2,1,0:T(8,128)(2,1)}, u32[]{:S(2)}, u32[]{:S(2)}) async-start(bf16[4,64,1280]{2,1,0:T(8,128)(2,1)} %broadcast_in_dim.209), calls=%async_computation.12 | async-start | bytes 1310720 | tf_op jit(solution)/shard_map/all_to_all | solution.py:42
  229.4 9.8 %collective-permute-start.20 = (bf16[256,1280]{1,0:T(8,128)(2,1)}, bf16[256,1280]{1,0:T(8,128)(2,1)}, u32[]{:S(2)}, u32[]{:S(2)}) collective-permute-start(bf16[256,1280]{1,0:T(8,128)(2,1)} %bitcast.18), channel_id=1, source_target_pairs={{0,16},{16,0},{1,17},{17,1},{2,18},{18,2},{3,19},{19,3},{4,20},{20... | collective-permute-start | bytes 1966088 | tf_op jit(solution)/shard_map/ppermute | solution.py:38
  (31 other events, 505.0 us)
Sparse Core Ops, SparseCore 0:
  16.4 39.6 reduce-scatter.1

commit v5 on v4

--- a/solution.py
+++ b/solution.py
@@ -218,22 +218,20 @@
 
     proj_all = both_cores(proj_wide, 0)
     gap = (product(student_out, proj_all) - added).astype(BF16)
-    difference = pair_sum(sum_scatter(gap, "y")) - base.astype(F32)
+    other_scaled = swap(student_all[:, LANES:], "c")[:, :width]
+    gap_sums, other_scaled = lax.optimization_barrier((sum_scatter(gap, "y"), other_scaled))
+    difference = pair_sum(gap_sums) - base.astype(F32)
     pred_grad = (tokens / 16 * weight * difference).astype(BF16)
     pred = spread(pred_grad, "y")
-    other_scaled = swap(student_all[:, LANES:], "c")[:, :width]
-    pred, other_scaled = lax.optimization_barrier((pred, other_scaled))
 
     pred_float = pred.astype(F32)
     token_loss = jnp.sum(pred_float * pred_float, axis=1, keepdims=True)
     token_loss = token_loss / ((tokens / 16) ** 2 * DT * weight_half)
     out_partial = with_parts(product_transposed(pred, proj_all), token_loss, place)
-    second = sum_scatter(out_partial, MODEL)
-    out_all = spread(with_parts(second, column_sum(second, place), place), MODEL)
-
     far_at = slice(LANES, LANES + width)
     proj_far = swap(transpose_product(student_out[:, far_at], pred).astype(BF16), "c")
-    out_all = after(out_all, proj_far)
+    second, proj_far = lax.optimization_barrier((sum_scatter(out_partial, MODEL), proj_far))
+    out_all = spread(with_parts(second, column_sum(second, place), place), MODEL)
 
     hidden_partial = product_transposed(out_all, down_all).astype(BF16)
     grad_proj = transpose_product(student_out[:, :width], after(pred, hidden_partial)) + proj_far.astype(F32)
@@ -257,10 +255,10 @@
     both_mine, grad_proj, loss = lax.optimization_barrier((both_mine, grad_proj, loss))
     both_other = swap(both_mine, "c")
     parts = (slice(0, columns), slice(columns, 2 * columns))
-    mine_grads = [transpose_product(student_all[:, :width], both_mine[:, part]) for part in parts]
-    both_other, mine_grads = lax.optimization_barrier((both_other, mine_grads))
     grad_gate, grad_up = [
-        mine + transpose_product(other_scaled, both_other[:, part]) for mine, part in zip(mine_grads, parts)
+        transpose_product(student_all[:, :width], both_mine[:, part])
+        + transpose_product(other_scaled, both_other[:, part])
+        for part in parts
     ]
     return (loss, grad_gate, grad_up, grad_down, grad_proj)
 

time: 253 us -> 261 us (1.032)
  waiting for transfers between devices: 37.2 us -> 51.7 us
  blocking collectives: 11 us -> 0 us
    all_to_all x11 -> x12, waiting for transfers between devices: 26.1 us -> 42.7 us  [exchange(): return lax.all_to_all(values, axis, 0, 0, tiled=True)]
    all_to_all x1 -> x0, blocking collectives: 11 us -> none  [exchange(): return lax.all_to_all(values, axis, 0, 0, tiled=True)]
    ppermute x12, starting transfers between devices: 49.7 us -> 40.4 us  [swap(): return lax.ppermute(values, axis, SWAP)]
    all_to_all x11 -> x12, starting transfers between devices: 54.4 us -> 63.1 us  [exchange(): return lax.all_to_all(values, axis, 0, 0, tiled=True)]
  transfers between devices with their start and end apart: 33 -> 34, of which waited for: 14 -> 16; matrix products, arithmetic and copies ran while one was open for 17% -> 17% of each run, Pallas kernels for 0% -> 0%
where the time goes in v5:
time: 261 us; the launch traced here: 258 us
  starting transfers between devices  117 us (45%)
  waiting for transfers between devices  51.7 us (20%)
  matrix products  38.8 us (15%)
  between operations  17.1 us (7%)
  other arithmetic  16.9 us (6%)
  local copies, waits for them, and re-layouts  16.7 us (6%)
    all_to_all x12, starting transfers between devices, exchange(): return lax.all_to_all(values, axis, 0, 0, tiled=True)  63.1 us
    all_to_all x12, waiting for transfers between devices, exchange(): return lax.all_to_all(values, axis, 0, 0, tiled=True)  42.7 us
    ppermute x12, starting transfers between devices, swap(): return lax.ppermute(values, axis, SWAP)  40.4 us
    dot_general x11, matrix products, product(): return jnp.dot(left, right, preferred_element_type=F32)  22.6 us
    dot_general x8, matrix products, transpose_product(): lax.dot_general(left, right, (((0,), (0,)), ((), ())), preferred_element_...  11.9 us
    ppermute x12, waiting for transfers between devices, swap(): return lax.ppermute(values, axis, SWAP)  6.71 us
  transfers between devices with their start and end apart: 34, of which 16 were waited for; matrix products, arithmetic and copies ran while one was open for 17% of the time, Pallas kernels for 0%

profile of v5, /device:TPU:1, one launch (start us, length us, event | category | flops | bytes accessed | tf_op | source)
XLA Modules:
  0.0 258.1 jit_solution(12543133971018971952)
XLA Ops:
  9.3 2.4 fusion.17
  13.6 2.6 %convolution_convert_fusion = bf16[512,2048]{1,0:T(8,128)(2,1)} fusion(bf16[512,512]{1,0:T(8,128)(2,1)S(1)} %bitcast.66, bf16[512,1024]{1,0:T(8,128)(2,1)S(1)} %copy-done.24, bf16[512,1024]{1,0:T(8,128)(2,1)S(1)} %copy-done.25), kind=kOutput, calls=%fused_computation.3 | convolution fusion | flops 1078984704 | bytes 4718592 | tf_op jit(solution)/shard_map/dot_general | solution.py:26
  16.3 9.2 %all-to-all-start = ((bf16[16,32,256]{2,1,0:T(8,128)(2,1)}), bf16[16,32,256]{2,1,0:T(8,128)(2,1)S(1)}, u32[]{:S(2)}, u32[]{:S(2)}) async-start(bf16[16,32,256]{2,1,0:T(8,128)(2,1)} %bitcast.2), calls=%async_computation | async-start | bytes 524288 | tf_op jit(solution)/shard_map/all_to_all | solution.py:42
  30.8 4.3 %all-to-all-done = bf16[16,32,256]{2,1,0:T(8,128)(2,1)S(1)} async-done(((bf16[16,32,256]{2,1,0:T(8,128)(2,1)}), bf16[16,32,256]{2,1,0:T(8,128)(2,1)S(1)}, u32[]{:S(2)}, u32[]{:S(2)}) %all-to-all-start) | async-done | bytes 262176 | tf_op jit(solution)/shard_map/all_to_all | solution.py:42
  39.9 3.5 %all-to-all-start.1 = ((bf16[16,16,512]{2,1,0:T(8,128)(2,1)}), bf16[16,16,512]{2,1,0:T(8,128)(2,1)S(1)}, u32[]{:S(2)}, u32[]{:S(2)}) async-start(bf16[16,16,512]{2,1,0:T(8,128)(2,1)} %broadcast_in_dim.191), calls=%async_computation.1 | async-start | bytes 524288 | tf_op jit(solution)/shard_map/all_to_all | solution.py:42
  44.3 9.2 %all-to-all-done.1 = bf16[16,16,512]{2,1,0:T(8,128)(2,1)S(1)} async-done(((bf16[16,16,512]{2,1,0:T(8,128)(2,1)}), bf16[16,16,512]{2,1,0:T(8,128)(2,1)S(1)}, u32[]{:S(2)}, u32[]{:S(2)}) %all-to-all-start.1) | async-done | bytes 262176 | tf_op jit(solution)/shard_map/all_to_all | solution.py:42
  53.4 2.7 %convolution_convert_fusion.1 = bf16[256,1408]{1,0:T(8,128)(2,1)} fusion(bf16[256,512]{1,0:T(8,128)(2,1)S(1)} %bitcast.53, bf16[256,1408]{1,0:T(8,128)(2,1)} %collective-permute-done.1, bf16[32,1408]{1,0:T(8,128)(2,1)S(1)} %pad_convert_fusion, bf16[224,128]{1,0:T(8,128)(2,1)} %copy-done.10, bf16[224,640]{1,0:T(8,128)(2,1)} %param.25, bf16[224,640]{1,0:T(8,128)(2,1)} %param.24), kind=kOutput, calls=%fused_computation.4 | convolution fusion | flops 376668160 | bytes 2424832 | tf_op jit(solution)/shard_map/dot_general | solution.py:26
  56.2 4.2 %all-to-all-start.2 = ((bf16[4,64,1408]{2,1,0:T(8,128)(2,1)}), bf16[4,64,1408]{2,1,0:T(8,128)(2,1)S(1)}, u32[]{:S(2)}, u32[]{:S(2)}) async-start(bf16[4,64,1408]{2,1,0:T(8,128)(2,1)} %bitcast.63), calls=%async_computation.2 | async-start | bytes 1441792 | tf_op jit(solution)/shard_map/all_to_all | solution.py:42
  69.9 4.2 %collective-permute-start.2 = (bf16[64,1408]{1,0:T(8,128)(2,1)S(1)}, bf16[64,1408]{1,0:T(8,128)(2,1)S(1)}, u32[]{:S(2)}, u32[]{:S(2)}) collective-permute-start(bf16[64,1408]{1,0:T(8,128)(2,1)S(1)} %convert_element_type.192), channel_id=1, source_target_pairs={{0,128},{128,0},{1,129},{129,1},{2,130},{130,2},{3,131},{131,3},{4... | collective-permute-start | bytes 540680 | tf_op jit(solution)/shard_map/ppermute | solution.py:38
  77.7 2.8 %collective-permute-start.8 = (bf16[32,1024]{1,0:T(8,128)(2,1)S(1)}, bf16[32,1024]{1,0:T(8,128)(2,1)}, u32[]{:S(2)}, u32[]{:S(2)}) collective-permute-start(bf16[32,1024]{1,0:T(8,128)(2,1)S(1)} %fusion.32), channel_id=1, source_target_pairs={{0,2},{1,3},{2,0},{3,1},{4,6},{5,7},{6,4},{7,5},{8,10},{9,11},{10,... | collective-permute-start | bytes 196616 | tf_op jit(solution)/shard_map/ppermute | solution.py:193
  84.3 4.1 %all-to-all-start.3 = ((bf16[4,64,640]{2,1,0:T(8,128)(2,1)}), bf16[4,64,640]{2,1,0:T(8,128)(2,1)}, u32[]{:S(2)}, u32[]{:S(2)}) async-start(bf16[4,64,640]{2,1,0:T(8,128)(2,1)} %broadcast_in_dim.192), calls=%async_computation.4 | async-start | bytes 655360 | tf_op jit(solution)/shard_map/all_to_all | solution.py:42
  90.1 4.6 %collective-permute-start.13 = (bf16[128,1024]{1,0:T(8,128)(2,1)}, bf16[128,1024]{1,0:T(8,128)(2,1)}, u32[]{:S(2)}, u32[]{:S(2)}) collective-permute-start(bf16[128,1024]{1,0:T(8,128)(2,1)} %pad_maximum_fusion.8), channel_id=1, source_target_pairs={{0,12},{4,8},{8,4},{12,0},{1,13},{5,9},{9,5},{13,1},{2,14},{6,10},... | collective-permute-start | bytes 786440 | tf_op jit(solution)/shard_map/ppermute | solution.py:199
  99.4 8.3 %all-to-all-start.4 = ((bf16[16,16,512]{2,1,0:T(8,128)(2,1)}), bf16[16,16,512]{2,1,0:T(8,128)(2,1)}, u32[]{:S(2)}, u32[]{:S(2)}) async-start(bf16[16,16,512]{2,1,0:T(8,128)(2,1)} %bitcast.68), calls=%async_computation.5 | async-start | bytes 524288 | tf_op jit(solution)/shard_map/all_to_all | solution.py:42
  117.5 4.9 %all-to-all-start.5 = ((bf16[16,16,512]{2,1,0:T(8,128)(2,1)}), bf16[16,16,512]{2,1,0:T(8,128)(2,1)S(1)}, u32[]{:S(2)}, u32[]{:S(2)}) async-start(bf16[16,16,512]{2,1,0:T(8,128)(2,1)} %broadcast_in_dim.193), calls=%async_computation.6 | async-start | bytes 524288 | tf_op jit(solution)/shard_map/all_to_all | solution.py:42
  124.0 5.1 %collective-permute-start.14 = (bf16[256,512]{1,0:T(8,128)(2,1)S(1)}, bf16[256,512]{1,0:T(8,128)(2,1)S(1)}, u32[]{:S(2)}, u32[]{:S(2)}) collective-permute-start(bf16[256,512]{1,0:T(8,128)(2,1)S(1)} %convolution_convert_fusion.3), channel_id=1, source_target_pairs={{0,16},{16,0},{1,17},{17,1},{2,18},{18,2},{3,19},{19,3},{4,20},{20... | collective-permute-start | bytes 786440 | tf_op jit(solution)/shard_map/ppermute | solution.py:38
  132.8 4.5 %all-to-all-start.6 = ((bf16[4,64,512]{2,1,0:T(8,128)(2,1)}), bf16[4,64,512]{2,1,0:T(8,128)(2,1)S(1)}, u32[]{:S(2)}, u32[]{:S(2)}) async-start(bf16[4,64,512]{2,1,0:T(8,128)(2,1)} %bitcast.13), calls=%async_computation.7 | async-start | bytes 524288 | tf_op jit(solution)/shard_map/all_to_all | solution.py:42
  137.3 6.3 %collective-permute-start.15 = (bf16[256,256]{1,0:T(8,128)(2,1)S(1)}, bf16[256,256]{1,0:T(8,128)(2,1)S(1)}, u32[]{:S(2)}, u32[]{:S(2)}) collective-permute-start(bf16[256,256]{1,0:T(8,128)(2,1)S(1)} %slice.151), channel_id=1, source_target_pairs={{0,16},{16,0},{1,17},{17,1},{2,18},{18,2},{3,19},{19,3},{4,20},{20... | collective-permute-start | bytes 393224 | tf_op jit(solution)/shard_map/ppermute | solution.py:38
  144.6 3.5 %collective-permute-start.16 = (bf16[64,512]{1,0:T(8,128)(2,1)S(1)}, bf16[64,512]{1,0:T(8,128)(2,1)S(1)}, u32[]{:S(2)}, u32[]{:S(2)}) collective-permute-start(bf16[64,512]{1,0:T(8,128)(2,1)S(1)} %reduce-precision_convert_fusion.1), channel_id=1, source_target_pairs={{0,128},{128,0},{1,129},{129,1},{2,130},{130,2},{3,131},{131,3},{4... | collective-permute-start | bytes 196616 | tf_op jit(solution)/shard_map/ppermute | solution.py:38
  148.2 3.5 %collective-permute-done.16 = bf16[64,512]{1,0:T(8,128)(2,1)S(1)} collective-permute-done((bf16[64,512]{1,0:T(8,128)(2,1)S(1)}, bf16[64,512]{1,0:T(8,128)(2,1)S(1)}, u32[]{:S(2)}, u32[]{:S(2)}) %collective-permute-start.16) | collective-permute-done | bytes 65568 | tf_op jit(solution)/shard_map/ppermute | solution.py:38
  153.4 4.5 %all-to-all-start.7 = ((bf16[4,64,512]{2,1,0:T(8,128)(2,1)}), bf16[4,64,512]{2,1,0:T(8,128)(2,1)S(1)}, u32[]{:S(2)}, u32[]{:S(2)}) async-start(bf16[4,64,512]{2,1,0:T(8,128)(2,1)} %broadcast_in_dim.196), calls=%async_computation.8 | async-start | bytes 524288 | tf_op jit(solution)/shard_map/all_to_all | solution.py:42
  157.9 5.5 %all-to-all-done.7 = bf16[4,64,512]{2,1,0:T(8,128)(2,1)S(1)} async-done(((bf16[4,64,512]{2,1,0:T(8,128)(2,1)}), bf16[4,64,512]{2,1,0:T(8,128)(2,1)S(1)}, u32[]{:S(2)}, u32[]{:S(2)}) %all-to-all-start.7) | async-done | bytes 262176 | tf_op jit(solution)/shard_map/all_to_all | solution.py:42
  165.9 4.4 %all-to-all-start.8 = ((bf16[16,16,512]{2,1,0:T(8,128)(2,1)}), bf16[16,16,512]{2,1,0:T(8,128)(2,1)S(1)}, u32[]{:S(2)}, u32[]{:S(2)}) async-start(bf16[16,16,512]{2,1,0:T(8,128)(2,1)} %bitcast.69), calls=%async_computation.9 | async-start | bytes 524288 | tf_op jit(solution)/shard_map/all_to_all | solution.py:42
  171.2 6.0 %collective-permute-start.17 = (bf16[224,512]{1,0:T(8,128)(2,1)}, bf16[224,512]{1,0:T(8,128)(2,1)}, u32[]{:S(2)}, u32[]{:S(2)}) collective-permute-start(bf16[224,512]{1,0:T(8,128)(2,1)} %convolution_convert_fusion.5), channel_id=1, source_target_pairs={{0,16},{16,0},{1,17},{17,1},{2,18},{18,2},{3,19},{19,3},{4,20},{20... | collective-permute-start | bytes 688136 | tf_op jit(solution)/shard_map/ppermute | solution.py:38
  180.3 7.2 %all-to-all-start.9 = ((bf16[16,16,512]{2,1,0:T(8,128)(2,1)}), bf16[16,16,512]{2,1,0:T(8,128)(2,1)S(1)}, u32[]{:S(2)}, u32[]{:S(2)}) async-start(bf16[16,16,512]{2,1,0:T(8,128)(2,1)} %broadcast_in_dim.203), calls=%async_computation.10 | async-start | bytes 524288 | tf_op jit(solution)/shard_map/all_to_all | solution.py:42
  188.0 7.6 %all-to-all-done.9 = bf16[16,16,512]{2,1,0:T(8,128)(2,1)S(1)} async-done(((bf16[16,16,512]{2,1,0:T(8,128)(2,1)}), bf16[16,16,512]{2,1,0:T(8,128)(2,1)S(1)}, u32[]{:S(2)}, u32[]{:S(2)}) %all-to-all-start.9) | async-done | bytes 262176 | tf_op jit(solution)/shard_map/all_to_all | solution.py:42
  200.9 4.1 %collective-permute-start.18 = (bf16[640,256]{1,0:T(8,128)(2,1)}, bf16[640,256]{1,0:T(8,128)(2,1)}, u32[]{:S(2)}, u32[]{:S(2)}) collective-permute-start(bf16[640,256]{1,0:T(8,128)(2,1)} %fusion.14), channel_id=1, source_target_pairs={{0,16},{16,0},{1,17},{17,1},{2,18},{18,2},{3,19},{19,3},{4,20},{20... | collective-permute-start | bytes 983048 | tf_op jit(solution)/shard_map/ppermute | solution.py:38
  205.1 4.1 %all-to-all-start.10 = ((bf16[4,64,640]{2,1,0:T(8,128)(2,1)}), bf16[4,64,640]{2,1,0:T(8,128)(2,1)}, u32[]{:S(2)}, u32[]{:S(2)}) async-start(bf16[4,64,640]{2,1,0:T(8,128)(2,1)} %bitcast.67), calls=%async_computation.11 | async-start | bytes 655360 | tf_op jit(solution)/shard_map/all_to_all | solution.py:42
  210.2 6.6 %all-to-all-done.10 = bf16[4,64,640]{2,1,0:T(8,128)(2,1)} async-done(((bf16[4,64,640]{2,1,0:T(8,128)(2,1)}), bf16[4,64,640]{2,1,0:T(8,128)(2,1)}, u32[]{:S(2)}, u32[]{:S(2)}) %all-to-all-start.10) | async-done | bytes 327712 | tf_op jit(solution)/shard_map/all_to_all | solution.py:42
  217.9 4.2 %collective-permute-start.19 = (bf16[64,640]{1,0:T(8,128)(2,1)S(1)}, bf16[64,640]{1,0:T(8,128)(2,1)S(1)}, u32[]{:S(2)}, u32[]{:S(2)}) collective-permute-start(bf16[64,640]{1,0:T(8,128)(2,1)S(1)} %reduce-precision_convert_fusion), channel_id=1, source_target_pairs={{0,128},{128,0},{1,129},{129,1},{2,130},{130,2},{3,131},{131,3},{4... | collective-permute-start | bytes 245768 | tf_op jit(solution)/shard_map/ppermute | solution.py:38
  226.4 4.2 %all-to-all-start.11 = ((bf16[4,64,1280]{2,1,0:T(8,128)(2,1)}), bf16[4,64,1280]{2,1,0:T(8,128)(2,1)}, u32[]{:S(2)}, u32[]{:S(2)}) async-start(bf16[4,64,1280]{2,1,0:T(8,128)(2,1)} %broadcast_in_dim.209), calls=%async_computation.12 | async-start | bytes 1310720 | tf_op jit(solution)/shard_map/all_to_all | solution.py:42
  235.6 3.9 %all-to-all-done.11 = bf16[4,64,1280]{2,1,0:T(8,128)(2,1)} async-done(((bf16[4,64,1280]{2,1,0:T(8,128)(2,1)}), bf16[4,64,1280]{2,1,0:T(8,128)(2,1)}, u32[]{:S(2)}, u32[]{:S(2)}) %all-to-all-start.11) | async-done | bytes 655392 | tf_op jit(solution)/shard_map/all_to_all | solution.py:42
  239.5 3.0 %collective-permute-start.20 = (bf16[256,1280]{1,0:T(8,128)(2,1)}, bf16[256,1280]{1,0:T(8,128)(2,1)}, u32[]{:S(2)}, u32[]{:S(2)}) collective-permute-start(bf16[256,1280]{1,0:T(8,128)(2,1)} %bitcast.18), channel_id=1, source_target_pairs={{0,16},{16,0},{1,17},{17,1},{2,18},{18,2},{3,19},{19,3},{4,20},{20... | collective-permute-start | bytes 1966088 | tf_op jit(solution)/shard_map/ppermute | solution.py:38
  (193 shorter events, 85.7 us)
Async XLA Ops:
  7.2 54.8 %reduce-scatter.2.cloned.1.call-start = ((), (), s32[]{:S(2)}) async-start(), calls=%async_computation.13 | async-start | bytes 2621440 | tf_op jit(solution)/shard_map/reduce_scatter | solution.py:147
  16.3 18.9 %all-to-all-start = ((bf16[16,32,256]{2,1,0:T(8,128)(2,1)}), bf16[16,32,256]{2,1,0:T(8,128)(2,1)S(1)}, u32[]{:S(2)}, u32[]{:S(2)}) async-start(bf16[16,32,256]{2,1,0:T(8,128)(2,1)} %bitcast.2), calls=%async_computation | async-start | bytes 524288 | tf_op jit(solution)/shard_map/all_to_all | solution.py:42
  27.3 16.9 %collective-permute-start.1 = (bf16[256,1408]{1,0:T(8,128)(2,1)S(1)}, bf16[256,1408]{1,0:T(8,128)(2,1)}, u32[]{:S(2)}, u32[]{:S(2)}) collective-permute-start(bf16[256,1408]{1,0:T(8,128)(2,1)S(1)} %pad_maximum_fusion), channel_id=1, source_target_pairs={{0,16},{16,0},{1,17},{17,1},{2,18},{18,2},{3,19},{19,3},{4,20},{20... | collective-permute-start | bytes 2162696 | tf_op jit(solution)/shard_map/ppermute | solution.py:38
  39.9 13.5 %all-to-all-start.1 = ((bf16[16,16,512]{2,1,0:T(8,128)(2,1)}), bf16[16,16,512]{2,1,0:T(8,128)(2,1)S(1)}, u32[]{:S(2)}, u32[]{:S(2)}) async-start(bf16[16,16,512]{2,1,0:T(8,128)(2,1)} %broadcast_in_dim.191), calls=%async_computation.1 | async-start | bytes 524288 | tf_op jit(solution)/shard_map/all_to_all | solution.py:42
  43.5 53.7 %collective-permute-start.3 = (bf16[640,256]{0,1:T(8,128)(2,1)}, bf16[640,256]{0,1:T(8,128)(2,1)}, u32[]{:S(2)}, u32[]{:S(2)}) collective-permute-start(bf16[640,256]{0,1:T(8,128)(2,1)} %pad.23), channel_id=1, source_target_pairs={{0,16},{16,0},{1,17},{17,1},{2,18},{18,2},{3,19},{19,3},{4,20},{20... | collective-permute-start | bytes 983048 | tf_op jit(solution)/shard_map/ppermute | solution.py:38
  43.9 86.8 %collective-permute-start.10 = (bf16[256,512]{1,0:T(8,128)(2,1)}, bf16[256,512]{1,0:T(8,128)(2,1)}, u32[]{:S(2)}, u32[]{:S(2)}) collective-permute-start(bf16[256,512]{1,0:T(8,128)(2,1)} %pad.24), channel_id=1, source_target_pairs={{0,16},{16,0},{1,17},{17,1},{2,18},{18,2},{3,19},{19,3},{4,20},{20... | collective-permute-start | bytes 786440 | tf_op jit(solution)/shard_map/ppermute | solution.py:38
  56.2 13.4 %all-to-all-start.2 = ((bf16[4,64,1408]{2,1,0:T(8,128)(2,1)}), bf16[4,64,1408]{2,1,0:T(8,128)(2,1)S(1)}, u32[]{:S(2)}, u32[]{:S(2)}) async-start(bf16[4,64,1408]{2,1,0:T(8,128)(2,1)} %bitcast.63), calls=%async_computation.2 | async-start | bytes 1441792 | tf_op jit(solution)/shard_map/all_to_all | solution.py:42
  64.5 11.7 %collective-permute-start.5 = (bf16[32,2048]{1,0:T(8,128)(2,1)}, bf16[32,2048]{1,0:T(8,128)(2,1)}, u32[]{:S(2)}, u32[]{:S(2)}) collective-permute-start(bf16[32,2048]{1,0:T(8,128)(2,1)} %get-tuple-element.86), channel_id=1, source_target_pairs={{0,2},{1,3},{2,0},{3,1},{4,6},{5,7},{6,4},{7,5},{8,10},{9,11},{10,... | collective-permute-start | bytes 393224 | tf_op jit(solution)/shard_map/ppermute | solution.py:184
  65.1 11.1 %collective-permute-start.6 = (bf16[32,2048]{1,0:T(8,128)(2,1)}, bf16[32,2048]{1,0:T(8,128)(2,1)}, u32[]{:S(2)}, u32[]{:S(2)}) collective-permute-start(bf16[32,2048]{1,0:T(8,128)(2,1)} %get-tuple-element.85), channel_id=1, source_target_pairs={{0,1},{1,0},{2,3},{3,2},{4,5},{5,4},{6,7},{7,6},{8,9},{9,8},{10,11... | collective-permute-start | bytes 393224 | tf_op jit(solution)/shard_map/ppermute | solution.py:184
  69.9 10.6 %collective-permute-start.2 = (bf16[64,1408]{1,0:T(8,128)(2,1)S(1)}, bf16[64,1408]{1,0:T(8,128)(2,1)S(1)}, u32[]{:S(2)}, u32[]{:S(2)}) collective-permute-start(bf16[64,1408]{1,0:T(8,128)(2,1)S(1)} %convert_element_type.192), channel_id=1, source_target_pairs={{0,128},{128,0},{1,129},{129,1},{2,130},{130,2},{3,131},{131,3},{4... | collective-permute-start | bytes 540680 | tf_op jit(solution)/shard_map/ppermute | solution.py:38
  77.5 10.9 %collective-permute-start.7 = (bf16[32,1024]{1,0:T(8,128)(2,1)S(1)}, bf16[32,1024]{1,0:T(8,128)(2,1)}, u32[]{:S(2)}, u32[]{:S(2)}) collective-permute-start(bf16[32,1024]{1,0:T(8,128)(2,1)S(1)} %fusion.32), channel_id=1, source_target_pairs={{0,1},{1,0},{2,3},{3,2},{4,5},{5,4},{6,7},{7,6},{8,9},{9,8},{10,11... | collective-permute-start | bytes 196616 | tf_op jit(solution)/shard_map/ppermute | solution.py:193
  77.7 10.8 %collective-permute-start.8 = (bf16[32,1024]{1,0:T(8,128)(2,1)S(1)}, bf16[32,1024]{1,0:T(8,128)(2,1)}, u32[]{:S(2)}, u32[]{:S(2)}) collective-permute-start(bf16[32,1024]{1,0:T(8,128)(2,1)S(1)} %fusion.32), channel_id=1, source_target_pairs={{0,2},{1,3},{2,0},{3,1},{4,6},{5,7},{6,4},{7,5},{8,10},{9,11},{10,... | collective-permute-start | bytes 196616 | tf_op jit(solution)/shard_map/ppermute | solution.py:193
  80.5 8.0 %collective-permute-start.9 = (bf16[32,1024]{1,0:T(8,128)(2,1)S(1)}, bf16[32,1024]{1,0:T(8,128)(2,1)}, u32[]{:S(2)}, u32[]{:S(2)}) collective-permute-start(bf16[32,1024]{1,0:T(8,128)(2,1)S(1)} %fusion.32), channel_id=1, source_target_pairs={{0,3},{1,2},{2,1},{3,0},{4,7},{5,6},{6,5},{7,4},{8,11},{9,10},{10,... | collective-permute-start | bytes 196616 | tf_op jit(solution)/shard_map/ppermute | solution.py:193
  84.3 12.8 %all-to-all-start.3 = ((bf16[4,64,640]{2,1,0:T(8,128)(2,1)}), bf16[4,64,640]{2,1,0:T(8,128)(2,1)}, u32[]{:S(2)}, u32[]{:S(2)}) async-start(bf16[4,64,640]{2,1,0:T(8,128)(2,1)} %broadcast_in_dim.192), calls=%async_computation.4 | async-start | bytes 655360 | tf_op jit(solution)/shard_map/all_to_all | solution.py:42
  90.1 17.7 %collective-permute-start.13 = (bf16[128,1024]{1,0:T(8,128)(2,1)}, bf16[128,1024]{1,0:T(8,128)(2,1)}, u32[]{:S(2)}, u32[]{:S(2)}) collective-permute-start(bf16[128,1024]{1,0:T(8,128)(2,1)} %pad_maximum_fusion.8), channel_id=1, source_target_pairs={{0,12},{4,8},{8,4},{12,0},{1,13},{5,9},{9,5},{13,1},{2,14},{6,10},... | collective-permute-start | bytes 786440 | tf_op jit(solution)/shard_map/ppermute | solution.py:199
  94.7 15.0 %collective-permute-start.12 = (bf16[128,1024]{1,0:T(8,128)(2,1)}, bf16[128,1024]{1,0:T(8,128)(2,1)}, u32[]{:S(2)}, u32[]{:S(2)}) collective-permute-start(bf16[128,1024]{1,0:T(8,128)(2,1)} %pad_maximum_fusion.8), channel_id=1, source_target_pairs={{0,8},{4,12},{8,0},{12,4},{1,9},{5,13},{9,1},{13,5},{2,10},{6,14},... | collective-permute-start | bytes 786440 | tf_op jit(solution)/shard_map/ppermute | solution.py:199
  94.7 16.9 %collective-permute-start.11 = (bf16[128,1024]{1,0:T(8,128)(2,1)}, bf16[128,1024]{1,0:T(8,128)(2,1)}, u32[]{:S(2)}, u32[]{:S(2)}) collective-permute-start(bf16[128,1024]{1,0:T(8,128)(2,1)} %pad_maximum_fusion.8), channel_id=1, source_target_pairs={{0,4},{4,0},{8,12},{12,8},{1,5},{5,1},{9,13},{13,9},{2,6},{6,2},{1... | collective-permute-start | bytes 786440 | tf_op jit(solution)/shard_map/ppermute | solution.py:199
  99.4 16.4 %all-to-all-start.4 = ((bf16[16,16,512]{2,1,0:T(8,128)(2,1)}), bf16[16,16,512]{2,1,0:T(8,128)(2,1)}, u32[]{:S(2)}, u32[]{:S(2)}) async-start(bf16[16,16,512]{2,1,0:T(8,128)(2,1)} %bitcast.68), calls=%async_computation.5 | async-start | bytes 524288 | tf_op jit(solution)/shard_map/all_to_all | solution.py:42
  117.5 13.2 %all-to-all-start.5 = ((bf16[16,16,512]{2,1,0:T(8,128)(2,1)}), bf16[16,16,512]{2,1,0:T(8,128)(2,1)S(1)}, u32[]{:S(2)}, u32[]{:S(2)}) async-start(bf16[16,16,512]{2,1,0:T(8,128)(2,1)} %broadcast_in_dim.193), calls=%async_computation.6 | async-start | bytes 524288 | tf_op jit(solution)/shard_map/all_to_all | solution.py:42
  124.0 6.7 %collective-permute-start.14 = (bf16[256,512]{1,0:T(8,128)(2,1)S(1)}, bf16[256,512]{1,0:T(8,128)(2,1)S(1)}, u32[]{:S(2)}, u32[]{:S(2)}) collective-permute-start(bf16[256,512]{1,0:T(8,128)(2,1)S(1)} %convolution_convert_fusion.3), channel_id=1, source_target_pairs={{0,16},{16,0},{1,17},{17,1},{2,18},{18,2},{3,19},{19,3},{4,20},{20... | collective-permute-start | bytes 786440 | tf_op jit(solution)/shard_map/ppermute | solution.py:38
  132.8 10.9 %all-to-all-start.6 = ((bf16[4,64,512]{2,1,0:T(8,128)(2,1)}), bf16[4,64,512]{2,1,0:T(8,128)(2,1)S(1)}, u32[]{:S(2)}, u32[]{:S(2)}) async-start(bf16[4,64,512]{2,1,0:T(8,128)(2,1)} %bitcast.13), calls=%async_computation.7 | async-start | bytes 524288 | tf_op jit(solution)/shard_map/all_to_all | solution.py:42
  137.3 7.3 %collective-permute-start.15 = (bf16[256,256]{1,0:T(8,128)(2,1)S(1)}, bf16[256,256]{1,0:T(8,128)(2,1)S(1)}, u32[]{:S(2)}, u32[]{:S(2)}) collective-permute-start(bf16[256,256]{1,0:T(8,128)(2,1)S(1)} %slice.151), channel_id=1, source_target_pairs={{0,16},{16,0},{1,17},{17,1},{2,18},{18,2},{3,19},{19,3},{4,20},{20... | collective-permute-start | bytes 393224 | tf_op jit(solution)/shard_map/ppermute | solution.py:38
  144.6 7.1 %collective-permute-start.16 = (bf16[64,512]{1,0:T(8,128)(2,1)S(1)}, bf16[64,512]{1,0:T(8,128)(2,1)S(1)}, u32[]{:S(2)}, u32[]{:S(2)}) collective-permute-start(bf16[64,512]{1,0:T(8,128)(2,1)S(1)} %reduce-precision_convert_fusion.1), channel_id=1, source_target_pairs={{0,128},{128,0},{1,129},{129,1},{2,130},{130,2},{3,131},{131,3},{4... | collective-permute-start | bytes 196616 | tf_op jit(solution)/shard_map/ppermute | solution.py:38
  153.4 10.0 %all-to-all-start.7 = ((bf16[4,64,512]{2,1,0:T(8,128)(2,1)}), bf16[4,64,512]{2,1,0:T(8,128)(2,1)S(1)}, u32[]{:S(2)}, u32[]{:S(2)}) async-start(bf16[4,64,512]{2,1,0:T(8,128)(2,1)} %broadcast_in_dim.196), calls=%async_computation.8 | async-start | bytes 524288 | tf_op jit(solution)/shard_map/all_to_all | solution.py:42
  165.9 12.4 %all-to-all-start.8 = ((bf16[16,16,512]{2,1,0:T(8,128)(2,1)}), bf16[16,16,512]{2,1,0:T(8,128)(2,1)S(1)}, u32[]{:S(2)}, u32[]{:S(2)}) async-start(bf16[16,16,512]{2,1,0:T(8,128)(2,1)} %bitcast.69), calls=%async_computation.9 | async-start | bytes 524288 | tf_op jit(solution)/shard_map/all_to_all | solution.py:42
  171.2 7.4 %collective-permute-start.17 = (bf16[224,512]{1,0:T(8,128)(2,1)}, bf16[224,512]{1,0:T(8,128)(2,1)}, u32[]{:S(2)}, u32[]{:S(2)}) collective-permute-start(bf16[224,512]{1,0:T(8,128)(2,1)} %convolution_convert_fusion.5), channel_id=1, source_target_pairs={{0,16},{16,0},{1,17},{17,1},{2,18},{18,2},{3,19},{19,3},{4,20},{20... | collective-permute-start | bytes 688136 | tf_op jit(solution)/shard_map/ppermute | solution.py:38
  180.3 15.3 %all-to-all-start.9 = ((bf16[16,16,512]{2,1,0:T(8,128)(2,1)}), bf16[16,16,512]{2,1,0:T(8,128)(2,1)S(1)}, u32[]{:S(2)}, u32[]{:S(2)}) async-start(bf16[16,16,512]{2,1,0:T(8,128)(2,1)} %broadcast_in_dim.203), calls=%async_computation.10 | async-start | bytes 524288 | tf_op jit(solution)/shard_map/all_to_all | solution.py:42
  200.9 17.0 %collective-permute-start.18 = (bf16[640,256]{1,0:T(8,128)(2,1)}, bf16[640,256]{1,0:T(8,128)(2,1)}, u32[]{:S(2)}, u32[]{:S(2)}) collective-permute-start(bf16[640,256]{1,0:T(8,128)(2,1)} %fusion.14), channel_id=1, source_target_pairs={{0,16},{16,0},{1,17},{17,1},{2,18},{18,2},{3,19},{19,3},{4,20},{20... | collective-permute-start | bytes 983048 | tf_op jit(solution)/shard_map/ppermute | solution.py:38
  205.1 11.7 %all-to-all-start.10 = ((bf16[4,64,640]{2,1,0:T(8,128)(2,1)}), bf16[4,64,640]{2,1,0:T(8,128)(2,1)}, u32[]{:S(2)}, u32[]{:S(2)}) async-start(bf16[4,64,640]{2,1,0:T(8,128)(2,1)} %bitcast.67), calls=%async_computation.11 | async-start | bytes 655360 | tf_op jit(solution)/shard_map/all_to_all | solution.py:42
  217.9 7.4 %collective-permute-start.19 = (bf16[64,640]{1,0:T(8,128)(2,1)S(1)}, bf16[64,640]{1,0:T(8,128)(2,1)S(1)}, u32[]{:S(2)}, u32[]{:S(2)}) collective-permute-start(bf16[64,640]{1,0:T(8,128)(2,1)S(1)} %reduce-precision_convert_fusion), channel_id=1, source_target_pairs={{0,128},{128,0},{1,129},{129,1},{2,130},{130,2},{3,131},{131,3},{4... | collective-permute-start | bytes 245768 | tf_op jit(solution)/shard_map/ppermute | solution.py:38
  226.4 13.0 %all-to-all-start.11 = ((bf16[4,64,1280]{2,1,0:T(8,128)(2,1)}), bf16[4,64,1280]{2,1,0:T(8,128)(2,1)}, u32[]{:S(2)}, u32[]{:S(2)}) async-start(bf16[4,64,1280]{2,1,0:T(8,128)(2,1)} %broadcast_in_dim.209), calls=%async_computation.12 | async-start | bytes 1310720 | tf_op jit(solution)/shard_map/all_to_all | solution.py:42
  239.5 6.6 %collective-permute-start.20 = (bf16[256,1280]{1,0:T(8,128)(2,1)}, bf16[256,1280]{1,0:T(8,128)(2,1)}, u32[]{:S(2)}, u32[]{:S(2)}) collective-permute-start(bf16[256,1280]{1,0:T(8,128)(2,1)} %bitcast.18), channel_id=1, source_target_pairs={{0,16},{16,0},{1,17},{17,1},{2,18},{18,2},{3,19},{19,3},{4,20},{20... | collective-permute-start | bytes 1966088 | tf_op jit(solution)/shard_map/ppermute | solution.py:38
  (29 other events, 327.3 us)
Sparse Core Ops, SparseCore 0:
  16.4 39.6 reduce-scatter.1

commit v6 on v5

--- a/solution.py
+++ b/solution.py
@@ -228,10 +228,12 @@
     token_loss = jnp.sum(pred_float * pred_float, axis=1, keepdims=True)
     token_loss = token_loss / ((tokens / 16) ** 2 * DT * weight_half)
     out_partial = with_parts(product_transposed(pred, proj_all), token_loss, place)
+    second = sum_scatter(out_partial, MODEL)
+    out_all = spread(with_parts(second, column_sum(second, place), place), MODEL)
+
     far_at = slice(LANES, LANES + width)
     proj_far = swap(transpose_product(student_out[:, far_at], pred).astype(BF16), "c")
-    second, proj_far = lax.optimization_barrier((sum_scatter(out_partial, MODEL), proj_far))
-    out_all = spread(with_parts(second, column_sum(second, place), place), MODEL)
+    out_all = after(out_all, proj_far)
 
     hidden_partial = product_transposed(out_all, down_all).astype(BF16)
     grad_proj = transpose_product(student_out[:, :width], after(pred, hidden_partial)) + proj_far.astype(F32)

time: 261 us -> 253 us (0.969)
  waiting for transfers between devices: 51.7 us -> 37 us
  blocking collectives: 0 us -> 12.2 us
  other arithmetic: 16.9 us -> 13.2 us
    all_to_all x12 -> x11, waiting for transfers between devices: 42.7 us -> 26.1 us  [exchange(): return lax.all_to_all(values, axis, 0, 0, tiled=True)]
    all_to_all x0 -> x1, blocking collectives: none -> 12.2 us  [exchange(): return lax.all_to_all(values, axis, 0, 0, tiled=True)]
    all_to_all x12 -> x11, starting transfers between devices: 63.1 us -> 55.5 us  [exchange(): return lax.all_to_all(values, axis, 0, 0, tiled=True)]
    ppermute x12, starting transfers between devices: 40.4 us -> 47.6 us  [swap(): return lax.ppermute(values, axis, SWAP)]
  transfers between devices with their start and end apart: 34 -> 33, of which waited for: 16 -> 14; matrix products, arithmetic and copies ran while one was open for 17% -> 17% of each run, Pallas kernels for 0% -> 0%
where the time goes in v6:
time: 253 us; the launch traced here: 251 us
  starting transfers between devices  116 us (46%)
  matrix products  38.7 us (15%)
  waiting for transfers between devices  37 us (15%)
  between operations  17.1 us (7%)
  local copies, waits for them, and re-layouts  16.7 us (7%)
  other arithmetic  13.2 us (5%)
  blocking collectives  12.2 us (5%)
    all_to_all x11, starting transfers between devices, exchange(): return lax.all_to_all(values, axis, 0, 0, tiled=True)  55.5 us
    ppermute x12, starting transfers between devices, swap(): return lax.ppermute(values, axis, SWAP)  47.6 us
    all_to_all x11, waiting for transfers between devices, exchange(): return lax.all_to_all(values, axis, 0, 0, tiled=True)  26.1 us
    dot_general x11, matrix products, product(): return jnp.dot(left, right, preferred_element_type=F32)  22.8 us
    dot_general x8, matrix products, transpose_product(): lax.dot_general(left, right, (((0,), (0,)), ((), ())), preferred_element_...  12.3 us
    all_to_all x1, blocking collectives, exchange(): return lax.all_to_all(values, axis, 0, 0, tiled=True)  12.2 us
    ppermute x12, waiting for transfers between devices, swap(): return lax.ppermute(values, axis, SWAP)  8.46 us
    ppermute x3, starting transfers between devices, shards(): arrived = [lax.ppermute(z_all, 'x', PAIRS[step]) for step in (1, 2, 3)]  5.16 us
  transfers between devices with their start and end apart: 33, of which 14 were waited for; matrix products, arithmetic and copies ran while one was open for 17% of the time, Pallas kernels for 0%

profile of v6, /device:TPU:1, one launch (start us, length us, event | category | flops | bytes accessed | tf_op | source)
XLA Modules:
  0.0 251.4 jit_solution(18189173022523360812)
XLA Ops:
  9.3 2.4 fusion.17
  13.6 2.6 %convolution_convert_fusion = bf16[512,2048]{1,0:T(8,128)(2,1)} fusion(bf16[512,512]{1,0:T(8,128)(2,1)S(1)} %bitcast.66, bf16[512,1024]{1,0:T(8,128)(2,1)S(1)} %copy-done.27, bf16[512,1024]{1,0:T(8,128)(2,1)S(1)} %copy-done.28), kind=kOutput, calls=%fused_computation.3 | convolution fusion | flops 1078984704 | bytes 4718592 | tf_op jit(solution)/shard_map/dot_general | solution.py:26
  16.3 9.2 %all-to-all-start = ((bf16[16,32,256]{2,1,0:T(8,128)(2,1)}), bf16[16,32,256]{2,1,0:T(8,128)(2,1)S(1)}, u32[]{:S(2)}, u32[]{:S(2)}) async-start(bf16[16,32,256]{2,1,0:T(8,128)(2,1)} %bitcast.2), calls=%async_computation | async-start | bytes 524288 | tf_op jit(solution)/shard_map/all_to_all | solution.py:42
  30.8 4.3 %all-to-all-done = bf16[16,32,256]{2,1,0:T(8,128)(2,1)S(1)} async-done(((bf16[16,32,256]{2,1,0:T(8,128)(2,1)}), bf16[16,32,256]{2,1,0:T(8,128)(2,1)S(1)}, u32[]{:S(2)}, u32[]{:S(2)}) %all-to-all-start) | async-done | bytes 262176 | tf_op jit(solution)/shard_map/all_to_all | solution.py:42
  35.4 2.3 collective-permute-start
  39.9 3.5 %all-to-all-start.1 = ((bf16[16,16,512]{2,1,0:T(8,128)(2,1)}), bf16[16,16,512]{2,1,0:T(8,128)(2,1)S(1)}, u32[]{:S(2)}, u32[]{:S(2)}) async-start(bf16[16,16,512]{2,1,0:T(8,128)(2,1)} %broadcast_in_dim.191), calls=%async_computation.1 | async-start | bytes 524288 | tf_op jit(solution)/shard_map/all_to_all | solution.py:42
  44.3 9.2 %all-to-all-done.1 = bf16[16,16,512]{2,1,0:T(8,128)(2,1)S(1)} async-done(((bf16[16,16,512]{2,1,0:T(8,128)(2,1)}), bf16[16,16,512]{2,1,0:T(8,128)(2,1)S(1)}, u32[]{:S(2)}, u32[]{:S(2)}) %all-to-all-start.1) | async-done | bytes 262176 | tf_op jit(solution)/shard_map/all_to_all | solution.py:42
  53.4 2.8 %convolution_convert_fusion.1 = bf16[256,1408]{1,0:T(8,128)(2,1)} fusion(bf16[256,512]{1,0:T(8,128)(2,1)S(1)} %bitcast.53, bf16[256,1408]{1,0:T(8,128)(2,1)} %collective-permute-done.1, bf16[32,1408]{1,0:T(8,128)(2,1)S(1)} %pad_convert_fusion, bf16[224,128]{1,0:T(8,128)(2,1)} %copy-done.14, bf16[224,640]{1,0:T(8,128)(2,1)} %param.25, bf16[224,640]{1,0:T(8,128)(2,1)} %param.24), kind=kOutput, calls=%fused_computation.4 | convolution fusion | flops 376668160 | bytes 2424832 | tf_op jit(solution)/shard_map/dot_general | solution.py:26
  56.3 4.2 %all-to-all-start.2 = ((bf16[4,64,1408]{2,1,0:T(8,128)(2,1)}), bf16[4,64,1408]{2,1,0:T(8,128)(2,1)S(1)}, u32[]{:S(2)}, u32[]{:S(2)}) async-start(bf16[4,64,1408]{2,1,0:T(8,128)(2,1)} %bitcast.63), calls=%async_computation.2 | async-start | bytes 1441792 | tf_op jit(solution)/shard_map/all_to_all | solution.py:42
  70.1 4.2 %collective-permute-start.2 = (bf16[64,1408]{1,0:T(8,128)(2,1)S(1)}, bf16[64,1408]{1,0:T(8,128)(2,1)S(1)}, u32[]{:S(2)}, u32[]{:S(2)}) collective-permute-start(bf16[64,1408]{1,0:T(8,128)(2,1)S(1)} %convert_element_type.196), channel_id=1, source_target_pairs={{0,128},{128,0},{1,129},{129,1},{2,130},{130,2},{3,131},{131,3},{4... | collective-permute-start | bytes 540680 | tf_op jit(solution)/shard_map/ppermute | solution.py:38
  77.8 2.8 %collective-permute-start.8 = (bf16[32,1024]{1,0:T(8,128)(2,1)S(1)}, bf16[32,1024]{1,0:T(8,128)(2,1)}, u32[]{:S(2)}, u32[]{:S(2)}) collective-permute-start(bf16[32,1024]{1,0:T(8,128)(2,1)S(1)} %fusion.34), channel_id=1, source_target_pairs={{0,2},{1,3},{2,0},{3,1},{4,6},{5,7},{6,4},{7,5},{8,10},{9,11},{10,... | collective-permute-start | bytes 196616 | tf_op jit(solution)/shard_map/ppermute | solution.py:193
  84.5 4.1 %all-to-all-start.3 = ((bf16[4,64,640]{2,1,0:T(8,128)(2,1)}), bf16[4,64,640]{2,1,0:T(8,128)(2,1)}, u32[]{:S(2)}, u32[]{:S(2)}) async-start(bf16[4,64,640]{2,1,0:T(8,128)(2,1)} %broadcast_in_dim.192), calls=%async_computation.4 | async-start | bytes 655360 | tf_op jit(solution)/shard_map/all_to_all | solution.py:42
  90.3 4.6 %collective-permute-start.13 = (bf16[128,1024]{1,0:T(8,128)(2,1)}, bf16[128,1024]{1,0:T(8,128)(2,1)}, u32[]{:S(2)}, u32[]{:S(2)}) collective-permute-start(bf16[128,1024]{1,0:T(8,128)(2,1)} %pad_maximum_fusion.8), channel_id=1, source_target_pairs={{0,12},{4,8},{8,4},{12,0},{1,13},{5,9},{9,5},{13,1},{2,14},{6,10},... | collective-permute-start | bytes 786440 | tf_op jit(solution)/shard_map/ppermute | solution.py:199
  99.6 8.3 %all-to-all-start.4 = ((bf16[16,16,512]{2,1,0:T(8,128)(2,1)}), bf16[16,16,512]{2,1,0:T(8,128)(2,1)}, u32[]{:S(2)}, u32[]{:S(2)}) async-start(bf16[16,16,512]{2,1,0:T(8,128)(2,1)} %bitcast.67), calls=%async_computation.5 | async-start | bytes 524288 | tf_op jit(solution)/shard_map/all_to_all | solution.py:42
  117.7 4.9 %all-to-all-start.5 = ((bf16[16,16,512]{2,1,0:T(8,128)(2,1)}), bf16[16,16,512]{2,1,0:T(8,128)(2,1)S(1)}, u32[]{:S(2)}, u32[]{:S(2)}) async-start(bf16[16,16,512]{2,1,0:T(8,128)(2,1)} %broadcast_in_dim.193), calls=%async_computation.6 | async-start | bytes 524288 | tf_op jit(solution)/shard_map/all_to_all | solution.py:42
  124.2 5.2 %collective-permute-start.14 = (bf16[256,512]{1,0:T(8,128)(2,1)S(1)}, bf16[256,512]{1,0:T(8,128)(2,1)S(1)}, u32[]{:S(2)}, u32[]{:S(2)}) collective-permute-start(bf16[256,512]{1,0:T(8,128)(2,1)S(1)} %convolution_convert_fusion.3), channel_id=1, source_target_pairs={{0,16},{16,0},{1,17},{17,1},{2,18},{18,2},{3,19},{19,3},{4,20},{20... | collective-permute-start | bytes 786440 | tf_op jit(solution)/shard_map/ppermute | solution.py:38
  133.1 4.5 %all-to-all-start.6 = ((bf16[4,64,512]{2,1,0:T(8,128)(2,1)}), bf16[4,64,512]{2,1,0:T(8,128)(2,1)S(1)}, u32[]{:S(2)}, u32[]{:S(2)}) async-start(bf16[4,64,512]{2,1,0:T(8,128)(2,1)} %bitcast.13), calls=%async_computation.7 | async-start | bytes 524288 | tf_op jit(solution)/shard_map/all_to_all | solution.py:42
  137.6 6.3 %collective-permute-start.15 = (bf16[256,256]{1,0:T(8,128)(2,1)S(1)}, bf16[256,256]{1,0:T(8,128)(2,1)S(1)}, u32[]{:S(2)}, u32[]{:S(2)}) collective-permute-start(bf16[256,256]{1,0:T(8,128)(2,1)S(1)} %slice.151), channel_id=1, source_target_pairs={{0,16},{16,0},{1,17},{17,1},{2,18},{18,2},{3,19},{19,3},{4,20},{20... | collective-permute-start | bytes 393224 | tf_op jit(solution)/shard_map/ppermute | solution.py:38
  144.9 3.5 %collective-permute-start.16 = (bf16[64,512]{1,0:T(8,128)(2,1)S(1)}, bf16[64,512]{1,0:T(8,128)(2,1)S(1)}, u32[]{:S(2)}, u32[]{:S(2)}) collective-permute-start(bf16[64,512]{1,0:T(8,128)(2,1)S(1)} %reduce-precision_convert_fusion.1), channel_id=1, source_target_pairs={{0,128},{128,0},{1,129},{129,1},{2,130},{130,2},{3,131},{131,3},{4... | collective-permute-start | bytes 196616 | tf_op jit(solution)/shard_map/ppermute | solution.py:38
  148.4 3.6 %collective-permute-done.16 = bf16[64,512]{1,0:T(8,128)(2,1)S(1)} collective-permute-done((bf16[64,512]{1,0:T(8,128)(2,1)S(1)}, bf16[64,512]{1,0:T(8,128)(2,1)S(1)}, u32[]{:S(2)}, u32[]{:S(2)}) %collective-permute-start.16) | collective-permute-done | bytes 65568 | tf_op jit(solution)/shard_map/ppermute | solution.py:38
  153.6 4.5 %all-to-all-start.7 = ((bf16[4,64,512]{2,1,0:T(8,128)(2,1)}), bf16[4,64,512]{2,1,0:T(8,128)(2,1)S(1)}, u32[]{:S(2)}, u32[]{:S(2)}) async-start(bf16[4,64,512]{2,1,0:T(8,128)(2,1)} %broadcast_in_dim.196), calls=%async_computation.8 | async-start | bytes 524288 | tf_op jit(solution)/shard_map/all_to_all | solution.py:42
  158.2 5.5 %all-to-all-done.7 = bf16[4,64,512]{2,1,0:T(8,128)(2,1)S(1)} async-done(((bf16[4,64,512]{2,1,0:T(8,128)(2,1)}), bf16[4,64,512]{2,1,0:T(8,128)(2,1)S(1)}, u32[]{:S(2)}, u32[]{:S(2)}) %all-to-all-start.7) | async-done | bytes 262176 | tf_op jit(solution)/shard_map/all_to_all | solution.py:42
  165.4 12.2 %all_to_all.108 = bf16[16,16,512]{2,1,0:T(8,128)(2,1)S(1)} all-to-all(bf16[16,16,512]{2,1,0:T(8,128)(2,1)S(1)} %bitcast.68), channel_id=1, replica_groups=mesh['zh'=2,'y'=4,'c'=2,'x'=4,'zl'=4] {'x','zl'}, dimensions={0} | all-to-all | bytes 524288 | tf_op jit(solution)/shard_map/all_to_all | solution.py:42
  178.6 3.5 %all-to-all-start.9 = ((bf16[16,16,512]{2,1,0:T(8,128)(2,1)}), bf16[16,16,512]{2,1,0:T(8,128)(2,1)S(1)}, u32[]{:S(2)}, u32[]{:S(2)}) async-start(bf16[16,16,512]{2,1,0:T(8,128)(2,1)} %broadcast_in_dim.203), calls=%async_computation.10 | async-start | bytes 524288 | tf_op jit(solution)/shard_map/all_to_all | solution.py:42
  182.4 7.2 %collective-permute-start.17 = (bf16[224,512]{1,0:T(8,128)(2,1)S(1)}, bf16[224,512]{1,0:T(8,128)(2,1)S(1)}, u32[]{:S(2)}, u32[]{:S(2)}) collective-permute-start(bf16[224,512]{1,0:T(8,128)(2,1)S(1)} %convolution_convert_fusion.5), channel_id=1, source_target_pairs={{0,16},{16,0},{1,17},{17,1},{2,18},{18,2},{3,19},{19,3},{4,20},{20... | collective-permute-start | bytes 688136 | tf_op jit(solution)/shard_map/ppermute | solution.py:38
  193.2 4.1 %all-to-all-start.10 = ((bf16[4,64,640]{2,1,0:T(8,128)(2,1)}), bf16[4,64,640]{2,1,0:T(8,128)(2,1)}, u32[]{:S(2)}, u32[]{:S(2)}) async-start(bf16[4,64,640]{2,1,0:T(8,128)(2,1)} %bitcast.17), calls=%async_computation.11 | async-start | bytes 655360 | tf_op jit(solution)/shard_map/all_to_all | solution.py:42
  199.4 7.6 %collective-permute-start.18 = (bf16[640,256]{1,0:T(8,128)(2,1)}, bf16[640,256]{1,0:T(8,128)(2,1)}, u32[]{:S(2)}, u32[]{:S(2)}) collective-permute-start(bf16[640,256]{1,0:T(8,128)(2,1)} %fusion.14), channel_id=1, source_target_pairs={{0,16},{16,0},{1,17},{17,1},{2,18},{18,2},{3,19},{19,3},{4,20},{20... | collective-permute-start | bytes 983048 | tf_op jit(solution)/shard_map/ppermute | solution.py:38
  208.6 3.5 %collective-permute-start.19 = (bf16[64,640]{1,0:T(8,128)(2,1)S(1)}, bf16[64,640]{1,0:T(8,128)(2,1)S(1)}, u32[]{:S(2)}, u32[]{:S(2)}) collective-permute-start(bf16[64,640]{1,0:T(8,128)(2,1)S(1)} %reduce-precision_convert_fusion), channel_id=1, source_target_pairs={{0,128},{128,0},{1,129},{129,1},{2,130},{130,2},{3,131},{131,3},{4... | collective-permute-start | bytes 245768 | tf_op jit(solution)/shard_map/ppermute | solution.py:38
  213.6 2.3 collective-permute-done.19
  217.1 4.6 %all-to-all-start.11 = ((bf16[4,64,1280]{2,1,0:T(8,128)(2,1)}), bf16[4,64,1280]{2,1,0:T(8,128)(2,1)}, u32[]{:S(2)}, u32[]{:S(2)}) async-start(bf16[4,64,1280]{2,1,0:T(8,128)(2,1)} %broadcast_in_dim.209), calls=%async_computation.12 | async-start | bytes 1310720 | tf_op jit(solution)/shard_map/all_to_all | solution.py:42
  226.8 2.7 %all-to-all-done.11 = bf16[4,64,1280]{2,1,0:T(8,128)(2,1)} async-done(((bf16[4,64,1280]{2,1,0:T(8,128)(2,1)}), bf16[4,64,1280]{2,1,0:T(8,128)(2,1)}, u32[]{:S(2)}, u32[]{:S(2)}) %all-to-all-start.11) | async-done | bytes 655392 | tf_op jit(solution)/shard_map/all_to_all | solution.py:42
  229.4 6.3 %collective-permute-start.20 = (bf16[256,1280]{1,0:T(8,128)(2,1)}, bf16[256,1280]{1,0:T(8,128)(2,1)}, u32[]{:S(2)}, u32[]{:S(2)}) collective-permute-start(bf16[256,1280]{1,0:T(8,128)(2,1)} %bitcast.18), channel_id=1, source_target_pairs={{0,16},{16,0},{1,17},{17,1},{2,18},{18,2},{3,19},{19,3},{4,20},{20... | collective-permute-start | bytes 1966088 | tf_op jit(solution)/shard_map/ppermute | solution.py:38
  (197 shorter events, 77.8 us)
Async XLA Ops:
  7.2 55.0 %reduce-scatter.2.cloned.1.call-start = ((), (), s32[]{:S(2)}) async-start(), calls=%async_computation.13 | async-start | bytes 2621440 | tf_op jit(solution)/shard_map/reduce_scatter | solution.py:147
  16.3 18.9 %all-to-all-start = ((bf16[16,32,256]{2,1,0:T(8,128)(2,1)}), bf16[16,32,256]{2,1,0:T(8,128)(2,1)S(1)}, u32[]{:S(2)}, u32[]{:S(2)}) async-start(bf16[16,32,256]{2,1,0:T(8,128)(2,1)} %bitcast.2), calls=%async_computation | async-start | bytes 524288 | tf_op jit(solution)/shard_map/all_to_all | solution.py:42
  27.3 16.9 %collective-permute-start.1 = (bf16[256,1408]{1,0:T(8,128)(2,1)S(1)}, bf16[256,1408]{1,0:T(8,128)(2,1)}, u32[]{:S(2)}, u32[]{:S(2)}) collective-permute-start(bf16[256,1408]{1,0:T(8,128)(2,1)S(1)} %pad_maximum_fusion), channel_id=1, source_target_pairs={{0,16},{16,0},{1,17},{17,1},{2,18},{18,2},{3,19},{19,3},{4,20},{20... | collective-permute-start | bytes 2162696 | tf_op jit(solution)/shard_map/ppermute | solution.py:38
  39.9 13.5 %all-to-all-start.1 = ((bf16[16,16,512]{2,1,0:T(8,128)(2,1)}), bf16[16,16,512]{2,1,0:T(8,128)(2,1)S(1)}, u32[]{:S(2)}, u32[]{:S(2)}) async-start(bf16[16,16,512]{2,1,0:T(8,128)(2,1)} %broadcast_in_dim.191), calls=%async_computation.1 | async-start | bytes 524288 | tf_op jit(solution)/shard_map/all_to_all | solution.py:42
  43.5 53.8 %collective-permute-start.3 = (bf16[640,256]{0,1:T(8,128)(2,1)}, bf16[640,256]{0,1:T(8,128)(2,1)}, u32[]{:S(2)}, u32[]{:S(2)}) collective-permute-start(bf16[640,256]{0,1:T(8,128)(2,1)} %pad.23), channel_id=1, source_target_pairs={{0,16},{16,0},{1,17},{17,1},{2,18},{18,2},{3,19},{19,3},{4,20},{20... | collective-permute-start | bytes 983048 | tf_op jit(solution)/shard_map/ppermute | solution.py:38
  43.9 87.0 %collective-permute-start.10 = (bf16[256,512]{1,0:T(8,128)(2,1)}, bf16[256,512]{1,0:T(8,128)(2,1)}, u32[]{:S(2)}, u32[]{:S(2)}) collective-permute-start(bf16[256,512]{1,0:T(8,128)(2,1)} %pad.24), channel_id=1, source_target_pairs={{0,16},{16,0},{1,17},{17,1},{2,18},{18,2},{3,19},{19,3},{4,20},{20... | collective-permute-start | bytes 786440 | tf_op jit(solution)/shard_map/ppermute | solution.py:38
  56.3 13.4 %all-to-all-start.2 = ((bf16[4,64,1408]{2,1,0:T(8,128)(2,1)}), bf16[4,64,1408]{2,1,0:T(8,128)(2,1)S(1)}, u32[]{:S(2)}, u32[]{:S(2)}) async-start(bf16[4,64,1408]{2,1,0:T(8,128)(2,1)} %bitcast.63), calls=%async_computation.2 | async-start | bytes 1441792 | tf_op jit(solution)/shard_map/all_to_all | solution.py:42
  64.0 6.1 %collective-permute-start.4 = (bf16[32,2048]{1,0:T(8,128)(2,1)}, bf16[32,2048]{1,0:T(8,128)(2,1)}, u32[]{:S(2)}, u32[]{:S(2)}) collective-permute-start(bf16[32,2048]{1,0:T(8,128)(2,1)} %get-tuple-element.85), channel_id=1, source_target_pairs={{0,3},{1,2},{2,1},{3,0},{4,7},{5,6},{6,5},{7,4},{8,11},{9,10},{10,... | collective-permute-start | bytes 393224 | tf_op jit(solution)/shard_map/ppermute | solution.py:184
  64.7 11.8 %collective-permute-start.5 = (bf16[32,2048]{1,0:T(8,128)(2,1)}, bf16[32,2048]{1,0:T(8,128)(2,1)}, u32[]{:S(2)}, u32[]{:S(2)}) collective-permute-start(bf16[32,2048]{1,0:T(8,128)(2,1)} %get-tuple-element.84), channel_id=1, source_target_pairs={{0,2},{1,3},{2,0},{3,1},{4,6},{5,7},{6,4},{7,5},{8,10},{9,11},{10,... | collective-permute-start | bytes 393224 | tf_op jit(solution)/shard_map/ppermute | solution.py:184
  65.3 11.2 %collective-permute-start.6 = (bf16[32,2048]{1,0:T(8,128)(2,1)}, bf16[32,2048]{1,0:T(8,128)(2,1)}, u32[]{:S(2)}, u32[]{:S(2)}) collective-permute-start(bf16[32,2048]{1,0:T(8,128)(2,1)} %get-tuple-element.83), channel_id=1, source_target_pairs={{0,1},{1,0},{2,3},{3,2},{4,5},{5,4},{6,7},{7,6},{8,9},{9,8},{10,11... | collective-permute-start | bytes 393224 | tf_op jit(solution)/shard_map/ppermute | solution.py:184
  70.1 10.6 %collective-permute-start.2 = (bf16[64,1408]{1,0:T(8,128)(2,1)S(1)}, bf16[64,1408]{1,0:T(8,128)(2,1)S(1)}, u32[]{:S(2)}, u32[]{:S(2)}) collective-permute-start(bf16[64,1408]{1,0:T(8,128)(2,1)S(1)} %convert_element_type.196), channel_id=1, source_target_pairs={{0,128},{128,0},{1,129},{129,1},{2,130},{130,2},{3,131},{131,3},{4... | collective-permute-start | bytes 540680 | tf_op jit(solution)/shard_map/ppermute | solution.py:38
  77.7 10.9 %collective-permute-start.7 = (bf16[32,1024]{1,0:T(8,128)(2,1)S(1)}, bf16[32,1024]{1,0:T(8,128)(2,1)}, u32[]{:S(2)}, u32[]{:S(2)}) collective-permute-start(bf16[32,1024]{1,0:T(8,128)(2,1)S(1)} %fusion.34), channel_id=1, source_target_pairs={{0,1},{1,0},{2,3},{3,2},{4,5},{5,4},{6,7},{7,6},{8,9},{9,8},{10,11... | collective-permute-start | bytes 196616 | tf_op jit(solution)/shard_map/ppermute | solution.py:193
  77.8 10.8 %collective-permute-start.8 = (bf16[32,1024]{1,0:T(8,128)(2,1)S(1)}, bf16[32,1024]{1,0:T(8,128)(2,1)}, u32[]{:S(2)}, u32[]{:S(2)}) collective-permute-start(bf16[32,1024]{1,0:T(8,128)(2,1)S(1)} %fusion.34), channel_id=1, source_target_pairs={{0,2},{1,3},{2,0},{3,1},{4,6},{5,7},{6,4},{7,5},{8,10},{9,11},{10,... | collective-permute-start | bytes 196616 | tf_op jit(solution)/shard_map/ppermute | solution.py:193
  80.7 7.9 %collective-permute-start.9 = (bf16[32,1024]{1,0:T(8,128)(2,1)S(1)}, bf16[32,1024]{1,0:T(8,128)(2,1)}, u32[]{:S(2)}, u32[]{:S(2)}) collective-permute-start(bf16[32,1024]{1,0:T(8,128)(2,1)S(1)} %fusion.34), channel_id=1, source_target_pairs={{0,3},{1,2},{2,1},{3,0},{4,7},{5,6},{6,5},{7,4},{8,11},{9,10},{10,... | collective-permute-start | bytes 196616 | tf_op jit(solution)/shard_map/ppermute | solution.py:193
  84.5 12.8 %all-to-all-start.3 = ((bf16[4,64,640]{2,1,0:T(8,128)(2,1)}), bf16[4,64,640]{2,1,0:T(8,128)(2,1)}, u32[]{:S(2)}, u32[]{:S(2)}) async-start(bf16[4,64,640]{2,1,0:T(8,128)(2,1)} %broadcast_in_dim.192), calls=%async_computation.4 | async-start | bytes 655360 | tf_op jit(solution)/shard_map/all_to_all | solution.py:42
  90.3 17.7 %collective-permute-start.13 = (bf16[128,1024]{1,0:T(8,128)(2,1)}, bf16[128,1024]{1,0:T(8,128)(2,1)}, u32[]{:S(2)}, u32[]{:S(2)}) collective-permute-start(bf16[128,1024]{1,0:T(8,128)(2,1)} %pad_maximum_fusion.8), channel_id=1, source_target_pairs={{0,12},{4,8},{8,4},{12,0},{1,13},{5,9},{9,5},{13,1},{2,14},{6,10},... | collective-permute-start | bytes 786440 | tf_op jit(solution)/shard_map/ppermute | solution.py:199
  94.8 15.0 %collective-permute-start.12 = (bf16[128,1024]{1,0:T(8,128)(2,1)}, bf16[128,1024]{1,0:T(8,128)(2,1)}, u32[]{:S(2)}, u32[]{:S(2)}) collective-permute-start(bf16[128,1024]{1,0:T(8,128)(2,1)} %pad_maximum_fusion.8), channel_id=1, source_target_pairs={{0,8},{4,12},{8,0},{12,4},{1,9},{5,13},{9,1},{13,5},{2,10},{6,14},... | collective-permute-start | bytes 786440 | tf_op jit(solution)/shard_map/ppermute | solution.py:199
  94.8 16.9 %collective-permute-start.11 = (bf16[128,1024]{1,0:T(8,128)(2,1)}, bf16[128,1024]{1,0:T(8,128)(2,1)}, u32[]{:S(2)}, u32[]{:S(2)}) collective-permute-start(bf16[128,1024]{1,0:T(8,128)(2,1)} %pad_maximum_fusion.8), channel_id=1, source_target_pairs={{0,4},{4,0},{8,12},{12,8},{1,5},{5,1},{9,13},{13,9},{2,6},{6,2},{1... | collective-permute-start | bytes 786440 | tf_op jit(solution)/shard_map/ppermute | solution.py:199
  99.6 16.4 %all-to-all-start.4 = ((bf16[16,16,512]{2,1,0:T(8,128)(2,1)}), bf16[16,16,512]{2,1,0:T(8,128)(2,1)}, u32[]{:S(2)}, u32[]{:S(2)}) async-start(bf16[16,16,512]{2,1,0:T(8,128)(2,1)} %bitcast.67), calls=%async_computation.5 | async-start | bytes 524288 | tf_op jit(solution)/shard_map/all_to_all | solution.py:42
  117.7 13.2 %all-to-all-start.5 = ((bf16[16,16,512]{2,1,0:T(8,128)(2,1)}), bf16[16,16,512]{2,1,0:T(8,128)(2,1)S(1)}, u32[]{:S(2)}, u32[]{:S(2)}) async-start(bf16[16,16,512]{2,1,0:T(8,128)(2,1)} %broadcast_in_dim.193), calls=%async_computation.6 | async-start | bytes 524288 | tf_op jit(solution)/shard_map/all_to_all | solution.py:42
  124.2 6.7 %collective-permute-start.14 = (bf16[256,512]{1,0:T(8,128)(2,1)S(1)}, bf16[256,512]{1,0:T(8,128)(2,1)S(1)}, u32[]{:S(2)}, u32[]{:S(2)}) collective-permute-start(bf16[256,512]{1,0:T(8,128)(2,1)S(1)} %convolution_convert_fusion.3), channel_id=1, source_target_pairs={{0,16},{16,0},{1,17},{17,1},{2,18},{18,2},{3,19},{19,3},{4,20},{20... | collective-permute-start | bytes 786440 | tf_op jit(solution)/shard_map/ppermute | solution.py:38
  133.1 10.9 %all-to-all-start.6 = ((bf16[4,64,512]{2,1,0:T(8,128)(2,1)}), bf16[4,64,512]{2,1,0:T(8,128)(2,1)S(1)}, u32[]{:S(2)}, u32[]{:S(2)}) async-start(bf16[4,64,512]{2,1,0:T(8,128)(2,1)} %bitcast.13), calls=%async_computation.7 | async-start | bytes 524288 | tf_op jit(solution)/shard_map/all_to_all | solution.py:42
  137.6 7.3 %collective-permute-start.15 = (bf16[256,256]{1,0:T(8,128)(2,1)S(1)}, bf16[256,256]{1,0:T(8,128)(2,1)S(1)}, u32[]{:S(2)}, u32[]{:S(2)}) collective-permute-start(bf16[256,256]{1,0:T(8,128)(2,1)S(1)} %slice.151), channel_id=1, source_target_pairs={{0,16},{16,0},{1,17},{17,1},{2,18},{18,2},{3,19},{19,3},{4,20},{20... | collective-permute-start | bytes 393224 | tf_op jit(solution)/shard_map/ppermute | solution.py:38
  144.9 7.1 %collective-permute-start.16 = (bf16[64,512]{1,0:T(8,128)(2,1)S(1)}, bf16[64,512]{1,0:T(8,128)(2,1)S(1)}, u32[]{:S(2)}, u32[]{:S(2)}) collective-permute-start(bf16[64,512]{1,0:T(8,128)(2,1)S(1)} %reduce-precision_convert_fusion.1), channel_id=1, source_target_pairs={{0,128},{128,0},{1,129},{129,1},{2,130},{130,2},{3,131},{131,3},{4... | collective-permute-start | bytes 196616 | tf_op jit(solution)/shard_map/ppermute | solution.py:38
  153.6 10.0 %all-to-all-start.7 = ((bf16[4,64,512]{2,1,0:T(8,128)(2,1)}), bf16[4,64,512]{2,1,0:T(8,128)(2,1)S(1)}, u32[]{:S(2)}, u32[]{:S(2)}) async-start(bf16[4,64,512]{2,1,0:T(8,128)(2,1)} %broadcast_in_dim.196), calls=%async_computation.8 | async-start | bytes 524288 | tf_op jit(solution)/shard_map/all_to_all | solution.py:42
  178.6 12.1 %all-to-all-start.9 = ((bf16[16,16,512]{2,1,0:T(8,128)(2,1)}), bf16[16,16,512]{2,1,0:T(8,128)(2,1)S(1)}, u32[]{:S(2)}, u32[]{:S(2)}) async-start(bf16[16,16,512]{2,1,0:T(8,128)(2,1)} %broadcast_in_dim.203), calls=%async_computation.10 | async-start | bytes 524288 | tf_op jit(solution)/shard_map/all_to_all | solution.py:42
  182.4 8.3 %collective-permute-start.17 = (bf16[224,512]{1,0:T(8,128)(2,1)S(1)}, bf16[224,512]{1,0:T(8,128)(2,1)S(1)}, u32[]{:S(2)}, u32[]{:S(2)}) collective-permute-start(bf16[224,512]{1,0:T(8,128)(2,1)S(1)} %convolution_convert_fusion.5), channel_id=1, source_target_pairs={{0,16},{16,0},{1,17},{17,1},{2,18},{18,2},{3,19},{19,3},{4,20},{20... | collective-permute-start | bytes 688136 | tf_op jit(solution)/shard_map/ppermute | solution.py:38
  193.2 14.0 %all-to-all-start.10 = ((bf16[4,64,640]{2,1,0:T(8,128)(2,1)}), bf16[4,64,640]{2,1,0:T(8,128)(2,1)}, u32[]{:S(2)}, u32[]{:S(2)}) async-start(bf16[4,64,640]{2,1,0:T(8,128)(2,1)} %bitcast.17), calls=%async_computation.11 | async-start | bytes 655360 | tf_op jit(solution)/shard_map/all_to_all | solution.py:42
  199.4 9.2 %collective-permute-start.18 = (bf16[640,256]{1,0:T(8,128)(2,1)}, bf16[640,256]{1,0:T(8,128)(2,1)}, u32[]{:S(2)}, u32[]{:S(2)}) collective-permute-start(bf16[640,256]{1,0:T(8,128)(2,1)} %fusion.14), channel_id=1, source_target_pairs={{0,16},{16,0},{1,17},{17,1},{2,18},{18,2},{3,19},{19,3},{4,20},{20... | collective-permute-start | bytes 983048 | tf_op jit(solution)/shard_map/ppermute | solution.py:38
  208.6 7.3 %collective-permute-start.19 = (bf16[64,640]{1,0:T(8,128)(2,1)S(1)}, bf16[64,640]{1,0:T(8,128)(2,1)S(1)}, u32[]{:S(2)}, u32[]{:S(2)}) collective-permute-start(bf16[64,640]{1,0:T(8,128)(2,1)S(1)} %reduce-precision_convert_fusion), channel_id=1, source_target_pairs={{0,128},{128,0},{1,129},{129,1},{2,130},{130,2},{3,131},{131,3},{4... | collective-permute-start | bytes 245768 | tf_op jit(solution)/shard_map/ppermute | solution.py:38
  217.1 12.4 %all-to-all-start.11 = ((bf16[4,64,1280]{2,1,0:T(8,128)(2,1)}), bf16[4,64,1280]{2,1,0:T(8,128)(2,1)}, u32[]{:S(2)}, u32[]{:S(2)}) async-start(bf16[4,64,1280]{2,1,0:T(8,128)(2,1)} %broadcast_in_dim.209), calls=%async_computation.12 | async-start | bytes 1310720 | tf_op jit(solution)/shard_map/all_to_all | solution.py:42
  229.4 9.9 %collective-permute-start.20 = (bf16[256,1280]{1,0:T(8,128)(2,1)}, bf16[256,1280]{1,0:T(8,128)(2,1)}, u32[]{:S(2)}, u32[]{:S(2)}) collective-permute-start(bf16[256,1280]{1,0:T(8,128)(2,1)} %bitcast.18), channel_id=1, source_target_pairs={{0,16},{16,0},{1,17},{17,1},{2,18},{18,2},{3,19},{19,3},{4,20},{20... | collective-permute-start | bytes 1966088 | tf_op jit(solution)/shard_map/ppermute | solution.py:38
  (31 other events, 485.0 us)
Sparse Core Ops, SparseCore 0:
  16.4 39.6 reduce-scatter.1
